TPU v7x, 32 devices: a whole 2x2x4 slice. The times are simulated.
32 devices in a mesh: dp: 8 (over y, x, core), seq: 4 (over z).
Axes of the slice: x: 2, y: 2, z: 4, core: 2. Of those that a mesh axis runs over, the one named last changes fastest.
Arguments:
- src_x: bfloat16 [16, 1024, 1024], P('dp', 'seq'), may hold values from -6 to 6
- tgt_x: bfloat16 [16, 1024, 1024], P('dp', 'seq'), may hold values from -6 to 6
- src_seg: int32 [16, 1024], P('dp'), may hold values from 0 to 3, never falling along the last dimension, each value on 1 to 512 neighbouring positions
- tgt_seg: int32 [16, 1024], P('dp'), may hold values from 0 to 3, never falling along the last dimension, each value on 1 to 512 neighbouring positions
- tgt_len: int32 [16], P('dp'), may hold values from 512 to 1024
- src_lang: int32 [16, 4], P('dp'), may hold values from 0 to 49
- tgt_lang: int32 [16, 4], P('dp'), may hold values from 0 to 49
- lang_table: bfloat16 [50, 1024], P(None, ('dp', 'seq')), may hold values from -3 to 3
- gains: bfloat16 [5, 1024], P(None, ('dp', 'seq')), may hold values from 0.25 to 1.75
- biases: bfloat16 [16, 1024], P(None, ('dp', 'seq')), may hold values from -2 to 2
- ff_biases: bfloat16 [2, 4096], P(None, ('dp', 'seq')), may hold values from -2 to 2
- enc_proj: bfloat16 [3, 1024, 1024], P(None, ('dp', 'seq')), may hold values from -0.1875 to 0.1875
- enc_oproj: bfloat16 [1024, 1024], P(('dp', 'seq')), may hold values from -0.5 to 0.5
- enc_in: bfloat16 [1024, 4096], P(('dp', 'seq')), may hold values from -0.1875 to 0.1875
- enc_out: bfloat16 [4096, 1024], P(('dp', 'seq')), may hold values from -0.09375 to 0.09375
- dec_proj: bfloat16 [6, 1024, 1024], P(None, ('dp', 'seq')), may hold values from -0.1875 to 0.1875
- dec_oproj: bfloat16 [2, 1024, 1024], P(None, ('dp', 'seq')), may hold values from -0.5 to 0.5
- dec_in: bfloat16 [1024, 4096], P(('dp', 'seq')), may hold values from -0.1875 to 0.1875
- dec_out: bfloat16 [4096, 1024], P(('dp', 'seq')), may hold values from -0.09375 to 0.09375
- src_cot: bfloat16 [16, 1024, 1024], P('dp', 'seq'), may hold values from -6 to 6
- tgt_cot: bfloat16 [16, 1024, 1024], P('dp', 'seq'), may hold values from -6 to 6
Outputs:
- enc_y: bfloat16 [16, 1024, 1024], P('dp', 'seq')
- dec_y: bfloat16 [16, 1024, 1024], P('dp', 'seq')
- src_grad: float32 [16, 1024, 1024], P('dp', 'seq')
- tgt_grad: float32 [16, 1024, 1024], P('dp', 'seq')
- lang_table_grad: float32 [50, 1024], P(None, ('dp', 'seq'))
- gains_grad: float32 [5, 1024], P(None, ('dp', 'seq'))
- biases_grad: float32 [16, 1024], P(None, ('dp', 'seq'))
- ff_biases_grad: float32 [2, 4096], P(None, ('dp', 'seq'))
- enc_proj_grad: float32 [3, 1024, 1024], P(None, ('dp', 'seq'))
- enc_oproj_grad: float32 [1024, 1024], P(('dp', 'seq'))
- enc_in_grad: float32 [1024, 4096], P(('dp', 'seq'))
- enc_out_grad: float32 [4096, 1024], P(('dp', 'seq'))
- dec_proj_grad: float32 [6, 1024, 1024], P(None, ('dp', 'seq'))
- dec_oproj_grad: float32 [2, 1024, 1024], P(None, ('dp', 'seq'))
- dec_in_grad: float32 [1024, 4096], P(('dp', 'seq'))
- dec_out_grad: float32 [4096, 1024], P(('dp', 'seq'))
Inputs may be any that keep to these rules, and one draw needn't show every extreme that they name: `src_seg`: along each row the document numbers never fall, and every one of 0 to 3 appears. `tgt_seg`: along each row the document numbers never fall, and every one of 0 to 3 appears. `tgt_len`: target positions at or beyond the row's length are padding.
All inputs are finite; a program needn't handle non-finite values.
Results may differ from a plain program's by a relative error of at most 0.04.
Values may be sent and summed in bfloat16 or wider, within the bound.
A program may use at most 512 MiB of HBM per device.

v0:
```python
import jax
import jax.numpy as jnp
from jax import lax
from jax.sharding import PartitionSpec as P

HEAD_DIM = 64


EPSILON = 1e-05
MASKED = -1000000000.0
HIGHEST = lax.Precision.HIGHEST


def layer_norm(hidden, gain_row, shift_row):
    centred = hidden - jnp.mean(hidden, axis=-1, keepdims=True)
    spread = jnp.mean(centred * centred, axis=-1, keepdims=True)
    return centred * lax.rsqrt(spread + EPSILON) * gain_row + shift_row


def gelu_exact(values):
    return jax.nn.gelu(values, approximate=False)


def product(left, right):
    return jnp.dot(left, right, preferred_element_type=jnp.float32)


def product_tn(left, right):
    return lax.dot_general(
        left, right, (((0,), (0,)), ((), ())), preferred_element_type=jnp.float32
    )


def product_nt(left, right):
    return lax.dot_general(
        left, right, (((1,), (1,)), ((), ())), preferred_element_type=jnp.float32
    )


def exact_tn(left, right):
    return lax.dot_general(
        left, right, (((0,), (0,)), ((), ())), precision=HIGHEST, preferred_element_type=jnp.float32
    )


def column_sum(values):
    return jnp.sum(values.astype(jnp.float32), axis=0)


def split_heads(rows):
    return rows.reshape(rows.shape[0], -1, HEAD_DIM)


def norm_backward(hidden, gain_row, shift_row, grad_normed):
    pullback = jax.vjp(layer_norm, hidden, gain_row, shift_row)[1]
    return pullback(grad_normed)


def language_rows(segments, languages, count):
    member = segments[:, None] == jnp.arange(languages.shape[0], dtype=jnp.int32)[None, :]
    token_language = jnp.sum(jnp.where(member, languages[None, :], 0), axis=1)
    return (token_language[:, None] == jnp.arange(count, dtype=jnp.int32)[None, :]).astype(
        jnp.bfloat16
    )


def scores_of(queries, keys, allowed):
    scores = jnp.einsum(
        "qhd,khd->hqk", split_heads(queries), split_heads(keys), preferred_element_type=jnp.float32
    ) * HEAD_DIM ** (-0.5)
    return jnp.where(allowed[None], scores, MASKED)


def attend_forward(queries, keys, values, allowed):
    scores = scores_of(queries, keys, allowed)
    highest = jnp.max(scores, axis=-1, keepdims=True)
    exponent = jnp.exp(scores - highest)
    totals = jnp.sum(exponent, axis=-1, keepdims=True)
    weights = (exponent / totals).astype(jnp.bfloat16)
    mixed = jnp.einsum(
        "hqk,khd->qhd", weights, split_heads(values), preferred_element_type=jnp.float32
    )
    return (mixed.reshape(queries.shape).astype(jnp.bfloat16), highest, totals)


def query_side(queries, keys, values, allowed, highest, totals, grad_mixed):
    scores = scores_of(queries, keys, allowed)
    chances = jnp.exp(scores - highest) / totals
    grad_chances = jnp.einsum(
        "qhd,khd->hqk",
        split_heads(grad_mixed),
        split_heads(values),
        preferred_element_type=jnp.float32,
    )
    inner = jnp.sum(grad_chances * chances, axis=-1, keepdims=True)
    grad_scores = (chances * (grad_chances - inner)).astype(jnp.bfloat16)
    grad_queries = jnp.einsum(
        "hqk,khd->qhd", grad_scores, split_heads(keys), preferred_element_type=jnp.float32
    ) * HEAD_DIM ** (-0.5)
    return (grad_queries.reshape(queries.shape), inner)


def key_side(all_queries, keys, values, allowed, highest, totals, inner, all_grads):
    scores = scores_of(all_queries, keys, allowed)
    chances = jnp.exp(scores - highest) / totals
    grad_heads = split_heads(all_grads)
    grad_values = jnp.einsum(
        "hqk,qhd->khd", chances.astype(jnp.bfloat16), grad_heads, preferred_element_type=jnp.float32
    )
    grad_chances = jnp.einsum(
        "qhd,khd->hqk", grad_heads, split_heads(values), preferred_element_type=jnp.float32
    )
    grad_scores = (chances * (grad_chances - inner)).astype(jnp.bfloat16)
    grad_keys = jnp.einsum(
        "hqk,qhd->khd", grad_scores, split_heads(all_queries), preferred_element_type=jnp.float32
    ) * HEAD_DIM ** (-0.5)
    return (grad_keys.reshape(keys.shape), grad_values.reshape(values.shape))


def self_forward(normed, proj, query_bias, value_bias, allowed):
    query_rows = (product(normed, proj[0]) + query_bias).astype(jnp.bfloat16)
    key_rows = product(normed, proj[1]).astype(jnp.bfloat16)
    value_rows = (product(normed, proj[2]) + value_bias).astype(jnp.bfloat16)
    all_keys, all_values = (
        lax.all_gather(key_rows, "seq", axis=0, tiled=True),
        lax.all_gather(value_rows, "seq", axis=0, tiled=True),
    )
    mixed, highest, totals = attend_forward(query_rows, all_keys, all_values, allowed)
    return (mixed, (query_rows, key_rows, value_rows, all_keys, all_values, highest, totals))


def self_backward(normed, proj, kept, allowed, allowed_keys, grad_mixed):
    query_rows, key_rows, value_rows, all_keys, all_values, highest, totals = kept
    grad_query, inner = query_side(
        query_rows, all_keys, all_values, allowed, highest, totals, grad_mixed
    )
    all_queries, all_grads = (
        lax.all_gather(query_rows, "seq", axis=0, tiled=True),
        lax.all_gather(grad_mixed, "seq", axis=0, tiled=True),
    )
    all_top, all_total, all_inner = (
        lax.all_gather(highest.astype(jnp.bfloat16), "seq", axis=1, tiled=True).astype(
            highest.dtype
        ),
        lax.all_gather(totals.astype(jnp.bfloat16), "seq", axis=1, tiled=True).astype(totals.dtype),
        lax.all_gather(inner.astype(jnp.bfloat16), "seq", axis=1, tiled=True).astype(inner.dtype),
    )
    grad_key, grad_value = key_side(
        all_queries, key_rows, value_rows, allowed_keys, all_top, all_total, all_inner, all_grads
    )
    grad_query = grad_query.astype(jnp.bfloat16)
    grad_key = grad_key.astype(jnp.bfloat16)
    grad_value = grad_value.astype(jnp.bfloat16)
    proj_grad = jnp.stack(
        [
            product_tn(normed, grad_query),
            product_tn(normed, grad_key),
            product_tn(normed, grad_value),
        ]
    )
    grad_normed = (
        product_nt(grad_query, proj[0])
        + product_nt(grad_key, proj[1])
        + product_nt(grad_value, proj[2])
    )
    return (grad_normed, proj_grad, column_sum(grad_query), column_sum(grad_value))


def ffn_forward(hidden, gain_row, shift_row, w_in, in_bias, w_out, out_bias):
    normed = layer_norm(hidden, gain_row, shift_row).astype(jnp.bfloat16)
    inner = product(normed, w_in) + in_bias
    acted = gelu_exact(inner).astype(jnp.bfloat16)
    return (hidden + product(acted, w_out) + out_bias, (normed, inner, acted))


def ffn_backward(hidden, gain_row, shift_row, w_in, w_out, kept, grad):
    normed, inner, acted = kept
    branch = grad.astype(jnp.bfloat16)
    grad_inner = jax.vjp(gelu_exact, inner)[1](product_nt(branch, w_out))[0].astype(jnp.bfloat16)
    grad_hidden, grad_gain, grad_shift = norm_backward(
        hidden, gain_row, shift_row, product_nt(grad_inner, w_in)
    )
    return (
        grad + grad_hidden,
        (
            product_tn(normed, grad_inner),
            product_tn(acted, branch),
            column_sum(grad_inner),
            column_sum(branch),
            grad_gain,
            grad_shift,
        ),
    )


def pair_step(full, row):
    (
        lang_table,
        gains,
        biases,
        ff_biases,
        enc_proj,
        enc_oproj,
        enc_in,
        enc_out,
        dec_proj,
        dec_oproj,
        dec_in,
        dec_out,
    ) = full
    source, target, src_seg, tgt_seg, tgt_len, src_lang, tgt_lang, src_cot, tgt_cot = row
    local = source.shape[0]
    offset = lax.axis_index("seq") * local
    gain_f = gains.astype(jnp.float32)
    bias_f = biases.astype(jnp.float32)
    ffb_f = ff_biases.astype(jnp.float32)
    src_here = lax.dynamic_slice_in_dim(src_seg, offset, local)
    tgt_here = lax.dynamic_slice_in_dim(tgt_seg, offset, local)
    src_onehot = language_rows(src_here, src_lang, lang_table.shape[0])
    tgt_onehot = language_rows(tgt_here, tgt_lang, lang_table.shape[0])
    positions = offset + jnp.arange(local, dtype=jnp.int32)
    columns = jnp.arange(tgt_seg.shape[0], dtype=jnp.int32)
    enc_allowed = src_here[:, None] == src_seg[None, :]
    enc_allowed_keys = src_seg[:, None] == src_here[None, :]
    self_allowed = (tgt_here[:, None] == tgt_seg[None, :]) & (
        columns[None, :] <= positions[:, None]
    )
    self_allowed = self_allowed & (
        (columns < tgt_len)[None, :] | (columns[None, :] == positions[:, None])
    )
    self_allowed_keys = (tgt_seg[:, None] == tgt_here[None, :]) & (
        positions[None, :] <= columns[:, None]
    )
    self_allowed_keys = self_allowed_keys & (
        (positions < tgt_len)[None, :] | (positions[None, :] == columns[:, None])
    )
    cross_allowed = tgt_here[:, None] == src_seg[None, :]
    cross_allowed_keys = tgt_seg[:, None] == src_here[None, :]
    enc_h0 = source.astype(jnp.float32) + product(src_onehot, lang_table)
    enc_n1 = layer_norm(enc_h0, gain_f[0], bias_f[0]).astype(jnp.bfloat16)
    enc_mixed, enc_kept = self_forward(enc_n1, enc_proj, bias_f[1], bias_f[2], enc_allowed)
    enc_h1 = enc_h0 + product(enc_mixed, enc_oproj) + bias_f[3]
    encoded, enc_ffn_kept = ffn_forward(
        enc_h1, gain_f[1], bias_f[4], enc_in, ffb_f[0], enc_out, bias_f[5]
    )
    memory = encoded.astype(jnp.bfloat16)
    dec_h0 = target.astype(jnp.float32) + product(tgt_onehot, lang_table)
    dec_n1 = layer_norm(dec_h0, gain_f[2], bias_f[6]).astype(jnp.bfloat16)
    dec_mixed, dec_kept = self_forward(dec_n1, dec_proj[0:3], bias_f[7], bias_f[8], self_allowed)
    dec_h1 = dec_h0 + product(dec_mixed, dec_oproj[0]) + bias_f[9]
    dec_n2 = layer_norm(dec_h1, gain_f[3], bias_f[10]).astype(jnp.bfloat16)
    cross_query = (product(dec_n2, dec_proj[3]) + bias_f[11]).astype(jnp.bfloat16)
    memory_key = product(memory, dec_proj[4]).astype(jnp.bfloat16)
    memory_value = (product(memory, dec_proj[5]) + bias_f[12]).astype(jnp.bfloat16)
    all_memory_keys, all_memory_values = (
        lax.all_gather(memory_key, "seq", axis=0, tiled=True),
        lax.all_gather(memory_value, "seq", axis=0, tiled=True),
    )
    cross_mixed, cross_top, cross_total = attend_forward(
        cross_query, all_memory_keys, all_memory_values, cross_allowed
    )
    dec_h2 = dec_h1 + product(cross_mixed, dec_oproj[1]) + bias_f[13]
    decoded, dec_ffn_kept = ffn_forward(
        dec_h2, gain_f[4], bias_f[14], dec_in, ffb_f[1], dec_out, bias_f[15]
    )
    grad_h2, dec_ffn_grads = ffn_backward(
        dec_h2, gain_f[4], bias_f[14], dec_in, dec_out, dec_ffn_kept, tgt_cot.astype(jnp.float32)
    )
    cross_branch = grad_h2.astype(jnp.bfloat16)
    grad_cross_mixed = product_nt(cross_branch, dec_oproj[1]).astype(jnp.bfloat16)
    grad_cross_query, cross_inner = query_side(
        cross_query,
        all_memory_keys,
        all_memory_values,
        cross_allowed,
        cross_top,
        cross_total,
        grad_cross_mixed,
    )
    all_cross_queries, all_cross_grads = (
        lax.all_gather(cross_query, "seq", axis=0, tiled=True),
        lax.all_gather(grad_cross_mixed, "seq", axis=0, tiled=True),
    )
    all_cross_top, all_cross_total, all_cross_inner = (
        lax.all_gather(cross_top.astype(jnp.bfloat16), "seq", axis=1, tiled=True).astype(
            cross_top.dtype
        ),
        lax.all_gather(cross_total.astype(jnp.bfloat16), "seq", axis=1, tiled=True).astype(
            cross_total.dtype
        ),
        lax.all_gather(cross_inner.astype(jnp.bfloat16), "seq", axis=1, tiled=True).astype(
            cross_inner.dtype
        ),
    )
    grad_memory_key, grad_memory_value = key_side(
        all_cross_queries,
        memory_key,
        memory_value,
        cross_allowed_keys,
        all_cross_top,
        all_cross_total,
        all_cross_inner,
        all_cross_grads,
    )
    grad_cross_query = grad_cross_query.astype(jnp.bfloat16)
    grad_memory_key = grad_memory_key.astype(jnp.bfloat16)
    grad_memory_value = grad_memory_value.astype(jnp.bfloat16)
    grad_memory = product_nt(grad_memory_key, dec_proj[4]) + product_nt(
        grad_memory_value, dec_proj[5]
    )
    grad_norm_two, gain_three_grad, shift_ten_grad = norm_backward(
        dec_h1, gain_f[3], bias_f[10], product_nt(grad_cross_query, dec_proj[3])
    )
    grad_h1 = grad_h2 + grad_norm_two
    self_branch = grad_h1.astype(jnp.bfloat16)
    grad_dec_mixed = product_nt(self_branch, dec_oproj[0]).astype(jnp.bfloat16)
    grad_dec_normed, dec_self_grad, bias_seven_grad, bias_eight_grad = self_backward(
        dec_n1, dec_proj[0:3], dec_kept, self_allowed, self_allowed_keys, grad_dec_mixed
    )
    grad_norm_one, gain_two_grad, shift_six_grad = norm_backward(
        dec_h0, gain_f[2], bias_f[6], grad_dec_normed
    )
    tgt_grad = grad_h1 + grad_norm_one
    grad_e1, enc_ffn_grads = ffn_backward(
        enc_h1,
        gain_f[1],
        bias_f[4],
        enc_in,
        enc_out,
        enc_ffn_kept,
        src_cot.astype(jnp.float32) + grad_memory,
    )
    enc_branch = grad_e1.astype(jnp.bfloat16)
    grad_enc_mixed = product_nt(enc_branch, enc_oproj).astype(jnp.bfloat16)
    grad_enc_normed, enc_self_grad, bias_one_grad, bias_two_grad = self_backward(
        enc_n1, enc_proj, enc_kept, enc_allowed, enc_allowed_keys, grad_enc_mixed
    )
    grad_norm_zero, gain_zero_grad, shift_zero_grad = norm_backward(
        enc_h0, gain_f[0], bias_f[0], grad_enc_normed
    )
    src_grad = grad_e1 + grad_norm_zero
    lang_grad = exact_tn(src_onehot.astype(jnp.float32), src_grad) + exact_tn(
        tgt_onehot.astype(jnp.float32), tgt_grad
    )
    gains_grad = jnp.stack(
        [gain_zero_grad, enc_ffn_grads[4], gain_two_grad, gain_three_grad, dec_ffn_grads[4]]
    )
    biases_grad = jnp.stack(
        [
            shift_zero_grad,
            bias_one_grad,
            bias_two_grad,
            column_sum(enc_branch),
            enc_ffn_grads[5],
            enc_ffn_grads[3],
            shift_six_grad,
            bias_seven_grad,
            bias_eight_grad,
            column_sum(self_branch),
            shift_ten_grad,
            column_sum(grad_cross_query),
            column_sum(grad_memory_value),
            column_sum(cross_branch),
            dec_ffn_grads[5],
            dec_ffn_grads[3],
        ]
    )
    ff_biases_grad = jnp.stack([enc_ffn_grads[2], dec_ffn_grads[2]])
    cross_grad = jnp.stack(
        [
            product_tn(dec_n2, grad_cross_query),
            product_tn(memory, grad_memory_key),
            product_tn(memory, grad_memory_value),
        ]
    )
    dec_proj_grad = jnp.concatenate([dec_self_grad, cross_grad], axis=0)
    dec_oproj_grad = jnp.stack(
        [product_tn(dec_mixed, self_branch), product_tn(cross_mixed, cross_branch)]
    )
    grads = (
        lang_grad,
        gains_grad,
        biases_grad,
        ff_biases_grad,
        enc_self_grad,
        product_tn(enc_mixed, enc_branch),
        enc_ffn_grads[0],
        enc_ffn_grads[1],
        dec_proj_grad,
        dec_oproj_grad,
        dec_ffn_grads[0],
        dec_ffn_grads[1],
    )
    return ((memory, decoded.astype(jnp.bfloat16), src_grad, tgt_grad), grads)


def on_device(
    src_x,
    tgt_x,
    src_seg,
    tgt_seg,
    tgt_len,
    src_lang,
    tgt_lang,
    lang_table,
    gains,
    biases,
    ff_biases,
    enc_proj,
    enc_oproj,
    enc_in,
    enc_out,
    dec_proj,
    dec_oproj,
    dec_in,
    dec_out,
    src_cot,
    tgt_cot,
):
    shards = (
        lang_table,
        gains,
        biases,
        ff_biases,
        enc_proj,
        enc_oproj,
        enc_in,
        enc_out,
        dec_proj,
        dec_oproj,
        dec_in,
        dec_out,
    )
    kept_weights = tuple(
        (
            lax.all_gather(lang_table, ("dp", "seq"), axis=1, tiled=True),
            lax.all_gather(gains, ("dp", "seq"), axis=1, tiled=True),
            lax.all_gather(biases, ("dp", "seq"), axis=1, tiled=True),
            lax.all_gather(ff_biases, ("dp", "seq"), axis=1, tiled=True),
            lax.all_gather(enc_proj, ("dp", "seq"), axis=1, tiled=True),
            lax.all_gather(enc_oproj, ("dp", "seq"), axis=0, tiled=True),
            lax.all_gather(enc_in, ("dp", "seq"), axis=0, tiled=True),
            lax.all_gather(enc_out, ("dp", "seq"), axis=0, tiled=True),
            lax.all_gather(dec_proj, ("dp", "seq"), axis=1, tiled=True),
            lax.all_gather(dec_oproj, ("dp", "seq"), axis=1, tiled=True),
            lax.all_gather(dec_in, ("dp", "seq"), axis=0, tiled=True),
            lax.all_gather(dec_out, ("dp", "seq"), axis=0, tiled=True),
        )
    )
    start = tuple((jnp.zeros(shard.shape, jnp.float32) for shard in shards))

    def step_fn(totals, row):
        outputs, grads = pair_step(kept_weights, row)
        grads = tuple(
            (
                lax.psum_scatter(grads[0], ("dp", "seq"), scatter_dimension=1, tiled=True),
                lax.psum_scatter(grads[1], ("dp", "seq"), scatter_dimension=1, tiled=True),
                lax.psum_scatter(grads[2], ("dp", "seq"), scatter_dimension=1, tiled=True),
                lax.psum_scatter(grads[3], ("dp", "seq"), scatter_dimension=1, tiled=True),
                lax.psum_scatter(grads[4], ("dp", "seq"), scatter_dimension=1, tiled=True),
                lax.psum_scatter(grads[5], ("dp", "seq"), scatter_dimension=0, tiled=True),
                lax.psum_scatter(grads[6], ("dp", "seq"), scatter_dimension=0, tiled=True),
                lax.psum_scatter(grads[7], ("dp", "seq"), scatter_dimension=0, tiled=True),
                lax.psum_scatter(grads[8], ("dp", "seq"), scatter_dimension=1, tiled=True),
                lax.psum_scatter(grads[9], ("dp", "seq"), scatter_dimension=1, tiled=True),
                lax.psum_scatter(grads[10], ("dp", "seq"), scatter_dimension=0, tiled=True),
                lax.psum_scatter(grads[11], ("dp", "seq"), scatter_dimension=0, tiled=True),
            )
        )
        totals = tuple((total + grad for total, grad in zip(totals, grads)))
        return (totals, outputs)

    rows = (src_x, tgt_x, src_seg, tgt_seg, tgt_len, src_lang, tgt_lang, src_cot, tgt_cot)
    totals, outputs = lax.scan(step_fn, start, rows)
    return (
        outputs[0],
        outputs[1],
        outputs[2],
        outputs[3],
        totals[0],
        totals[1],
        totals[2],
        totals[3],
        totals[4],
        totals[5],
        totals[6],
        totals[7],
        totals[8],
        totals[9],
        totals[10],
        totals[11],
    )


def solution(mesh):
    return jax.shard_map(
        on_device,
        mesh=mesh,
        in_specs=(
            P("dp", "seq", None),
            P("dp", "seq", None),
            P("dp", None),
            P("dp", None),
            P("dp"),
            P("dp", None),
            P("dp", None),
            P(None, ("dp", "seq")),
            P(None, ("dp", "seq")),
            P(None, ("dp", "seq")),
            P(None, ("dp", "seq")),
            P(None, ("dp", "seq"), None),
            P(("dp", "seq"), None),
            P(("dp", "seq"), None),
            P(("dp", "seq"), None),
            P(None, ("dp", "seq"), None),
            P(None, ("dp", "seq"), None),
            P(("dp", "seq"), None),
            P(("dp", "seq"), None),
            P("dp", "seq", None),
            P("dp", "seq", None),
        ),
        out_specs=(
            P("dp", "seq", None),
            P("dp", "seq", None),
            P("dp", "seq", None),
            P("dp", "seq", None),
            P(None, ("dp", "seq")),
            P(None, ("dp", "seq")),
            P(None, ("dp", "seq")),
            P(None, ("dp", "seq")),
            P(None, ("dp", "seq"), None),
            P(("dp", "seq"), None),
            P(("dp", "seq"), None),
            P(("dp", "seq"), None),
            P(None, ("dp", "seq"), None),
            P(None, ("dp", "seq"), None),
            P(("dp", "seq"), None),
            P(("dp", "seq"), None),
        ),
        check_vma=False,
    )
```

profile of v0, /device:TPU:0, one launch (start us, length us, event | category | flops | bytes accessed | tf_op | source)
XLA Modules:
  0.0 7715.8 jit_solution(7644607497880068313)
XLA Ops:
  521.5 97.4 %all-gather.59.cloned.1.call-done = bf16[6,1024,1024]{2,1,0:T(8,128)(2,1)} async-done(((bf16[6,32,1024]{2,1,0:T(8,128)(2,1)}), bf16[6,1024,1024]{2,1,0:T(8,128)(2,1)}) %all-gather.59.cloned.1.call-update) | async-done | bytes 12582928 | tf_op jit(solution)/shard_map/all_gather | solution.py:444
  618.8 7089.8 %while.44 = (s32[]{:T(128)}, f32[50,32]{0,1:T(8,128)}, f32[5,32]{1,0:T(8,128)}, f32[16,32]{1,0:T(8,128)}, f32[2,128]{1,0:T(2,128)}, /*index=5*/f32[3,32,1024]{2,...) while((s32[]{:T(128)}, f32[50,32]{0,1:T(8,128)}, ...), condition=%wide.region_67.68_spmd.clone, body=%wide.region_0.67_spmd.clone.sunk | while | flops 59014103040 | bytes 2139486208 | solution.py:474
  1448.9 133.8 %reduce-scatter.27.cloned.1.call-done = f32[32,5]{1,0:T(8,128)} async-done(((f32[1024,5]{1,0:T(8,128)}), f32[32,5]{1,0:T(8,128)}) %reduce-scatter.27.cloned.1.call-update) | async-done | bytes 656 | tf_op jit(solution)/shard_map/while
  1583.5 131.7 %reduce-scatter.29.cloned.1.call-done = f32[32,16]{1,0:T(8,128)} async-done(((f32[1024,16]{1,0:T(8,128)}), f32[32,16]{1,0:T(8,128)}) %reduce-scatter.29.cloned.1.call-update) | async-done | bytes 2064 | tf_op jit(solution)/shard_map/while
  1716.0 131.7 %reduce-scatter.25.cloned.1.call-done = f32[50,32]{0,1:T(8,128)} async-done(((f32[50,1024]{0,1:T(8,128)}), f32[50,32]{0,1:T(8,128)}) %reduce-scatter.25.cloned.1.call-update) | async-done | bytes 6416 | tf_op jit(solution)/shard_map/while/body/eval_jaxpr/reduce_scatter | solution.py:456
  1848.5 145.4 %reduce-scatter.35.cloned.1.call-done = f32[32,1024]{1,0:T(8,128)} async-done(((f32[1024,1024]{1,0:T(8,128)}), f32[32,1024]{1,0:T(8,128)}) %reduce-scatter.35.cloned.1.call-update) | async-done | bytes 131088 | tf_op jit(solution)/shard_map/while/body/eval_jaxpr/reduce_scatter | solution.py:461
  1994.8 185.7 %reduce-scatter.43.cloned.1.call-done = f32[2,32,1024]{2,1,0:T(8,128)} async-done(((f32[2,1024,1024]{2,1,0:T(8,128)}), f32[2,32,1024]{2,1,0:T(8,128)}) %reduce-scatter.43.cloned.1.call-update) | async-done | bytes 262160 | tf_op jit(solution)/shard_map/while/body/eval_jaxpr/reduce_scatter | solution.py:465
  2181.5 271.5 %reduce-scatter.33.cloned.1.call-done = f32[3,32,1024]{2,1,0:T(8,128)} async-done(((f32[3,1024,1024]{2,1,0:T(8,128)}), f32[3,32,1024]{2,1,0:T(8,128)}) %reduce-scatter.33.cloned.1.call-update) | async-done | bytes 393232 | tf_op jit(solution)/shard_map/while/body/eval_jaxpr/reduce_scatter | solution.py:460
  2454.8 362.2 %reduce-scatter.47.cloned.1.call-done = f32[128,1024]{1,0:T(8,128)} async-done(((f32[4096,1024]{1,0:T(8,128)}), f32[128,1024]{1,0:T(8,128)}) %reduce-scatter.47.cloned.1.call-update) | async-done | bytes 524304 | tf_op jit(solution)/shard_map/while/body/eval_jaxpr/reduce_scatter | solution.py:467
  2818.3 363.2 %reduce-scatter.45.cloned.1.call-done = f32[32,4096]{1,0:T(8,128)} async-done(((f32[1024,4096]{1,0:T(8,128)}), f32[32,4096]{1,0:T(8,128)}) %reduce-scatter.45.cloned.1.call-update) | async-done | bytes 524304 | tf_op jit(solution)/shard_map/while/body/eval_jaxpr/reduce_scatter | solution.py:466
  3182.7 246.9 %reduce-scatter.41.cloned.1.call-done = f32[6,32,1024]{2,1,0:T(8,128)} async-done(((f32[6,1024,1024]{2,1,0:T(8,128)}), f32[6,32,1024]{2,1,0:T(8,128)}) %reduce-scatter.41.cloned.1.call-update) | async-done | bytes 786448 | tf_op jit(solution)/shard_map/while/body/eval_jaxpr/reduce_scatter | solution.py:464
  3431.1 364.8 %reduce-scatter.37.cloned.1.call-done = f32[32,4096]{1,0:T(8,128)} async-done(((f32[1024,4096]{1,0:T(8,128)}), f32[32,4096]{1,0:T(8,128)}) %reduce-scatter.37.cloned.1.call-update) | async-done | bytes 524304 | tf_op jit(solution)/shard_map/while/body/eval_jaxpr/reduce_scatter | solution.py:462
  3797.1 363.4 %reduce-scatter.39.cloned.1.call-done = f32[128,1024]{1,0:T(8,128)} async-done(((f32[4096,1024]{1,0:T(8,128)}), f32[128,1024]{1,0:T(8,128)}) %reduce-scatter.39.cloned.1.call-update) | async-done | bytes 524304 | tf_op jit(solution)/shard_map/while/body/eval_jaxpr/reduce_scatter | solution.py:463
  4994.1 133.5 %reduce-scatter.27.cloned.1.call-done = f32[32,5]{1,0:T(8,128)} async-done(((f32[1024,5]{1,0:T(8,128)}), f32[32,5]{1,0:T(8,128)}) %reduce-scatter.27.cloned.1.call-update) | async-done | bytes 656 | tf_op jit(solution)/shard_map/while
  5128.3 131.8 %reduce-scatter.29.cloned.1.call-done = f32[32,16]{1,0:T(8,128)} async-done(((f32[1024,16]{1,0:T(8,128)}), f32[32,16]{1,0:T(8,128)}) %reduce-scatter.29.cloned.1.call-update) | async-done | bytes 2064 | tf_op jit(solution)/shard_map/while
  5260.9 131.9 %reduce-scatter.25.cloned.1.call-done = f32[50,32]{0,1:T(8,128)} async-done(((f32[50,1024]{0,1:T(8,128)}), f32[50,32]{0,1:T(8,128)}) %reduce-scatter.25.cloned.1.call-update) | async-done | bytes 6416 | tf_op jit(solution)/shard_map/while/body/eval_jaxpr/reduce_scatter | solution.py:456
  5393.6 145.3 %reduce-scatter.35.cloned.1.call-done = f32[32,1024]{1,0:T(8,128)} async-done(((f32[1024,1024]{1,0:T(8,128)}), f32[32,1024]{1,0:T(8,128)}) %reduce-scatter.35.cloned.1.call-update) | async-done | bytes 131088 | tf_op jit(solution)/shard_map/while/body/eval_jaxpr/reduce_scatter | solution.py:461
  5539.8 185.8 %reduce-scatter.43.cloned.1.call-done = f32[2,32,1024]{2,1,0:T(8,128)} async-done(((f32[2,1024,1024]{2,1,0:T(8,128)}), f32[2,32,1024]{2,1,0:T(8,128)}) %reduce-scatter.43.cloned.1.call-update) | async-done | bytes 262160 | tf_op jit(solution)/shard_map/while/body/eval_jaxpr/reduce_scatter | solution.py:465
  5726.7 271.5 %reduce-scatter.33.cloned.1.call-done = f32[3,32,1024]{2,1,0:T(8,128)} async-done(((f32[3,1024,1024]{2,1,0:T(8,128)}), f32[3,32,1024]{2,1,0:T(8,128)}) %reduce-scatter.33.cloned.1.call-update) | async-done | bytes 393232 | tf_op jit(solution)/shard_map/while/body/eval_jaxpr/reduce_scatter | solution.py:460
  6000.1 362.1 %reduce-scatter.47.cloned.1.call-done = f32[128,1024]{1,0:T(8,128)} async-done(((f32[4096,1024]{1,0:T(8,128)}), f32[128,1024]{1,0:T(8,128)}) %reduce-scatter.47.cloned.1.call-update) | async-done | bytes 524304 | tf_op jit(solution)/shard_map/while/body/eval_jaxpr/reduce_scatter | solution.py:467
  6363.4 363.1 %reduce-scatter.45.cloned.1.call-done = f32[32,4096]{1,0:T(8,128)} async-done(((f32[1024,4096]{1,0:T(8,128)}), f32[32,4096]{1,0:T(8,128)}) %reduce-scatter.45.cloned.1.call-update) | async-done | bytes 524304 | tf_op jit(solution)/shard_map/while/body/eval_jaxpr/reduce_scatter | solution.py:466
  6727.7 247.1 %reduce-scatter.41.cloned.1.call-done = f32[6,32,1024]{2,1,0:T(8,128)} async-done(((f32[6,1024,1024]{2,1,0:T(8,128)}), f32[6,32,1024]{2,1,0:T(8,128)}) %reduce-scatter.41.cloned.1.call-update) | async-done | bytes 786448 | tf_op jit(solution)/shard_map/while/body/eval_jaxpr/reduce_scatter | solution.py:464
  6976.2 364.8 %reduce-scatter.37.cloned.1.call-done = f32[32,4096]{1,0:T(8,128)} async-done(((f32[1024,4096]{1,0:T(8,128)}), f32[32,4096]{1,0:T(8,128)}) %reduce-scatter.37.cloned.1.call-update) | async-done | bytes 524304 | tf_op jit(solution)/shard_map/while/body/eval_jaxpr/reduce_scatter | solution.py:462
  7342.3 363.4 %reduce-scatter.39.cloned.1.call-done = f32[128,1024]{1,0:T(8,128)} async-done(((f32[4096,1024]{1,0:T(8,128)}), f32[128,1024]{1,0:T(8,128)}) %reduce-scatter.39.cloned.1.call-update) | async-done | bytes 524304 | tf_op jit(solution)/shard_map/while/body/eval_jaxpr/reduce_scatter | solution.py:463
  (1368 shorter events, 2196.1 us)
Async XLA Ops:
  10.6 432.0 %all-gather.71.cloned.1.call-start = ((), (), s32[]{:S(2)}) async-start(), calls=%async_computation.18 | async-start | bytes 8650752 | tf_op jit(solution)/shard_map/all_gather | solution.py:446
  11.1 510.3 %all-gather.73.cloned.1.call-start = ((), (), s32[]{:S(2)}) async-start(), calls=%async_computation.19 | async-start | bytes 8650752 | tf_op jit(solution)/shard_map/all_gather | solution.py:447
  11.9 606.9 %all-gather.59.cloned.1.call-start = ((), (), s32[]{:S(2)}) async-start(), calls=%async_computation.12 | async-start | bytes 12976128 | tf_op jit(solution)/shard_map/all_gather | solution.py:444
  794.2 377.6 %all-gather.91.cloned.1.call-start = ((), (), s32[]{:S(2)}) async-start(), calls=%async_computation.28 | async-start | bytes 2621440 | tf_op jit(solution)/shard_map/while/body/eval_jaxpr/all_gather | solution.py:281
  1349.0 498.7 %reduce-scatter.25.cloned.1.call-start = ((), (), s32[]{:S(2)}) async-start(), calls=%async_computation.32 | async-start | bytes 540672 | tf_op jit(solution)/shard_map/while/body/eval_jaxpr/reduce_scatter | solution.py:456
  1352.3 641.5 %reduce-scatter.35.cloned.1.call-start = ((), (), s32[]{:S(2)}) async-start(), calls=%async_computation.37 | async-start | bytes 4325376 | tf_op jit(solution)/shard_map/while/body/eval_jaxpr/reduce_scatter | solution.py:461
  1355.1 825.4 %reduce-scatter.43.cloned.1.call-start = ((), (), s32[]{:S(2)}) async-start(), calls=%async_computation.41 | async-start | bytes 8650752 | tf_op jit(solution)/shard_map/while/body/eval_jaxpr/reduce_scatter | solution.py:465
  1362.2 1090.8 %reduce-scatter.33.cloned.1.call-start = ((), (), s32[]{:S(2)}) async-start(), calls=%async_computation.36 | async-start | bytes 12976128 | tf_op jit(solution)/shard_map/while/body/eval_jaxpr/reduce_scatter | solution.py:460
  1370.6 1446.4 %reduce-scatter.47.cloned.1.call-start = ((), (), s32[]{:S(2)}) async-start(), calls=%async_computation.43 | async-start | bytes 17301504 | tf_op jit(solution)/shard_map/while/body/eval_jaxpr/reduce_scatter | solution.py:467
  1381.5 1800.0 %reduce-scatter.45.cloned.1.call-start = ((), (), s32[]{:S(2)}) async-start(), calls=%async_computation.42 | async-start | bytes 17301504 | tf_op jit(solution)/shard_map/while/body/eval_jaxpr/reduce_scatter | solution.py:466
  1392.7 2037.0 %reduce-scatter.41.cloned.1.call-start = ((), (), s32[]{:S(2)}) async-start(), calls=%async_computation.40 | async-start | bytes 25952256 | tf_op jit(solution)/shard_map/while/body/eval_jaxpr/reduce_scatter | solution.py:464
  1410.9 2385.0 %reduce-scatter.37.cloned.1.call-start = ((), (), s32[]{:S(2)}) async-start(), calls=%async_computation.38 | async-start | bytes 17301504 | tf_op jit(solution)/shard_map/while/body/eval_jaxpr/reduce_scatter | solution.py:462
  1422.0 2738.5 %reduce-scatter.39.cloned.1.call-start = ((), (), s32[]{:S(2)}) async-start(), calls=%async_computation.39 | async-start | bytes 17301504 | tf_op jit(solution)/shard_map/while/body/eval_jaxpr/reduce_scatter | solution.py:463
  4337.9 378.8 %all-gather.91.cloned.1.call-start = ((), (), s32[]{:S(2)}) async-start(), calls=%async_computation.28 | async-start | bytes 2621440 | tf_op jit(solution)/shard_map/while/body/eval_jaxpr/all_gather | solution.py:281
  4888.0 372.1 %reduce-scatter.29.cloned.1.call-start = ((), (), s32[]{:S(2)}) async-start(), calls=%async_computation.34 | async-start | bytes 540672 | tf_op jit(solution)/shard_map/while
  4893.7 499.1 %reduce-scatter.25.cloned.1.call-start = ((), (), s32[]{:S(2)}) async-start(), calls=%async_computation.32 | async-start | bytes 540672 | tf_op jit(solution)/shard_map/while/body/eval_jaxpr/reduce_scatter | solution.py:456
  4897.1 641.8 %reduce-scatter.35.cloned.1.call-start = ((), (), s32[]{:S(2)}) async-start(), calls=%async_computation.37 | async-start | bytes 4325376 | tf_op jit(solution)/shard_map/while/body/eval_jaxpr/reduce_scatter | solution.py:461
  4899.8 825.8 %reduce-scatter.43.cloned.1.call-start = ((), (), s32[]{:S(2)}) async-start(), calls=%async_computation.41 | async-start | bytes 8650752 | tf_op jit(solution)/shard_map/while/body/eval_jaxpr/reduce_scatter | solution.py:465
  4907.0 1091.2 %reduce-scatter.33.cloned.1.call-start = ((), (), s32[]{:S(2)}) async-start(), calls=%async_computation.36 | async-start | bytes 12976128 | tf_op jit(solution)/shard_map/while/body/eval_jaxpr/reduce_scatter | solution.py:460
  4915.3 1446.8 %reduce-scatter.47.cloned.1.call-start = ((), (), s32[]{:S(2)}) async-start(), calls=%async_computation.43 | async-start | bytes 17301504 | tf_op jit(solution)/shard_map/while/body/eval_jaxpr/reduce_scatter | solution.py:467
  4926.2 1800.3 %reduce-scatter.45.cloned.1.call-start = ((), (), s32[]{:S(2)}) async-start(), calls=%async_computation.42 | async-start | bytes 17301504 | tf_op jit(solution)/shard_map/while/body/eval_jaxpr/reduce_scatter | solution.py:466
  4937.4 2037.4 %reduce-scatter.41.cloned.1.call-start = ((), (), s32[]{:S(2)}) async-start(), calls=%async_computation.40 | async-start | bytes 25952256 | tf_op jit(solution)/shard_map/while/body/eval_jaxpr/reduce_scatter | solution.py:464
  4955.6 2385.4 %reduce-scatter.37.cloned.1.call-start = ((), (), s32[]{:S(2)}) async-start(), calls=%async_computation.38 | async-start | bytes 17301504 | tf_op jit(solution)/shard_map/while/body/eval_jaxpr/reduce_scatter | solution.py:462
  4966.7 2738.9 %reduce-scatter.39.cloned.1.call-start = ((), (), s32[]{:S(2)}) async-start(), calls=%async_computation.39 | async-start | bytes 17301504 | tf_op jit(solution)/shard_map/while/body/eval_jaxpr/reduce_scatter | solution.py:463
  (420 other events, 65449.1 us)
Sparse Core Ops, SparseCore 0:
  1311.7 136.2 reduce-scatter.30
  1450.3 132.3 reduce-scatter.26
  1585.0 130.1 reduce-scatter.28
  1717.4 130.3 reduce-scatter.24
  1850.0 143.7 reduce-scatter.34
  1996.0 184.4 reduce-scatter.42
  2182.6 270.3 reduce-scatter.32
  2455.3 361.6 reduce-scatter.46
  2819.4 362.1 reduce-scatter.44
  3187.8 241.7 reduce-scatter.40
  3432.1 363.7 reduce-scatter.36
  3798.3 362.1 reduce-scatter.38
  4856.6 136.4 reduce-scatter.30
  4995.3 132.1 reduce-scatter.26
  5129.6 130.4 reduce-scatter.28
  5262.3 130.5 reduce-scatter.24
  5395.0 143.8 reduce-scatter.34
  5541.1 184.4 reduce-scatter.42
  5727.8 270.3 reduce-scatter.32
  6000.5 361.6 reduce-scatter.46
  6364.3 362.1 reduce-scatter.44
  6732.9 241.8 reduce-scatter.40
  6977.2 363.7 reduce-scatter.36
  7343.4 362.1 reduce-scatter.38
  (32 shorter events, 1661.5 us)
where the time goes:
time: 7720 us
  waiting for transfers between devices  6020 us (78%)
  matrix products  851 us (11%)
  blocking collectives  510 us (7%)
  local copies, waits for them, and re-layouts  200 us (3%)
  other arithmetic  108 us (1%)
    reduce_scatter x2, waiting for transfers between devices, step_fn(): lax.psum_scatter(grads[6], ('dp', 'seq'), scatter_dimension=0, tiled=True)  730 us
    reduce_scatter x2, waiting for transfers between devices, step_fn(): lax.psum_scatter(grads[7], ('dp', 'seq'), scatter_dimension=0, tiled=True)  727 us
    reduce_scatter x2, waiting for transfers between devices, step_fn(): lax.psum_scatter(grads[10], ('dp', 'seq'), scatter_dimension=0, tiled=True)  726 us
    reduce_scatter x2, waiting for transfers between devices, step_fn(): lax.psum_scatter(grads[11], ('dp', 'seq'), scatter_dimension=0, tiled=True)  724 us
    while x54, waiting for transfers between devices  545 us
    reduce_scatter x2, waiting for transfers between devices, step_fn(): lax.psum_scatter(grads[4], ('dp', 'seq'), scatter_dimension=1, tiled=True)  543 us
    reduce_scatter x2, waiting for transfers between devices, step_fn(): lax.psum_scatter(grads[8], ('dp', 'seq'), scatter_dimension=1, tiled=True)  494 us
    reduce_scatter x2, waiting for transfers between devices, step_fn(): lax.psum_scatter(grads[9], ('dp', 'seq'), scatter_dimension=1, tiled=True)  371 us
  transfers between devices with their start and end apart: 56, of which 40 were waited for; matrix products, arithmetic and copies ran while one was open for 14% of the time, Pallas kernels for 0%

commit v1 on v0

v1 whole, which is shorter than its diff:
```python
import functools

import jax
import jax.numpy as jnp
from jax import lax
from jax.experimental import pallas as pl
from jax.experimental.pallas import tpu as pltpu
from jax.sharding import PartitionSpec as P

HEAD_DIM = 64
EPSILON = 1e-05
MASKED = -1000000000.0
BLOCK = 256
PAIR = 2 * HEAD_DIM
B16 = jnp.bfloat16
F32 = jnp.float32


def product(left, right):
    return jnp.dot(left, right, preferred_element_type=F32)


def product_tn(left, right):
    return lax.dot_general(left, right, (((0,), (0,)), ((), ())), preferred_element_type=F32)


def product_nt(left, right):
    return lax.dot_general(left, right, (((1,), (1,)), ((), ())), preferred_element_type=F32)


def column_sum(values):
    return jnp.sum(values.astype(F32), axis=0)


def norm_parts(hidden):
    centred = hidden - jnp.mean(hidden, axis=-1, keepdims=True)
    spread = jnp.mean(centred * centred, axis=-1, keepdims=True)
    scale = lax.rsqrt(spread + EPSILON)
    return centred * scale, scale


def layer_norm(hidden, gain_row, shift_row):
    return (norm_parts(hidden)[0] * gain_row + shift_row).astype(B16)


def norm_backward(hidden, gain_row, grad):
    unit, scale = norm_parts(hidden)
    weighted = grad * gain_row
    grad_hidden = scale * (
        weighted
        - jnp.mean(weighted, axis=-1, keepdims=True)
        - unit * jnp.mean(weighted * unit, axis=-1, keepdims=True)
    )
    return grad_hidden, jnp.sum(grad * unit, axis=0), jnp.sum(grad, axis=0)


def gelu_both(values):
    below = 0.5 * (1.0 + lax.erf(values * (0.5**0.5)))
    density = jnp.exp(-0.5 * values * values) * (0.5 / jnp.pi) ** 0.5
    return (values * below).astype(B16), (below + values * density).astype(B16)


def allowed_block(causal, kseg_ref, qseg, length, key_at, query_at):
    allowed = kseg_ref[key_at : key_at + BLOCK, :] == qseg
    if causal:
        keys = key_at + lax.broadcasted_iota(jnp.int32, (BLOCK, BLOCK), 0)
        queries = query_at + lax.broadcasted_iota(jnp.int32, (BLOCK, BLOCK), 1)
        allowed = allowed & (keys <= queries) & ((keys < length) | (keys == queries))
    return allowed


def head_lanes(head, shape):
    lane = lax.broadcasted_iota(jnp.int32, shape, 1)
    return (lane >= head * HEAD_DIM) & (lane < (head + 1) * HEAD_DIM)


def dot_nt(left, right):
    return lax.dot_general(left, right, (((1,), (1,)), ((), ())), preferred_element_type=F32)


def forward_kernel(causal, info_ref, q_ref, k_ref, v_ref, qseg_ref, kseg_ref, o_ref, lse_ref, vt_ref, s_ref, acc_ref, stat_ref):
    block = pl.program_id(1)
    blocks = k_ref.shape[0] // BLOCK
    length = info_ref[blocks * blocks]

    @pl.when(block == 0)
    def _():
        vt_ref[...] = v_ref[...].T

    qseg = qseg_ref[...]
    scaled = q_ref[...] * jnp.asarray(HEAD_DIM**-0.5, B16)
    zero = jnp.zeros_like(scaled)
    heads = [jnp.where(head_lanes(h, scaled.shape), scaled, zero) for h in range(2)]
    stat_ref[0:16, :] = jnp.full((16, BLOCK), -1e30, F32)
    stat_ref[16:32, :] = jnp.zeros((16, BLOCK), F32)
    acc_ref[...] = jnp.zeros_like(acc_ref)
    for j in range(blocks):

        @pl.when(info_ref[block * blocks + j] > 0)
        def _(j=j):
            keys = k_ref[j * BLOCK : (j + 1) * BLOCK, :]
            allowed = allowed_block(causal, kseg_ref, qseg, length, j * BLOCK, block * BLOCK)
            for h in range(2):
                scores = jnp.where(allowed, dot_nt(keys, heads[h]), MASKED)
                s_ref[h, j * BLOCK : (j + 1) * BLOCK, :] = scores
                top = jnp.max(scores.reshape(BLOCK // 8, 8, BLOCK), axis=0)
                stat_ref[h * 8 : h * 8 + 8, :] = jnp.maximum(stat_ref[h * 8 : h * 8 + 8, :], top)

    highest = [jnp.max(stat_ref[h * 8 : h * 8 + 8, :], axis=0, keepdims=True) for h in range(2)]
    for j in range(blocks):

        @pl.when(info_ref[block * blocks + j] > 0)
        def _(j=j):
            for h in range(2):
                weights = jnp.exp(s_ref[h, j * BLOCK : (j + 1) * BLOCK, :] - highest[h])
                total = jnp.sum(weights.reshape(BLOCK // 8, 8, BLOCK), axis=0)
                stat_ref[16 + h * 8 : 24 + h * 8, :] += total
                rows = pl.ds(h * HEAD_DIM, HEAD_DIM)
                acc_ref[rows, :] += jnp.dot(
                    vt_ref[rows, j * BLOCK : (j + 1) * BLOCK],
                    weights.astype(B16),
                    preferred_element_type=F32,
                )

    lse_ref[...] = jnp.zeros_like(lse_ref)
    for h in range(2):
        total = jnp.sum(stat_ref[16 + h * 8 : 24 + h * 8, :], axis=0, keepdims=True)
        rows = pl.ds(h * HEAD_DIM, HEAD_DIM)
        acc_ref[rows, :] = acc_ref[rows, :] / total
        lse_ref[0, h : h + 1, :] = highest[h] + jnp.log(total)
    o_ref[...] = acc_ref[...].T.astype(B16)


def backward_kernel(
    causal,
    info_ref,
    q_ref,
    k_ref,
    v_ref,
    o_ref,
    do_ref,
    lse_ref,
    qseg_ref,
    kseg_ref,
    dq_ref,
    dk_ref,
    dv_ref,
    kt_ref,
    dqt_ref,
    sums_ref,
):
    block = pl.program_id(1)
    blocks = k_ref.shape[0] // BLOCK
    length = info_ref[blocks * blocks]

    @pl.when(block == 0)
    def _():
        kt_ref[...] = k_ref[...].T
        sums_ref[...] = jnp.zeros_like(sums_ref)

    qseg = qseg_ref[...]
    scaled = q_ref[...] * jnp.asarray(HEAD_DIM**-0.5, B16)
    grads = do_ref[...]
    zero = jnp.zeros_like(scaled)
    lanes = [head_lanes(h, scaled.shape) for h in range(2)]
    query_heads = [jnp.where(lanes[h], scaled, zero) for h in range(2)]
    grad_heads = [jnp.where(lanes[h], grads, zero) for h in range(2)]
    mixed = grads.astype(F32) * o_ref[...].astype(F32)
    picks = jnp.concatenate(
        [head_lanes(h, (8, PAIR)).astype(F32) for h in range(2)], axis=0
    )
    inner_both = lax.dot_general(
        picks, mixed, (((1,), (1,)), ((), ())), precision=lax.Precision.HIGHEST, preferred_element_type=F32
    )
    inner = [inner_both[8 * h : 8 * h + 1, :] for h in range(2)]
    lse = [lse_ref[0, h : h + 1, :] for h in range(2)]
    dqt_ref[...] = jnp.zeros_like(dqt_ref)
    for j in range(blocks):

        @pl.when(info_ref[block * blocks + j] > 0)
        def _(j=j):
            rows = slice(j * BLOCK, (j + 1) * BLOCK)
            keys = k_ref[rows, :]
            values = v_ref[rows, :]
            allowed = allowed_block(causal, kseg_ref, qseg, length, j * BLOCK, block * BLOCK)
            key_sum = sums_ref[0, rows, :]
            value_sum = sums_ref[1, rows, :]
            for h in range(2):
                scores = dot_nt(keys, query_heads[h])
                chances = jnp.where(allowed, jnp.exp(scores - lse[h]), 0.0)
                grad_chances = dot_nt(values, grad_heads[h])
                grad_scores = (chances * (grad_chances - inner[h])).astype(B16)
                value_sum += jnp.dot(chances.astype(B16), grad_heads[h], preferred_element_type=F32)
                key_sum += jnp.dot(grad_scores, query_heads[h], preferred_element_type=F32)
                part = pl.ds(h * HEAD_DIM, HEAD_DIM)
                dqt_ref[part, :] += jnp.dot(kt_ref[part, rows], grad_scores, preferred_element_type=F32)
            sums_ref[0, rows, :] = key_sum
            sums_ref[1, rows, :] = value_sum

    dq_ref[...] = (dqt_ref[...].T * HEAD_DIM**-0.5).astype(B16)

    @pl.when(block == blocks - 1)
    def _():
        dk_ref[...] = sums_ref[0].astype(B16)
        dv_ref[...] = sums_ref[1].astype(B16)


def block_info(causal, query_seg, key_seg, length):
    blocks = query_seg.shape[0] // BLOCK
    query_low, query_high = query_seg[::BLOCK], query_seg[BLOCK - 1 :: BLOCK]
    key_low, key_high = key_seg[::BLOCK], key_seg[BLOCK - 1 :: BLOCK]
    meets = (key_low[None, :] <= query_high[:, None]) & (key_high[None, :] >= query_low[:, None])
    if causal:
        at = jnp.arange(blocks)
        meets = meets & (at[None, :] <= at[:, None])
    return jnp.concatenate([meets.astype(jnp.int32).reshape(-1), length[None]])


def attention_specs(count, offsets):
    query = pl.BlockSpec((BLOCK, PAIR), lambda p, i, info: (i, p + offsets[0]))
    key = pl.BlockSpec((count, PAIR), lambda p, i, info: (0, p + offsets[1]))
    value = pl.BlockSpec((count, PAIR), lambda p, i, info: (0, p + offsets[2]))
    plain = pl.BlockSpec((BLOCK, PAIR), lambda p, i, info: (i, p))
    whole = pl.BlockSpec((count, PAIR), lambda p, i, info: (0, p))
    stats = pl.BlockSpec((1, 8, BLOCK), lambda p, i, info: (p, 0, i))
    qseg = pl.BlockSpec((1, BLOCK), lambda p, i, info: (0, i))
    kseg = pl.BlockSpec((count, 1), lambda p, i, info: (0, 0))
    return query, key, value, plain, whole, stats, qseg, kseg


def attend_forward(causal, masks, queries, keys, values, offsets, width):
    info, qseg_row, kseg_column = masks
    count = queries.shape[0]
    pairs = width // PAIR
    query, key, value, plain, _, stats, qseg, kseg = attention_specs(count, offsets)
    return pl.pallas_call(
        functools.partial(forward_kernel, causal),
        grid_spec=pltpu.PrefetchScalarGridSpec(
            num_scalar_prefetch=1,
            grid=(pairs, count // BLOCK),
            in_specs=[query, key, value, qseg, kseg],
            out_specs=[plain, stats],
            scratch_shapes=[pltpu.VMEM((PAIR, count), B16), pltpu.VMEM((2, count, BLOCK), F32), pltpu.VMEM((PAIR, BLOCK), F32), pltpu.VMEM((32, BLOCK), F32)],
        ),
        out_shape=[
            jax.ShapeDtypeStruct((count, width), B16),
            jax.ShapeDtypeStruct((pairs, 8, count), F32),
        ],
        compiler_params=pltpu.CompilerParams(vmem_limit_bytes=24 * 2**20),
        cost_estimate=pl.CostEstimate(
            flops=2 * 2 * count * count * width * 2, bytes_accessed=count * width * 8, transcendentals=0
        ),
        name="attend_causal" if causal else "attend",
    )(info, queries, keys, values, qseg_row, kseg_column)


def attend_backward(causal, masks, queries, keys, values, offsets, width, mixed, lse, grad):
    info, qseg_row, kseg_column = masks
    count = queries.shape[0]
    pairs = width // PAIR
    query, key, value, plain, whole, stats, qseg, kseg = attention_specs(count, offsets)
    return pl.pallas_call(
        functools.partial(backward_kernel, causal),
        grid_spec=pltpu.PrefetchScalarGridSpec(
            num_scalar_prefetch=1,
            grid=(pairs, count // BLOCK),
            in_specs=[query, key, value, plain, plain, stats, qseg, kseg],
            out_specs=[plain, whole, whole],
            scratch_shapes=[
                pltpu.VMEM((PAIR, count), B16),
                pltpu.VMEM((PAIR, BLOCK), F32),
                pltpu.VMEM((2, count, PAIR), F32),
            ],
        ),
        out_shape=[jax.ShapeDtypeStruct((count, width), B16)] * 3,
        compiler_params=pltpu.CompilerParams(vmem_limit_bytes=24 * 2**20),
        cost_estimate=pl.CostEstimate(
            flops=5 * 2 * count * count * width * 2, bytes_accessed=count * width * 16, transcendentals=0
        ),
        name="attend_grad_causal" if causal else "attend_grad",
    )(info, queries, keys, values, mixed, grad, lse, qseg_row, kseg_column)


def xor_arrange(pieces, place):
    pieces, bit = list(pieces), 0
    while 1 << bit < len(pieces):
        odd = ((place >> bit) & 1) == 1
        pieces = [jnp.where(odd, pieces[k ^ (1 << bit)], pieces[k]) for k in range(len(pieces))]
        bit += 1
    return pieces


class Place:
    def __init__(self, dp, seq):
        self.dp, self.seq = dp, seq
        self.at = lax.axis_index("dp")
        self.z = lax.axis_index("seq")
        self.core = self.at % 2
        self.x = (self.at // 2) % 2
        self.y = self.at // 4

    def over_dp(self, value, mask):
        return lax.ppermute(value, "dp", [(i, i ^ mask) for i in range(self.dp)])

    def over_seq(self, value, mask):
        return lax.ppermute(value, "seq", [(i, i ^ mask) for i in range(self.seq)])

    def over_core(self, value):
        return self.over_dp(value, 1)

    def row_in(self, array):
        parts = array.reshape(2, array.shape[1], 2, -1)
        got = []
        for m in range(4):
            code = self.z ^ m
            piece = lax.dynamic_index_in_dim(parts, code // 2, 0, keepdims=False)
            piece = lax.dynamic_index_in_dim(piece, code % 2, 1, keepdims=False)
            moves = []
            for d in range(self.dp):
                for z in range(4):
                    q = m ^ z
                    moves.append((d * 4 + z, (d - d % 2 + q % 2) * 4 + 2 * (d % 2) + q // 2))
            got.append(lax.ppermute(piece, ("dp", "seq"), moves))
        half = jnp.concatenate(xor_arrange(got, (self.z % 2) * 2 + self.core), axis=0)
        return jnp.concatenate(xor_arrange([half, self.over_core(half)], self.core), axis=1)

    def row_out(self, row):
        parts = row.reshape(4, -1, 2, row.shape[1] // 2)
        mine = lax.dynamic_index_in_dim(parts, self.core, 2, keepdims=False)
        q_here = (self.z % 2) * 2 + self.core
        got = []
        for m in range(4):
            piece = lax.dynamic_index_in_dim(mine, q_here ^ m, 0, keepdims=False)
            moves = []
            for d in range(self.dp):
                for z in range(4):
                    q = (z % 2) * 2 + d % 2
                    moves.append((d * 4 + z, (d - d % 2 + z // 2) * 4 + (m ^ q)))
            got.append(lax.ppermute(piece, ("dp", "seq"), moves))
        placed = xor_arrange(got, self.z)
        return jnp.stack([jnp.concatenate(placed[2 * i : 2 * i + 2], axis=1) for i in range(2)])

    def both_cores(self, part):
        part = part.astype(B16)
        return part.astype(F32) + self.over_core(part).astype(F32)


def own_columns(array, core, runs=8):
    split = array.reshape(array.shape[:-1] + (runs // 2, 2, array.shape[-1] // runs))
    mine = lax.dynamic_index_in_dim(split, core, split.ndim - 2, keepdims=False)
    return mine.reshape(array.shape[:-1] + (array.shape[-1] // 2,))


def lay_side(array):
    return jnp.concatenate([array[i] for i in range(array.shape[0])], axis=1)


class Tree:
    def __init__(self, place):
        self.place = place

    def gather(self, local, x_first):
        place = self.place
        pieces = [local] + [place.over_seq(local, j) for j in range(1, 4)]
        held = jnp.stack(xor_arrange(pieces, place.z))
        if x_first:
            held = jnp.stack(xor_arrange([held, place.over_dp(held, 2)], place.x))
            return jnp.stack(xor_arrange([held, place.over_dp(held, 4)], place.y))
        held = jnp.stack(xor_arrange([held, place.over_dp(held, 4)], place.y))
        return jnp.stack(xor_arrange([held, place.over_dp(held, 2)], place.x), axis=1)

    def by_columns(self, local, x_first):
        core = self.place.core
        mine = lay_side(own_columns(local, core))
        other = lay_side(own_columns(local, 1 - core))
        both = jnp.stack(xor_arrange([mine, self.place.over_core(other)], core))
        full = self.gather(both, x_first)
        return full.transpose(0, 1, 3, 2, 4, 5).reshape(-1, full.shape[-1])

    def by_rows(self, local, x_first):
        return self.gather(local, x_first).reshape(-1, local.shape[-1])

    def sum_chips(self, features, grad, x_first):
        place = self.place
        count, size = features.shape
        quarter = size // 4
        split = features.reshape(count, 2, 2, quarter)
        axis, here, mask = (2, place.x, 2) if x_first else (1, place.y, 4)
        here_two, mask_two = (place.y, 4) if x_first else (place.x, 2)

        def part(index):
            cut = lax.dynamic_index_in_dim(split, index, axis, keepdims=False)
            return product_tn(cut.reshape(count, size // 2), grad)

        sent = place.over_dp(part(1 - here).astype(B16), mask)
        kept = (part(here) + sent.astype(F32)).astype(B16).reshape(2, quarter, grad.shape[1])
        away = lax.dynamic_index_in_dim(kept, 1 - here_two, 0, keepdims=False)
        stay = lax.dynamic_index_in_dim(kept, here_two, 0, keepdims=False)
        return (stay.astype(F32) + place.over_dp(away, mask_two).astype(F32)).astype(B16)

    def sum_z(self, value, axis):
        place = self.place
        total = lax.dynamic_index_in_dim(value, place.z, axis, keepdims=False).astype(F32)
        for j in range(1, 4):
            piece = lax.dynamic_index_in_dim(value, place.z ^ j, axis, keepdims=False)
            total = total + place.over_seq(piece, j).astype(F32)
        return total

    def grad_by_columns(self, features, grad, x_first, parts):
        place = self.place
        value = self.sum_chips(features, grad, x_first)
        rows = value.shape[0] // 8
        total = self.sum_z(value.reshape(2, 4, rows, value.shape[1]), 1)
        mine = lax.dynamic_index_in_dim(total, place.core, 0, keepdims=False)
        other = lax.dynamic_index_in_dim(total, 1 - place.core, 0, keepdims=False).astype(B16)
        got = place.over_core(other).astype(F32)
        both = [v.reshape(rows, parts, 4, -1) for v in xor_arrange([mine, got], place.core)]
        return jnp.stack(both, axis=3).reshape(rows, parts, -1).transpose(1, 0, 2)

    def grad_by_rows(self, features, grad, x_first):
        value = self.sum_chips(features, grad, x_first)
        return self.sum_z(value.reshape(4, -1, value.shape[1]), 0)

    def small(self, table, hidden):
        place = self.place
        n, m = table.shape[0], hidden.shape[0]
        both = jnp.concatenate(
            [
                table.reshape(n, 2, 2, 4, -1).transpose(1, 2, 3, 0, 4).reshape(2, 2, 4, -1),
                hidden.reshape(m, 2, 2, 4, -1).transpose(1, 2, 3, 0, 4).reshape(2, 2, 4, -1),
            ],
            axis=-1,
        )
        for here, mask in ((place.y, 4), (place.x, 2)):
            away = lax.dynamic_index_in_dim(both, 1 - here, 0, keepdims=False)
            both = lax.dynamic_index_in_dim(both, here, 0, keepdims=False) + place.over_dp(away, mask)
        flat = self.sum_z(both, 0)
        edge = table.shape[1] // 16 * n
        return flat[:edge].reshape(n, -1), flat[edge:].reshape(m, -1)


class Plain:
    def __init__(self, place):
        self.place = place
        self.axes = ("dp", "seq")

    def by_columns(self, local, x_first):
        full = lax.all_gather(local, self.axes, axis=1, tiled=True)
        return lay_side(own_columns(full, self.place.core))

    def by_rows(self, local, x_first):
        full = lax.all_gather(local, self.axes, axis=0, tiled=True)
        split = full.reshape(4, 2, full.shape[0] // 8, full.shape[1])
        return lax.dynamic_index_in_dim(split, self.place.core, 1, keepdims=False).reshape(-1, full.shape[1])

    def spread(self, half, axis):
        shape = half.shape[:axis] + (4, 1, half.shape[axis] // 4) + half.shape[axis + 1 :]
        half = half.reshape(shape)
        empty = jnp.zeros_like(half)
        first = jnp.where(self.place.core == 0, half, empty)
        second = jnp.where(self.place.core == 1, half, empty)
        both = jnp.concatenate([first, second], axis=axis + 1)
        return both.reshape(shape[:axis] + (-1,) + shape[axis + 3 :])

    def grad_by_columns(self, features, grad, x_first, parts):
        full = product_tn(features, grad)
        full = full.reshape(full.shape[0], parts, -1).transpose(1, 0, 2).astype(B16)
        full = self.spread(full, 2)
        return lax.psum_scatter(full, self.axes, scatter_dimension=1, tiled=True).astype(F32)

    def grad_by_rows(self, features, grad, x_first):
        full = self.spread(product_tn(features, grad).astype(B16), 0)
        return lax.psum_scatter(full, self.axes, scatter_dimension=0, tiled=True).astype(F32)

    def small(self, table, hidden):
        return tuple(
            lax.psum_scatter(self.spread(v, 1), self.axes, scatter_dimension=1, tiled=True)
            for v in (table, hidden)
        )


def on_device(
    dp,
    seq,
    src_x,
    tgt_x,
    src_seg,
    tgt_seg,
    tgt_len,
    src_lang,
    tgt_lang,
    lang_table,
    gains,
    biases,
    ff_biases,
    enc_proj,
    enc_oproj,
    enc_in,
    enc_out,
    dec_proj,
    dec_oproj,
    dec_in,
    dec_out,
    src_cot,
    tgt_cot,
):
    place = Place(dp, seq)
    core = place.core
    moves = Tree(place) if (dp, seq) == (8, 4) else Plain(place)
    width = enc_oproj.shape[1]
    half = width // 2
    langs = lang_table.shape[0]

    n_small = langs + gains.shape[0] + biases.shape[0]
    table = jnp.concatenate([lang_table, gains, biases], axis=0)
    flat = jnp.concatenate([table.reshape(-1), ff_biases.reshape(-1)])
    everything = lax.all_gather(flat, ("dp", "seq"), axis=0, tiled=False)
    edge = table.size
    table = everything[:, :edge].reshape(dp * seq, n_small, -1).transpose(1, 0, 2).reshape(n_small, width)
    ffb = everything[:, edge:].reshape(dp * seq, 2, -1).transpose(1, 0, 2).reshape(2, -1)
    languages = table[:langs]
    gain_f = table[langs : langs + gains.shape[0]].astype(F32)
    bias_f = table[langs + gains.shape[0] :].astype(F32)
    ffb_own = own_columns(ffb.astype(F32), core)
    bias_own = own_columns(bias_f, core)

    meta = jnp.concatenate([src_seg, tgt_seg, tgt_len[:, None], src_lang, tgt_lang], axis=1)
    rows = jnp.where(place.z // 2 == core, meta, place.over_core(meta))
    row = lax.dynamic_index_in_dim(rows, place.z % 2, 0, keepdims=False)
    count, segs = src_seg.shape[1], src_lang.shape[1]
    s_seg, t_seg, t_len = row[:count], row[count : 2 * count], row[2 * count]
    s_lang, t_lang = row[2 * count + 1 : 2 * count + 1 + segs], row[2 * count + 1 + segs :]

    def onehot(segments, chosen):
        member = segments[:, None] == jnp.arange(segs, dtype=jnp.int32)[None, :]
        token = jnp.sum(jnp.where(member, chosen[None, :], 0), axis=1)
        return (token[:, None] == jnp.arange(langs, dtype=jnp.int32)[None, :]).astype(B16)

    src_hot, tgt_hot = onehot(s_seg, s_lang), onehot(t_seg, t_lang)
    enc_masks = (block_info(False, s_seg, s_seg, t_len), s_seg[None, :], s_seg[:, None])
    dec_masks = (block_info(True, t_seg, t_seg, t_len), t_seg[None, :], t_seg[:, None])
    cross_masks = (block_info(False, t_seg, s_seg, t_len), t_seg[None, :], s_seg[:, None])

    source = place.row_in(src_x)
    target = place.row_in(tgt_x)
    target_cot = place.row_in(tgt_cot)
    source_cot = place.row_in(src_cot)

    enc_qkv_w = moves.by_columns(enc_proj, True)
    enc_o_w = moves.by_rows(enc_oproj, False)
    enc_in_w = moves.by_columns(enc_in[None], False)
    enc_out_w = moves.by_rows(enc_out, True)
    dec_qkv_w = moves.by_columns(dec_proj[0:3], False)
    dec_o_w = moves.by_rows(dec_oproj[0], True)
    cross_w = moves.by_columns(dec_proj[3:6], True)
    cross_o_w = moves.by_rows(dec_oproj[1], False)
    dec_in_w = moves.by_columns(dec_in[None], False)
    dec_out_w = moves.by_rows(dec_out, True)

    none = jnp.zeros((half,), F32)
    packed = (0, half // PAIR, 2 * half // PAIR)

    enc_h0 = source.astype(F32) + product(src_hot, languages)
    enc_n1 = layer_norm(enc_h0, gain_f[0], bias_f[0])
    enc_qkv_bias = jnp.concatenate([bias_own[1], none, bias_own[2]])
    enc_qkv = (product(enc_n1, enc_qkv_w) + enc_qkv_bias).astype(B16)
    enc_mixed, enc_lse = attend_forward(False, enc_masks, enc_qkv, enc_qkv, enc_qkv, packed, half)
    enc_h1 = enc_h0 + place.both_cores(product(enc_mixed, enc_o_w)) + bias_f[3]
    enc_n2 = layer_norm(enc_h1, gain_f[1], bias_f[4])
    enc_acted, enc_slope = gelu_both(product(enc_n2, enc_in_w) + ffb_own[0])
    encoded = enc_h1 + place.both_cores(product(enc_acted, enc_out_w)) + bias_f[5]
    memory = encoded.astype(B16)

    dec_h0 = target.astype(F32) + product(tgt_hot, languages)
    dec_n1 = layer_norm(dec_h0, gain_f[2], bias_f[6])
    dec_qkv_bias = jnp.concatenate([bias_own[7], none, bias_own[8]])
    dec_qkv = (product(dec_n1, dec_qkv_w) + dec_qkv_bias).astype(B16)
    dec_mixed, dec_lse = attend_forward(True, dec_masks, dec_qkv, dec_qkv, dec_qkv, packed, half)
    dec_h1 = dec_h0 + place.both_cores(product(dec_mixed, dec_o_w)) + bias_f[9]
    dec_n2 = layer_norm(dec_h1, gain_f[3], bias_f[10])
    cross_q = (product(dec_n2, cross_w[:, :half]) + bias_own[11]).astype(B16)
    cross_kv_bias = jnp.concatenate([none, bias_own[12]])
    cross_kv = (product(memory, cross_w[:, half:]) + cross_kv_bias).astype(B16)
    apart = (0, 0, half // PAIR)
    cross_mixed, cross_lse = attend_forward(False, cross_masks, cross_q, cross_kv, cross_kv, apart, half)
    dec_h2 = dec_h1 + place.both_cores(product(cross_mixed, cross_o_w)) + bias_f[13]
    dec_n3 = layer_norm(dec_h2, gain_f[4], bias_f[14])
    dec_acted, dec_slope = gelu_both(product(dec_n3, dec_in_w) + ffb_own[1])
    decoded = dec_h2 + place.both_cores(product(dec_acted, dec_out_w)) + bias_f[15]

    dec_du = (product_nt(target_cot, dec_out_w) * dec_slope.astype(F32)).astype(B16)
    dec_dn3 = place.both_cores(product_nt(dec_du, dec_in_w))
    dec_out_grad = moves.grad_by_rows(dec_acted, target_cot, True)
    dec_in_grad = moves.grad_by_columns(dec_n3, dec_du, False, 1)[0]
    target_cot_f = target_cot.astype(F32)
    step, gain_four, shift_14 = norm_backward(dec_h2, gain_f[4], dec_dn3)
    grad_h2 = target_cot_f + step

    cross_branch = grad_h2.astype(B16)
    cross_do = product_nt(cross_branch, cross_o_w).astype(B16)
    cross_dq, cross_dk, cross_dv = attend_backward(
        False, cross_masks, cross_q, cross_kv, cross_kv, apart, half, cross_mixed, cross_lse, cross_do
    )
    cross_dkv = jnp.concatenate([cross_dk, cross_dv], axis=1)
    grad_memory = place.both_cores(product_nt(cross_dkv, cross_w[:, half:]))
    dec_dn2 = place.both_cores(product_nt(cross_dq, cross_w[:, :half]))
    cross_o_grad = moves.grad_by_rows(cross_mixed, cross_branch, True)
    cross_q_grad = moves.grad_by_columns(dec_n2, cross_dq, True, 1)
    cross_kv_grad = moves.grad_by_columns(memory, cross_dkv, False, 2)

    source_cot_f = source_cot.astype(F32) + grad_memory
    enc_ff_branch = source_cot_f.astype(B16)
    enc_du = (product_nt(enc_ff_branch, enc_out_w) * enc_slope.astype(F32)).astype(B16)
    enc_dn2 = place.both_cores(product_nt(enc_du, enc_in_w))
    enc_out_grad = moves.grad_by_rows(enc_acted, enc_ff_branch, True)
    enc_in_grad = moves.grad_by_columns(enc_n2, enc_du, False, 1)[0]

    step, gain_three, shift_10 = norm_backward(dec_h1, gain_f[3], dec_dn2)
    grad_h1 = grad_h2 + step
    self_branch = grad_h1.astype(B16)
    dec_do = product_nt(self_branch, dec_o_w).astype(B16)
    dec_dqkv = jnp.concatenate(
        attend_backward(
            True, dec_masks, dec_qkv, dec_qkv, dec_qkv, packed, half, dec_mixed, dec_lse, dec_do
        ),
        axis=1,
    )
    dec_dn1 = place.both_cores(product_nt(dec_dqkv, dec_qkv_w))
    dec_o_grad = moves.grad_by_rows(dec_mixed, self_branch, False)
    dec_qkv_grad = moves.grad_by_columns(dec_n1, dec_dqkv, True, 3)
    step, gain_two, shift_6 = norm_backward(dec_h0, gain_f[2], dec_dn1)
    target_grad = grad_h1 + step

    step, gain_one, shift_4 = norm_backward(enc_h1, gain_f[1], enc_dn2)
    grad_e1 = source_cot_f + step
    enc_branch = grad_e1.astype(B16)
    enc_do = product_nt(enc_branch, enc_o_w).astype(B16)
    enc_dqkv = jnp.concatenate(
        attend_backward(
            False, enc_masks, enc_qkv, enc_qkv, enc_qkv, packed, half, enc_mixed, enc_lse, enc_do
        ),
        axis=1,
    )
    enc_dn1 = place.both_cores(product_nt(enc_dqkv, enc_qkv_w))
    enc_o_grad = moves.grad_by_rows(enc_mixed, enc_branch, False)
    enc_qkv_grad = moves.grad_by_columns(enc_n1, enc_dqkv, True, 3)
    step, gain_zero, shift_0 = norm_backward(enc_h0, gain_f[0], enc_dn1)
    source_grad = grad_e1 + step

    def split_two(value):
        high = value.astype(B16)
        return high, (value - high.astype(F32)).astype(B16)

    lang_grad = 0.0
    for hot, value in ((src_hot, source_grad), (tgt_hot, target_grad)):
        for piece in split_two(own_columns(value, core)):
            lang_grad = lang_grad + product_tn(hot, piece)
    own = functools.partial(own_columns, core=core)
    gain_rows = jnp.stack([gain_zero, gain_one, gain_two, gain_three, gain_four])
    enc_qkv_sum, dec_qkv_sum = column_sum(enc_dqkv), column_sum(dec_dqkv)
    bias_rows = jnp.stack(
        [
            own(shift_0),
            enc_qkv_sum[:half],
            enc_qkv_sum[2 * half :],
            own(column_sum(enc_branch)),
            own(shift_4),
            own(column_sum(enc_ff_branch)),
            own(shift_6),
            dec_qkv_sum[:half],
            dec_qkv_sum[2 * half :],
            own(column_sum(self_branch)),
            own(shift_10),
            column_sum(cross_dq),
            column_sum(cross_dv),
            own(column_sum(cross_branch)),
            own(shift_14),
            own(column_sum(target_cot)),
        ]
    )
    small, ffb_grad = moves.small(
        jnp.concatenate([lang_grad, own(gain_rows), bias_rows], axis=0),
        jnp.stack([column_sum(enc_du), column_sum(dec_du)]),
    )
    return (
        place.row_out(memory),
        place.row_out(decoded.astype(B16)),
        place.row_out(source_grad.astype(B16)).astype(F32),
        place.row_out(target_grad.astype(B16)).astype(F32),
        small[:langs],
        small[langs : langs + 5],
        small[langs + 5 :],
        ffb_grad,
        enc_qkv_grad,
        enc_o_grad,
        enc_in_grad,
        enc_out_grad,
        jnp.concatenate([dec_qkv_grad, cross_q_grad, cross_kv_grad], axis=0),
        jnp.stack([dec_o_grad, cross_o_grad]),
        dec_in_grad,
        dec_out_grad,
    )


def solution(mesh):
    rows = P("dp", "seq", None)
    columns = P(None, ("dp", "seq"))
    middle = P(None, ("dp", "seq"), None)
    first = P(("dp", "seq"), None)
    weights = (columns, columns, columns, columns, middle, first, first, first, middle, middle, first, first)
    return jax.shard_map(
        functools.partial(on_device, mesh.shape["dp"], mesh.shape["seq"]),
        mesh=mesh,
        in_specs=(rows, rows, P("dp", None), P("dp", None), P("dp"), P("dp", None), P("dp", None))
        + weights
        + (rows, rows),
        out_specs=(rows, rows, rows, rows) + weights,
        check_vma=False,
    )
```

time: 7720 us -> 1650 us (0.21)
  waiting for transfers between devices: 6020 us -> 542 us
  matrix products: 851 us -> 170 us
  blocking collectives: 510 us -> 0 us
  starting transfers between devices: 4.42 us -> 255 us
  Pallas kernels: 0 us -> 183 us
  local copies, waits for them, and re-layouts: 200 us -> 296 us
    reduce_scatter x18 -> x0, waiting for transfers between devices: 4870 us -> none  [the longest x2 730 us: step_fn(): lax.psum_scatter(grads[6], ('dp', 'seq'), scatter_dimension=0, tiled=True)]
    all_gather x32 -> x0, waiting for transfers between devices: 600 us -> none  [the longest x1 97.4 us: on_device(): lax.all_gather(dec_proj, ('dp', 'seq'), axis=1, tiled=True)]
    dot_general x82 -> x13, matrix products: 597 us -> 50 us  [product(): return jnp.dot(left, right, preferred_element_type=F32)]
    while x54 -> x0, waiting for transfers between devices: 545 us -> none
    all_gather x22 -> x0, blocking collectives: 510 us -> none  [the longest x1 72.4 us: on_device(): lax.all_gather(lang_table, ('dp', 'seq'), axis=1, tiled=True)]
    ppermute x0 -> x169, waiting for transfers between devices: none -> 467 us  [the longest x71 263 us: over_dp(): return lax.ppermute(value, 'dp', [(i, i ^ mask) for i in range(self.dp)])]
    ppermute x0 -> x169, starting transfers between devices: none -> 255 us  [the longest x66 111 us: over_seq(): return lax.ppermute(value, 'seq', [(i, i ^ mask) for i in range(self.seq)])]
    pallas_call x0 -> x6, Pallas kernels: none -> 183 us  [the longest x3 109 us: attend_backward(): pl.pallas_call(functools.partial(backward_kernel, causal), grid_spec=pltp...]
  transfers between devices with their start and end apart: 56 -> 170, of which waited for: 40 -> 53; matrix products, arithmetic and copies ran while one was open for 14% -> 35% of each run, Pallas kernels for 0% -> 10%
where the time goes in v1:
time: 1650 us; the launch traced here: 1640 us
  waiting for transfers between devices  542 us (33%)
  local copies, waits for them, and re-layouts  296 us (18%)
  starting transfers between devices  255 us (15%)
  Pallas kernels  183 us (11%)
  other arithmetic  173 us (10%)
  matrix products  170 us (10%)
  between operations  19.4 us (1%)
    ppermute x71, waiting for transfers between devices, over_dp(): return lax.ppermute(value, 'dp', [(i, i ^ mask) for i in range(self.dp)])  263 us
    ppermute x66, waiting for transfers between devices, over_seq(): return lax.ppermute(value, 'seq', [(i, i ^ mask) for i in range(self.seq)])  171 us
    ppermute x66, starting transfers between devices, over_seq(): return lax.ppermute(value, 'seq', [(i, i ^ mask) for i in range(self.seq)])  111 us
    pallas_call x3, Pallas kernels, attend_backward(): pl.pallas_call(functools.partial(backward_kernel, causal), grid_spec=pltp...  109 us
    unnamed x577, local copies, waits for them, and re-layouts  83.8 us
    unnamed x2, waiting for transfers between devices  74.6 us
    pallas_call x3, Pallas kernels, attend_forward(): pl.pallas_call(functools.partial(forward_kernel, causal), grid_spec=pltpu...  73.9 us
    dot_general x26, matrix products, product_tn(): lax.dot_general(left, right, (((0,), (0,)), ((), ())), preferred_element_...  64 us
  transfers between devices with their start and end apart: 170, of which 53 were waited for; matrix products, arithmetic and copies ran while one was open for 35% of the time, Pallas kernels for 10%

profile of v1, /device:TPU:0, one launch (start us, length us, event | category | flops | bytes accessed | tf_op | source)
XLA Modules:
  0.0 1638.2 jit_solution(13825956418949045360)
XLA Ops:
  69.6 74.6 %all-reduce.4.cloned.1.call-done = bf16[80896]{0:T(1024)(128)(2,1)} async-done(((bf16[80896]{0:T(1024)(128)(2,1)}), bf16[80896]{0:T(1024)(128)(2,1)}) %all-reduce.4.cloned.1.call-update) | async-done | bytes 161808
  175.2 22.2 %collective-permute-start.34 = (bf16[256,512]{0,1:T(8,128)(2,1)S(1)}, bf16[256,512]{0,1:T(8,128)(2,1)S(1)}, u32[]{:S(2)}, u32[]{:S(2)}) collective-permute-start(bf16[256,512]{0,1:T(8,128)(2,1)S(1)} %copy-done.187), channel_id=1, source_target_pairs={{0,5},{1,1},{2,4},{3,0},{4,7},{5,3},{6,6},{7,2},{8,13},{9,9},{10,1... | collective-permute-start | bytes 786440 | tf_op jit(solution)/shard_map/ppermute | solution.py:323
  226.7 13.4 collective-permute-start.79
  250.9 17.0 %collective-permute-done.80 = bf16[256,512]{0,1:T(8,128)(2,1)S(1)} collective-permute-done((bf16[256,512]{0,1:T(8,128)(2,1)S(1)}, bf16[256,512]{0,1:T(8,128)(2,1)S(1)}, u32[]{:S(2)}, u32[]{:S(2)}) %collective-permute-start.80) | collective-permute-done | bytes 262176 | tf_op jit(solution)/shard_map/ppermute | solution.py:323
  270.7 12.4 collective-permute-start.8
  342.5 16.3 collective-permute-done.20
  372.5 36.8 %collective-permute-done.61 = bf16[2,4,32,1024]{3,2,1,0:T(8,128)(2,1)S(1)} collective-permute-done((bf16[2,4,32,1024]{3,2,1,0:T(8,128)(2,1)S(1)}, bf16[2,4,32,1024]{3,2,1,0:T(8,128)(2,1)S(1)}, u32[]{:S(2)}, u32[]{:S(2)}) %collective-permute-start.61) | collective-permute-done | bytes 524320 | tf_op jit(solution)/shard_map/ppermute | solution.py:303
  433.4 14.4 collective-permute-done.43
  448.6 21.1 %collective-permute-done.55 = bf16[4,2,32,1536]{3,2,1,0:T(8,128)(2,1)S(1)} collective-permute-done((bf16[4,2,32,1536]{3,2,1,0:T(8,128)(2,1)S(1)}, bf16[4,2,32,1536]{3,2,1,0:T(8,128)(2,1)S(1)}, u32[]{:S(2)}, u32[]{:S(2)}) %collective-permute-start.55) | collective-permute-done | bytes 786464 | tf_op jit(solution)/shard_map/ppermute | solution.py:303
  502.2 21.7 %collective-permute-done.67 = bf16[4,2,32,2048]{3,2,1,0:T(8,128)(2,1)S(1)} collective-permute-done((bf16[4,2,32,2048]{3,2,1,0:T(8,128)(2,1)S(1)}, bf16[4,2,32,2048]{3,2,1,0:T(8,128)(2,1)S(1)}, u32[]{:S(2)}, u32[]{:S(2)}) %collective-permute-start.67) | collective-permute-done | bytes 1048608 | tf_op jit(solution)/shard_map/ppermute | solution.py:303
  527.9 29.7 %collective-permute-done.11 = bf16[2,4,2,32,1536]{4,3,2,1,0:T(8,128)(2,1)S(1)} collective-permute-done((bf16[2,4,2,32,1536]{4,3,2,1,0:T(8,128)(2,1)S(1)}, bf16[2,4,2,32,1536]{4,3,2,1,0:T(8,128)(2,1)S(1)}, u32[]{:S(2)}, u32[]{:S(2)}) %collective-permute-start.11) | collective-permute-done | bytes 1572896 | tf_op jit(solution)/shard_map/ppermute | solution.py:303
  566.9 27.3 %attend.2 = (bf16[1024,512]{1,0:T(8,128)(2,1)S(1)}, f32[4,8,1024]{2,1,0:T(8,128)S(1)}) custom-call(s32[17]{0:T(128)S(1)} %pad_add_fusion.info_ref, bf16[1024,1536]{1,0:T(8,128)(2,1)S(1)} %add_convert_fusion.1.q_ref.k_ref.v_ref, bf16[1024,1536]{1,0:T(8,128)(2,1)S(1)} %add_convert_fusion.1.q_ref.k_ref.v_ref, ...), custom_call_target="tpu_custom_call" | custom-call | flops 4294967296 | bytes 4194304 | tf_op jit(solution)/shard_map/attend/pallas_call | solution.py:236
  609.0 21.1 %attend_causal.1 = (bf16[1024,512]{1,0:T(8,128)(2,1)S(1)}, f32[4,8,1024]{2,1,0:T(8,128)S(1)}) custom-call(s32[17]{0:T(128)S(1)} %pad_add_fusion.1.info_ref, bf16[1024,1536]{1,0:T(8,128)(2,1)S(1)} %add_convert_fusion.q_ref.k_ref.v_ref, bf16[1024,1536]{1,0:T(8,128)(2,1)S(1)} %add_convert_fusion.q_ref.k_ref.v_ref, ...), custom_call_target="tpu_custom_call" | custom-call | flops 4294967296 | bytes 4194304 | tf_op jit(solution)/shard_map/attend_causal/pallas_call | solution.py:236
  641.0 39.4 %collective-permute-done.73 = bf16[2,4,128,1024]{3,2,1,0:T(8,128)(2,1)} collective-permute-done((bf16[2,4,128,1024]{3,2,1,0:T(8,128)(2,1)}, bf16[2,4,128,1024]{3,2,1,0:T(8,128)(2,1)}, u32[]{:S(2)}, u32[]{:S(2)}) %collective-permute-start.73) | collective-permute-done | bytes 2097184 | tf_op jit(solution)/shard_map/ppermute | solution.py:303
  736.1 25.5 %attend.3 = (bf16[1024,512]{1,0:T(8,128)(2,1)S(1)}, f32[4,8,1024]{2,1,0:T(8,128)S(1)}) custom-call(s32[17]{0:T(128)S(1)} %pad_add_fusion.2.info_ref, bf16[1024,512]{1,0:T(8,128)(2,1)S(1)} %add_convert_fusion.17.q_ref, bf16[1024,1024]{1,0:T(8,128)(2,1)S(1)} %add_convert_fusion.8.k_ref.v_ref, bf16[1024,1024]{1,0:T(8,128)(2,1)S(1)} %add_convert_fusion.8.k_ref.v_ref, ...), custom_call_target="tpu_custom_call" | custom-call | flops 4294967296 | bytes 4194304 | tf_op jit(solution)/shard_map/attend/pallas_call | solution.py:236
  948.9 37.0 %attend_grad.2 = (bf16[1024,512]{1,0:T(8,128)(2,1)S(1)}, bf16[1024,512]{1,0:T(8,128)(2,1)S(1)}, bf16[1024,512]{1,0:T(8,128)(2,1)S(1)}) custom-call(s32[17]{0:T(128)S(1)} %pad_add_fusion.2.info_ref, bf16[1024,512]{1,0:T(8,128)(2,1)S(1)} %copy-done.22, bf16[1024,1024]{1,0:T(8,128)(2,1)S(1)} %copy-done.24, bf16[1024,1024]{1,0:T(8,128)(2,1)S(1)} %copy-done.24, ...), custom_call_target="tpu_custom_call" | custom-call | flops 10737418240 | bytes 8388608 | tf_op jit(solution)/shard_map/attend_grad/pallas_call | solution.py:262
  1071.9 15.2 collective-permute-done.159
  1100.8 17.5 %collective-permute-done.161 = bf16[2,32,2048]{2,1,0:T(8,128)(2,1)S(1)} collective-permute-done((bf16[2,32,2048]{2,1,0:T(8,128)(2,1)S(1)}, bf16[2,32,2048]{2,1,0:T(8,128)(2,1)S(1)}, u32[]{:S(2)}, u32[]{:S(2)}) %collective-permute-start.161) | collective-permute-done | bytes 262176 | tf_op jit(solution)/shard_map/ppermute | solution.py:306
  1168.0 32.0 %attend_grad_causal.1 = (bf16[1024,512]{1,0:T(8,128)(2,1)S(1)}, bf16[1024,512]{1,0:T(8,128)(2,1)S(1)}, bf16[1024,512]{1,0:T(8,128)(2,1)S(1)}) custom-call(s32[17]{0:T(128)S(1)} %copy-done.16, bf16[1024,1536]{1,0:T(8,128)(2,1)S(1)} %copy-done.20, bf16[1024,1536]{1,0:T(8,128)(2,1)S(1)} %copy-done.20, bf16[1024,1536]{1,0:T(8,128)(2,1)S(1)} %copy-done.20, ...), custom_call_target="tpu_custom_call" | custom-call | flops 10737418240 | bytes 8388608 | tf_op jit(solution)/shard_map/attend_grad_causal/pallas_call | solution.py:262
  1259.9 18.1 %collective-permute-done.149 = bf16[128,1024]{1,0:T(8,128)(2,1)} collective-permute-done((bf16[128,1024]{1,0:T(8,128)(2,1)}, bf16[128,1024]{1,0:T(8,128)(2,1)}, u32[]{:S(2)}, u32[]{:S(2)}) %collective-permute-start.149) | collective-permute-done | bytes 262176 | tf_op jit(solution)/shard_map/ppermute | solution.py:303
  1345.1 40.2 %attend_grad.3 = (bf16[1024,512]{1,0:T(8,128)(2,1)S(1)}, bf16[1024,512]{1,0:T(8,128)(2,1)S(1)}, bf16[1024,512]{1,0:T(8,128)(2,1)S(1)}) custom-call(s32[17]{0:T(128)S(1)} %copy-done.14, bf16[1024,1536]{1,0:T(8,128)(2,1)S(1)} %copy-done.18, bf16[1024,1536]{1,0:T(8,128)(2,1)S(1)} %copy-done.18, bf16[1024,1536]{1,0:T(8,128)(2,1)S(1)} %copy-done.18, ...), custom_call_target="tpu_custom_call" | custom-call | flops 10737418240 | bytes 8388608 | tf_op jit(solution)/shard_map/attend_grad/pallas_call | solution.py:262
  1434.2 13.6 collective-permute-done.131
  1502.9 17.4 %collective-permute-done.122 = bf16[2,32,2048]{2,1,0:T(8,128)(2,1)S(1)} collective-permute-done((bf16[2,32,2048]{2,1,0:T(8,128)(2,1)S(1)}, bf16[2,32,2048]{2,1,0:T(8,128)(2,1)S(1)}, u32[]{:S(2)}, u32[]{:S(2)}) %collective-permute-start.122) | collective-permute-done | bytes 262176 | tf_op jit(solution)/shard_map/ppermute | solution.py:306
  1611.1 16.4 collective-permute-done.111
  (1362 shorter events, 1018.7 us)
Async XLA Ops:
  7.2 136.9 %all-reduce.4.cloned.1.call-start = ((), (), s32[]{:S(2)}) async-start(), calls=%async_computation | async-start | bytes 323584
  59.9 106.3 %collective-permute-start.24 = (bf16[128,1024]{1,0:T(8,128)(2,1)}, bf16[128,1024]{1,0:T(8,128)(2,1)}, u32[]{:S(2)}, u32[]{:S(2)}) collective-permute-start(bf16[128,1024]{1,0:T(8,128)(2,1)} %param.35), channel_id=1, source_target_pairs={{0,3},{1,2},{2,1},{3,0},{4,7},{5,6},{6,5},{7,4},{8,11},{9,10},{10,... | collective-permute-start | bytes 786440 | tf_op jit(solution)/shard_map/ppermute | solution.py:306
  62.8 104.4 %collective-permute-start.25 = (bf16[128,1024]{1,0:T(8,128)(2,1)}, bf16[128,1024]{1,0:T(8,128)(2,1)}, u32[]{:S(2)}, u32[]{:S(2)}) collective-permute-start(bf16[128,1024]{1,0:T(8,128)(2,1)} %param.35), channel_id=1, source_target_pairs={{0,2},{1,3},{2,0},{3,1},{4,6},{5,7},{6,4},{7,5},{8,10},{9,11},{10,... | collective-permute-start | bytes 786440 | tf_op jit(solution)/shard_map/ppermute | solution.py:306
  62.9 105.9 %collective-permute-start.26 = (bf16[128,1024]{1,0:T(8,128)(2,1)}, bf16[128,1024]{1,0:T(8,128)(2,1)}, u32[]{:S(2)}, u32[]{:S(2)}) collective-permute-start(bf16[128,1024]{1,0:T(8,128)(2,1)} %param.35), channel_id=1, source_target_pairs={{0,1},{1,0},{2,3},{3,2},{4,5},{5,4},{6,7},{7,6},{8,9},{9,8},{10,11... | collective-permute-start | bytes 786440 | tf_op jit(solution)/shard_map/ppermute | solution.py:306
  64.3 108.5 %collective-permute-start = (bf16[256,512]{0,1:T(8,128)(2,1)}, bf16[256,512]{0,1:T(8,128)(2,1)}, u32[]{:S(2)}, u32[]{:S(2)}) collective-permute-start(bf16[256,512]{0,1:T(8,128)(2,1)} %get-tuple-element.336), channel_id=1, source_target_pairs={{0,5},{1,1},{2,4},{3,0},{4,7},{5,3},{6,6},{7,2},{8,13},{9,9},{10,1... | collective-permute-start | bytes 786440 | tf_op jit(solution)/shard_map/ppermute | solution.py:323
  66.5 89.0 %collective-permute-start.6 = (bf16[32,1536]{1,0:T(8,128)(2,1)S(1)}, bf16[32,1536]{1,0:T(8,128)(2,1)}, u32[]{:S(2)}, u32[]{:S(2)}) collective-permute-start(bf16[32,1536]{1,0:T(8,128)(2,1)S(1)} %pad_maximum_fusion.46), channel_id=1, source_target_pairs={{0,4},{4,0},{8,12},{12,8},{16,20},{20,16},{24,28},{28,24},{1,5},{5... | collective-permute-start | bytes 294920 | tf_op jit(solution)/shard_map/ppermute | solution.py:303
  358.8 113.2 %collective-permute-start.4 = (bf16[1024,512]{0,1:T(8,128)(2,1)S(1)}, bf16[1024,512]{0,1:T(8,128)(2,1)S(1)}, u32[]{:S(2)}, u32[]{:S(2)}) collective-permute-start(bf16[1024,512]{0,1:T(8,128)(2,1)S(1)} %pad_maximum_fusion.11), channel_id=1, source_target_pairs={{0,4},{4,0},{8,12},{12,8},{16,20},{20,16},{24,28},{28,24},{1,5},{5... | collective-permute-start | bytes 3145736 | tf_op jit(solution)/shard_map/ppermute | solution.py:303
  361.7 116.2 %collective-permute-start.27 = (bf16[4,128,1024]{2,1,0:T(8,128)(2,1)S(1)}, bf16[4,128,1024]{2,1,0:T(8,128)(2,1)S(1)}, u32[]{:S(2)}, u32[]{:S(2)}) collective-permute-start(bf16[4,128,1024]{2,1,0:T(8,128)(2,1)S(1)} %pad_maximum_fusion.14), channel_id=1, source_target_pairs={{0,8},{4,12},{8,0},{12,4},{16,24},{20,28},{24,16},{28,20},{1,9},{5... | collective-permute-start | bytes 3145736 | tf_op jit(solution)/shard_map/ppermute | solution.py:303
  363.4 112.0 %collective-permute-start.38 = (bf16[1024,512]{0,1:T(8,128)(2,1)S(1)}, bf16[1024,512]{0,1:T(8,128)(2,1)S(1)}, u32[]{:S(2)}, u32[]{:S(2)}) collective-permute-start(bf16[1024,512]{0,1:T(8,128)(2,1)S(1)} %pad_maximum_fusion.16), channel_id=1, source_target_pairs={{0,4},{4,0},{8,12},{12,8},{16,20},{20,16},{24,28},{28,24},{1,5},{5... | collective-permute-start | bytes 3145736 | tf_op jit(solution)/shard_map/ppermute | solution.py:303
  486.3 113.2 %collective-permute-start.56 = (bf16[2,4,2,32,1536]{4,3,2,1,0:T(8,128)(2,1)}, bf16[2,4,2,32,1536]{4,3,2,1,0:T(8,128)(2,1)}, u32[]{:S(2)}, u32[]{:S(2)}) collective-permute-start(bf16[2,4,2,32,1536]{4,3,2,1,0:T(8,128)(2,1)} %pad_maximum_fusion.10), channel_id=1, source_target_pairs={{0,16},{4,20},{8,24},{12,28},{16,0},{20,4},{24,8},{28,12},{1,17},{... | collective-permute-start | bytes 4718600 | tf_op jit(solution)/shard_map/ppermute | solution.py:303
  501.5 136.6 %collective-permute-start.28 = (bf16[2,4,128,1024]{3,2,1,0:T(8,128)(2,1)}, bf16[2,4,128,1024]{3,2,1,0:T(8,128)(2,1)}, u32[]{:S(2)}, u32[]{:S(2)}) collective-permute-start(bf16[2,4,128,1024]{3,2,1,0:T(8,128)(2,1)} %pad_maximum_fusion.3), channel_id=1, source_target_pairs={{0,16},{4,20},{8,24},{12,28},{16,0},{20,4},{24,8},{28,12},{1,17},{... | collective-permute-start | bytes 6291464 | tf_op jit(solution)/shard_map/ppermute | solution.py:303
  524.0 156.5 %collective-permute-start.73 = (bf16[2,4,128,1024]{3,2,1,0:T(8,128)(2,1)}, bf16[2,4,128,1024]{3,2,1,0:T(8,128)(2,1)}, u32[]{:S(2)}, u32[]{:S(2)}) collective-permute-start(bf16[2,4,128,1024]{3,2,1,0:T(8,128)(2,1)} %pad_maximum_fusion.5), channel_id=1, source_target_pairs={{0,16},{4,20},{8,24},{12,28},{16,0},{20,4},{24,8},{28,12},{1,17},{... | collective-permute-start | bytes 6291464 | tf_op jit(solution)/shard_map/ppermute | solution.py:303
  557.7 127.0 %collective-permute-start.23 = (bf16[2,4,2,32,2048]{4,3,2,1,0:T(8,128)(2,1)}, bf16[2,4,2,32,2048]{4,3,2,1,0:T(8,128)(2,1)}, u32[]{:S(2)}, u32[]{:S(2)}) collective-permute-start(bf16[2,4,2,32,2048]{4,3,2,1,0:T(8,128)(2,1)} %pad_maximum_fusion.2), channel_id=1, source_target_pairs={{0,8},{4,12},{8,0},{12,4},{16,24},{20,28},{24,16},{28,20},{1,9},{5... | collective-permute-start | bytes 6291464 | tf_op jit(solution)/shard_map/ppermute | solution.py:303
  559.1 128.3 %collective-permute-start.68 = (bf16[2,4,2,32,2048]{4,3,2,1,0:T(8,128)(2,1)}, bf16[2,4,2,32,2048]{4,3,2,1,0:T(8,128)(2,1)}, u32[]{:S(2)}, u32[]{:S(2)}) collective-permute-start(bf16[2,4,2,32,2048]{4,3,2,1,0:T(8,128)(2,1)} %pad_maximum_fusion.4), channel_id=1, source_target_pairs={{0,8},{4,12},{8,0},{12,4},{16,24},{20,28},{24,16},{28,20},{1,9},{5... | collective-permute-start | bytes 6291464 | tf_op jit(solution)/shard_map/ppermute | solution.py:303
  599.5 92.5 %collective-permute-start.17 = (bf16[1024,1024]{0,1:T(8,128)(2,1)}, bf16[1024,1024]{0,1:T(8,128)(2,1)}, u32[]{:S(2)}, u32[]{:S(2)}) collective-permute-start(bf16[1024,1024]{0,1:T(8,128)(2,1)} %convolution_convert_fusion.16), channel_id=1, source_target_pairs={{0,4},{4,0},{8,12},{12,8},{16,20},{20,16},{24,28},{28,24},{1,5},{5... | collective-permute-start | bytes 6291464 | tf_op jit(solution)/shard_map/ppermute | solution.py:303
  896.0 126.8 %collective-permute-start.158 = (bf16[512,2048]{1,0:T(8,128)(2,1)}, bf16[512,2048]{1,0:T(8,128)(2,1)}, u32[]{:S(2)}, u32[]{:S(2)}) collective-permute-start(bf16[512,2048]{1,0:T(8,128)(2,1)} %convolution_convert_fusion), channel_id=1, source_target_pairs={{0,16},{4,20},{8,24},{12,28},{16,0},{20,4},{24,8},{28,12},{1,17},{... | collective-permute-start | bytes 6291464 | tf_op jit(solution)/shard_map/ppermute | solution.py:303
  921.8 106.1 %collective-permute-start.164 = (bf16[1024,1024]{1,0:T(8,128)(2,1)}, bf16[1024,1024]{1,0:T(8,128)(2,1)}, u32[]{:S(2)}, u32[]{:S(2)}) collective-permute-start(bf16[1024,1024]{1,0:T(8,128)(2,1)} %convolution_convert_fusion.4), channel_id=1, source_target_pairs={{0,8},{4,12},{8,0},{12,4},{16,24},{20,28},{24,16},{28,20},{1,9},{5... | collective-permute-start | bytes 6291464 | tf_op jit(solution)/shard_map/ppermute | solution.py:303
  990.2 160.3 %collective-permute-start.97 = (bf16[1024,1024]{0,1:T(8,128)(2,1)}, bf16[1024,1024]{0,1:T(8,128)(2,1)}, u32[]{:S(2)}, u32[]{:S(2)}) collective-permute-start(bf16[1024,1024]{0,1:T(8,128)(2,1)} %convolution_convert_fusion.7), channel_id=1, source_target_pairs={{0,4},{4,0},{8,12},{12,8},{16,20},{20,16},{24,28},{28,24},{1,5},{5... | collective-permute-start | bytes 6291464 | tf_op jit(solution)/shard_map/ppermute | solution.py:303
  1119.8 87.2 %collective-permute-start.90 = (bf16[1024,1024]{0,1:T(8,128)(2,1)}, bf16[1024,1024]{0,1:T(8,128)(2,1)}, u32[]{:S(2)}, u32[]{:S(2)}) collective-permute-start(bf16[1024,1024]{0,1:T(8,128)(2,1)} %convolution_convert_fusion.10), channel_id=1, source_target_pairs={{0,4},{4,0},{8,12},{12,8},{16,20},{20,16},{24,28},{28,24},{1,5},{5... | collective-permute-start | bytes 6291464 | tf_op jit(solution)/shard_map/ppermute | solution.py:303
  1206.6 96.8 %collective-permute-start.98 = (bf16[1024,1024]{0,1:T(8,128)(2,1)}, bf16[1024,1024]{0,1:T(8,128)(2,1)}, u32[]{:S(2)}, u32[]{:S(2)}) collective-permute-start(bf16[1024,1024]{0,1:T(8,128)(2,1)} %convolution_convert_fusion.6), channel_id=1, source_target_pairs={{0,4},{4,0},{8,12},{12,8},{16,20},{20,16},{24,28},{28,24},{1,5},{5... | collective-permute-start | bytes 6291464 | tf_op jit(solution)/shard_map/ppermute | solution.py:303
  1287.6 125.9 %collective-permute-start.76 = (bf16[256,512]{1,0:T(8,128)(2,1)}, bf16[256,512]{1,0:T(8,128)(2,1)}, u32[]{:S(2)}, u32[]{:S(2)}) collective-permute-start(bf16[256,512]{1,0:T(8,128)(2,1)} %bitcast.932), channel_id=1, source_target_pairs={{0,2},{1,0},{2,6},{3,4},{4,3},{5,1},{6,7},{7,5},{8,10},{9,8},{10,1... | collective-permute-start | bytes 786440 | tf_op jit(solution)/shard_map/ppermute | solution.py:339
  1287.6 126.0 %collective-permute-start.75 = (bf16[256,512]{1,0:T(8,128)(2,1)}, bf16[256,512]{1,0:T(8,128)(2,1)}, u32[]{:S(2)}, u32[]{:S(2)}) collective-permute-start(bf16[256,512]{1,0:T(8,128)(2,1)} %bitcast.931), channel_id=1, source_target_pairs={{0,3},{1,1},{2,7},{3,5},{4,2},{5,0},{6,6},{7,4},{8,11},{9,9},{10,1... | collective-permute-start | bytes 786440 | tf_op jit(solution)/shard_map/ppermute | solution.py:339
  1291.8 123.8 %collective-permute-start.78 = (bf16[256,512]{1,0:T(8,128)(2,1)}, bf16[256,512]{1,0:T(8,128)(2,1)}, u32[]{:S(2)}, u32[]{:S(2)}) collective-permute-start(bf16[256,512]{1,0:T(8,128)(2,1)} %bitcast.930), channel_id=1, source_target_pairs={{0,0},{1,2},{2,4},{3,6},{4,1},{5,3},{6,5},{7,7},{8,8},{9,10},{10,1... | collective-permute-start | bytes 786440 | tf_op jit(solution)/shard_map/ppermute | solution.py:339
  1303.3 87.6 %collective-permute-start.119 = (bf16[512,2048]{1,0:T(8,128)(2,1)}, bf16[512,2048]{1,0:T(8,128)(2,1)}, u32[]{:S(2)}, u32[]{:S(2)}) collective-permute-start(bf16[512,2048]{1,0:T(8,128)(2,1)} %convolution_convert_fusion.1), channel_id=1, source_target_pairs={{0,16},{4,20},{8,24},{12,28},{16,0},{20,4},{24,8},{28,12},{1,17},{... | collective-permute-start | bytes 6291464 | tf_op jit(solution)/shard_map/ppermute | solution.py:303
  (415 other events, 11564.2 us)
Sparse Core Ops, SparseCore 0:
  17.4 126.6 all-reduce.3

commit v2 on v1

--- a/solution.py
+++ b/solution.py
@@ -281,6 +281,19 @@
     )(info, queries, keys, values, mixed, grad, lse, qseg_row, kseg_column)
 
 
+MESH = pl.DeviceIdType.MESH
+
+
+def own_columns(array, core, runs=8):
+    split = array.reshape(array.shape[:-1] + (runs // 2, 2, array.shape[-1] // runs))
+    mine = lax.dynamic_index_in_dim(split, core, split.ndim - 2, keepdims=False)
+    return mine.reshape(array.shape[:-1] + (array.shape[-1] // 2,))
+
+
+def lay_side(array):
+    return jnp.concatenate([array[i] for i in range(array.shape[0])], axis=1)
+
+
 def xor_arrange(pieces, place):
     pieces, bit = list(pieces), 0
     while 1 << bit < len(pieces):
@@ -290,139 +303,447 @@
     return pieces
 
 
+class Here:
+    def __init__(self):
+        self.at = lax.axis_index("dp")
+        self.z = lax.axis_index("seq")
+        self.c = self.at % 2
+        self.x = (self.at // 2) % 2
+        self.y = self.at // 4
+        self.core_peer = (self.at + 1 - 2 * self.c, self.z)
+        self.x_peer = (self.at + 2 - 4 * self.x, self.z)
+        self.y_peer = (self.at + 4 - 8 * self.y, self.z)
+
+    def z_flip(self, j):
+        return (self.z // 2 + j // 2) % 2 * 2 + (self.z % 2 + j % 2) % 2
+
+    def z_peer(self, j):
+        return (self.at, self.z_flip(j))
+
+    def enter(self):
+        barrier = pltpu.get_barrier_semaphore()
+        peers = [self.x_peer, self.y_peer, self.core_peer]
+        other = self.at + 1 - 2 * self.c
+        for j in range(1, 4):
+            peers += [(self.at, self.z_flip(j)), (other, self.z_flip(j))]
+        for peer in peers:
+            pl.semaphore_signal(barrier, inc=1, device_id=peer, device_id_type=MESH)
+        pl.semaphore_wait(barrier, len(peers))
+
+
+def remote(source, target, send_sem, recv_sem, peer):
+    return pltpu.make_async_remote_copy(
+        src_ref=source,
+        dst_ref=target,
+        send_sem=send_sem,
+        recv_sem=recv_sem,
+        device_id=peer,
+        device_id_type=MESH,
+    )
+
+
+class GatherItem:
+    def __init__(self, here, mine, other, out, send, recv, local):
+        self.here, self.mine, self.other, self.out = here, mine, other, out
+        self.send, self.recv, self.local = send, recv, local
+        self.half = out.shape[-1] // 2
+        self.core = here.c if other is not None else 0
+        self.copies = {}
+
+    def go(self, slot, region, peer):
+        self.copies[slot] = remote(region, region, self.send.at[slot], self.recv.at[slot], peer)
+        self.copies[slot].start()
+
+    def begin(self):
+        here = self.here
+        block = self.out.at[here.y, here.x, self.core, here.z]
+        self.own = pltpu.make_async_copy(self.mine, block, self.local)
+        self.own.start()
+        if self.other is not None:
+            self.copies[0] = remote(self.other, block, self.send.at[0], self.recv.at[0], here.core_peer)
+            self.copies[0].start()
+
+    def stage_z(self):
+        here = self.here
+        self.own.wait()
+        if self.other is not None:
+            self.copies[0].wait_recv()
+        for j in range(1, 4):
+            self.go(j, self.out.at[here.y, here.x, :, here.z], here.z_peer(j))
+
+    def stage_one(self):
+        here, h = self.here, self.half
+        for j in range(1, 4):
+            self.copies[j].wait_recv()
+        self.go(4, self.out.at[here.y, here.x, :, :, :, pl.ds(0, h)], here.x_peer)
+        self.go(5, self.out.at[here.y, here.x, :, :, :, pl.ds(h, h)], here.y_peer)
+
+    def stage_two(self):
+        here, h = self.here, self.half
+        self.copies[4].wait_recv()
+        self.go(6, self.out.at[here.y, :, :, :, :, pl.ds(0, h)], here.y_peer)
+        self.copies[5].wait_recv()
+        self.go(7, self.out.at[:, here.x, :, :, :, pl.ds(h, h)], here.x_peer)
+
+    def finish(self):
+        self.copies[6].wait_recv()
+        self.copies[7].wait_recv()
+        for copy in self.copies.values():
+            copy.wait_send()
+
+
+class RowIn:
+    def __init__(self, here, source, out, send, recv, local):
+        self.here, self.source, self.out = here, source, out
+        self.send, self.recv, self.local = send, recv, local
+        self.half = source.shape[-1] // 2
+
+    def lanes(self, f):
+        return pl.ds(f * self.half, self.half) if isinstance(f, int) else pl.ds(pl.multiple_of(f * self.half, 128), self.half)
+
+    def parts(self):
+        here = self.here
+        for i in range(2):
+            for f in range(2):
+                source = self.source.at[i, :, self.lanes(f)]
+                target = self.out.at[here.z, :, self.lanes(f)]
+                self_sent = (2 * here.c + i == here.z) & (here.c == f)
+                peer = (here.at - here.c + f, 2 * here.c + i)
+                away = remote(source, target, self.send.at[2 * i + f], self.recv.at[here.z], peer)
+                stay = pltpu.make_async_copy(source, target, self.local)
+                yield self_sent, away, stay
+
+    def begin(self):
+        for self_sent, away, stay in self.parts():
+            pl.when(self_sent)(stay.start)
+            pl.when(jnp.logical_not(self_sent))(away.start)
+
+    def across(self):
+        here = self.here
+        lanes = self.lanes(here.c)
+        for k in range(4):
+            target = self.out.at[k, :, lanes]
+            from_self = (here.z == k) & (here.z // 2 == here.c)
+            stay = pltpu.make_async_copy(target, target, self.local)
+            away = remote(target, target, self.send.at[0], self.recv.at[k], here.core_peer)
+            pl.when(from_self)(stay.wait)
+            pl.when(jnp.logical_not(from_self))(away.wait_recv)
+        region = self.out.at[:, :, lanes]
+        self.copy = remote(region, region, self.send.at[4], self.recv.at[4], here.core_peer)
+        self.copy.start()
+
+    def finish(self):
+        self.copy.wait()
+        for self_sent, away, _ in self.parts():
+            pl.when(jnp.logical_not(self_sent))(away.wait_send)
+
+
+def gather_kernel(kinds, rows_at, refs):
+    here = Here()
+    refs = list(refs)
+    take = lambda n: [refs.pop(0) for _ in range(n)]
+    count = len(kinds)
+    ins = [take(2) if columns else take(1) + [None] for columns in kinds]
+    row_ins = take(len(rows_at))
+    outs = take(count)
+    row_outs = take(len(rows_at))
+    send, recv, local, row_send, row_recv, row_local = refs
+    items = [
+        GatherItem(here, mine, other, outs[k], send.at[k], recv.at[k], local.at[k])
+        for k, (mine, other) in enumerate(ins)
+    ]
+    rows = [
+        RowIn(here, row_ins[t], row_outs[t], row_send.at[t], row_recv.at[t], row_local.at[t])
+        for t in range(len(rows_at))
+    ]
+    here.enter()
+    for item in items:
+        item.begin()
+    for step in range(count + 3):
+        for t, start in enumerate(rows_at):
+            if start == step:
+                rows[t].begin()
+            if start + 1 == step:
+                rows[t].across()
+        if step < count:
+            items[step].stage_z()
+        if 0 <= step - 1 < count:
+            items[step - 1].stage_one()
+        if 0 <= step - 2 < count:
+            items[step - 2].stage_two()
+        if 0 <= step - 3 < count:
+            items[step - 3].finish()
+    for row in rows:
+        row.finish()
+
+
+def gather_all(locals_, rows, rows_at):
+    kinds = [other is not None for _, other in locals_]
+    inputs = [v for pair in locals_ for v in pair if v is not None] + list(rows)
+    shapes = [
+        jax.ShapeDtypeStruct((2, 2, 2 if other is not None else 1, 4) + mine.shape, mine.dtype)
+        for mine, other in locals_
+    ] + [jax.ShapeDtypeStruct((4,) + row.shape[1:], row.dtype) for row in rows]
+    count, tensors = len(kinds), len(rows)
+    hbm = pl.BlockSpec(memory_space=pl.ANY)
+
+    def kernel(*refs):
+        gather_kernel(kinds, rows_at, refs)
+
+    dma = pltpu.SemaphoreType.DMA
+    return pl.pallas_call(
+        kernel,
+        in_specs=[hbm] * len(inputs),
+        out_specs=[hbm] * len(shapes),
+        out_shape=shapes,
+        scratch_shapes=[
+            dma((count, 8)),
+            dma((count, 8)),
+            dma((count,)),
+            dma((tensors, 5)),
+            dma((tensors, 5)),
+            dma((tensors,)),
+        ],
+        compiler_params=pltpu.CompilerParams(collective_id=0, has_side_effects=True),
+        name="gather_all",
+    )(*inputs)
+
+
+class SumItem:
+    def __init__(self, here, source, out, scratch, send, recv, local):
+        self.here, self.source, self.out = here, source, out
+        self.own, self.b1, self.b2, self.b3 = scratch[:4]
+        self.columns = source.shape[2] == 2
+        if self.columns:
+            self.b4, self.b4s = scratch[4:]
+        self.send, self.recv, self.local = send, recv, local
+        self.half = source.shape[-1] // 2
+        self.sides = ((pl.ds(0, self.half)), (pl.ds(self.half, self.half)))
+        self.copies = {}
+
+    def go(self, slot, source, target, peer):
+        self.copies[slot] = remote(source, target, self.send.at[slot], self.recv.at[slot], peer)
+        self.copies[slot].start()
+
+    def blocks(self, body):
+        cores = self.b2.shape[0]
+
+        def step(k, carry):
+            body(k // 4, k % 4)
+            return carry
+
+        lax.fori_loop(0, cores * 4, step, 0)
+
+    def stage_one(self):
+        here, (a, b), source = self.here, self.sides, self.source
+        self.go(0, source.at[:, 1 - here.x, :, :, :, a], self.b1.at[:, :, :, :, a], here.x_peer)
+        self.go(1, source.at[1 - here.y, :, :, :, :, b], self.b1.at[:, :, :, :, b], here.y_peer)
+        self.loads = [
+            pltpu.make_async_copy(source.at[:, here.x, :, :, :, a], self.own.at[:, :, :, :, a], self.local.at[0]),
+            pltpu.make_async_copy(source.at[here.y, :, :, :, :, b], self.own.at[:, :, :, :, b], self.local.at[1]),
+        ]
+        for load in self.loads:
+            load.start()
+
+    def stage_two(self):
+        here = self.here
+        for side, near, peer in ((0, here.y, here.y_peer), (1, here.x, here.x_peer)):
+            lanes = self.sides[side]
+            away = 1 - near
+            self.loads[side].wait()
+            self.copies[side].wait_recv()
+
+            def add(c, z, away=away, lanes=lanes):
+                total = self.own[away, c, z, :, lanes].astype(F32) + self.b1[away, c, z, :, lanes].astype(F32)
+                self.own[away, c, z, :, lanes] = total.astype(self.own.dtype)
+
+            self.blocks(add)
+            self.go(2 + side, self.own.at[away, :, :, :, lanes], self.b2.at[:, :, :, lanes], peer)
+
+    def stage_three(self):
+        here = self.here
+        for side, near in ((0, here.y), (1, here.x)):
+            lanes = self.sides[side]
+            self.copies[2 + side].wait_recv()
+
+            def add(c, z, near=near, lanes=lanes):
+                total = self.own[near, c, z, :, lanes].astype(F32) + self.b1[near, c, z, :, lanes].astype(F32)
+                total = total + self.b2[c, z, :, lanes].astype(F32)
+                self.b2[c, z, :, lanes] = total.astype(self.b2.dtype)
+
+            self.blocks(add)
+        for j in range(1, 4):
+            self.go(3 + j, self.b2.at[:, here.z_flip(j)], self.b3.at[j - 1], here.z_peer(j))
+
+    def total(self, c):
+        total = self.b2[c, self.here.z].astype(F32)
+        for j in range(3):
+            total = total + self.b3[j, c].astype(F32)
+        return total
+
+    def stage_four(self):
+        here = self.here
+        for j in range(1, 4):
+            self.copies[3 + j].wait_recv()
+        if self.columns:
+            self.b4s[...] = self.total(1 - here.c).astype(self.b4s.dtype)
+            self.go(7, self.b4s, self.b4, here.core_peer)
+            self.out[here.c] = self.total(here.c)
+        else:
+            self.out[...] = self.total(0)
+
+    def finish(self):
+        if self.columns:
+            self.copies[7].wait_recv()
+            self.out[1 - self.here.c] = self.b4[...].astype(F32)
+        for copy in self.copies.values():
+            copy.wait_send()
+
+
+class RowOut:
+    def __init__(self, here, source, out, send, recv, local):
+        self.here, self.source, self.out = here, source, out
+        self.send, self.recv, self.local = send, recv, local
+        self.half = source.shape[-1] // 2
+
+    def parts(self):
+        here = self.here
+        lanes = pl.ds(pl.multiple_of(here.c * self.half, 128), self.half)
+        for k in range(4):
+            source = self.source.at[k, :, lanes]
+            target = self.out.at[here.z % 2, :, lanes]
+            self_sent = (here.z == k) & (here.z // 2 == here.c)
+            peer = (here.at - here.c + here.z // 2, k)
+            away = remote(source, target, self.send.at[k], self.recv.at[here.z % 2 * 2 + here.c], peer)
+            yield self_sent, away, pltpu.make_async_copy(source, target, self.local)
+
+    def begin(self):
+        for self_sent, away, stay in self.parts():
+            pl.when(self_sent)(stay.start)
+            pl.when(jnp.logical_not(self_sent))(away.start)
+
+    def finish(self):
+        here = self.here
+        for i in range(2):
+            for f in range(2):
+                target = self.out.at[i, :, pl.ds(f * self.half, self.half)]
+                from_self = (2 * here.c + i == here.z) & (here.c == f)
+                away = remote(target, target, self.send.at[0], self.recv.at[2 * i + f], here.core_peer)
+                stay = pltpu.make_async_copy(target, target, self.local)
+                pl.when(from_self)(stay.wait)
+                pl.when(jnp.logical_not(from_self))(away.wait_recv)
+        for self_sent, away, _ in self.parts():
+            pl.when(jnp.logical_not(self_sent))(away.wait_send)
+
+
+def sum_kernel(column_flags, tensors, refs):
+    here = Here()
+    refs = list(refs)
+    take = lambda n: [refs.pop(0) for _ in range(n)]
+    count = len(column_flags)
+    sources, row_sources = take(count), take(tensors)
+    outs, row_outs = take(count), take(tensors)
+    scratch = [take(6 if columns else 4) for columns in column_flags]
+    send, recv, local, row_send, row_recv, row_local = refs
+    items = [
+        SumItem(here, sources[k], outs[k], scratch[k], send.at[k], recv.at[k], local.at[k]) for k in range(count)
+    ]
+    rows = [
+        RowOut(here, row_sources[t], row_outs[t], row_send.at[t], row_recv.at[t], row_local.at[t])
+        for t in range(tensors)
+    ]
+    here.enter()
+    for step in range(count + 4):
+        if step < count:
+            items[step].stage_one()
+        if 0 <= step - 1 < count:
+            items[step - 1].stage_two()
+        if 0 <= step - 2 < count:
+            items[step - 2].stage_three()
+        if 0 <= step - 3 < count:
+            items[step - 3].stage_four()
+        if 0 <= step - 4 < count:
+            items[step - 4].finish()
+        if step < 2 * tensors and step % 2 == 0:
+            rows[step // 2].begin()
+    for row in rows:
+        row.finish()
+
+
+def sum_all(grads, rows):
+    flags = [grad.shape[2] == 2 for grad in grads]
+    hbm = pl.BlockSpec(memory_space=pl.ANY)
+    vmem = pl.BlockSpec(memory_space=pltpu.VMEM)
+    shapes, scratch = [], []
+    for grad, columns in zip(grads, flags):
+        _, _, cores, places, r, n = grad.shape
+        shapes.append(jax.ShapeDtypeStruct((2, r, n) if columns else (r, n), F32))
+        sizes = [(2, cores, places, r, n)] * 2 + [(cores, places, r, n), (3, cores, r, n)]
+        sizes += [(r, n)] * 2 if columns else []
+        scratch += [pltpu.VMEM(size, grad.dtype) for size in sizes]
+    count, tensors = len(grads), len(rows)
+    row_shapes = [jax.ShapeDtypeStruct((2,) + row.shape[1:], row.dtype) for row in rows]
+
+    def kernel(*refs):
+        sum_kernel(flags, tensors, refs)
+
+    dma = pltpu.SemaphoreType.DMA
+    return pl.pallas_call(
+        kernel,
+        in_specs=[hbm] * (count + tensors),
+        out_specs=[vmem] * count + [hbm] * tensors,
+        out_shape=shapes + row_shapes,
+        scratch_shapes=scratch
+        + [
+            dma((count, 8)),
+            dma((count, 8)),
+            dma((count, 2)),
+            dma((tensors, 4)),
+            dma((tensors, 4)),
+            dma((tensors,)),
+        ],
+        compiler_params=pltpu.CompilerParams(
+            collective_id=1, has_side_effects=True, vmem_limit_bytes=60 * 2**20
+        ),
+        name="sum_all",
+    )(*grads, *rows)
+
+
 class Place:
     def __init__(self, dp, seq):
         self.dp, self.seq = dp, seq
         self.at = lax.axis_index("dp")
         self.z = lax.axis_index("seq")
         self.core = self.at % 2
-        self.x = (self.at // 2) % 2
-        self.y = self.at // 4
-
-    def over_dp(self, value, mask):
-        return lax.ppermute(value, "dp", [(i, i ^ mask) for i in range(self.dp)])
-
-    def over_seq(self, value, mask):
-        return lax.ppermute(value, "seq", [(i, i ^ mask) for i in range(self.seq)])
 
     def over_core(self, value):
-        return self.over_dp(value, 1)
-
-    def row_in(self, array):
-        parts = array.reshape(2, array.shape[1], 2, -1)
-        got = []
-        for m in range(4):
-            code = self.z ^ m
-            piece = lax.dynamic_index_in_dim(parts, code // 2, 0, keepdims=False)
-            piece = lax.dynamic_index_in_dim(piece, code % 2, 1, keepdims=False)
-            moves = []
-            for d in range(self.dp):
-                for z in range(4):
-                    q = m ^ z
-                    moves.append((d * 4 + z, (d - d % 2 + q % 2) * 4 + 2 * (d % 2) + q // 2))
-            got.append(lax.ppermute(piece, ("dp", "seq"), moves))
-        half = jnp.concatenate(xor_arrange(got, (self.z % 2) * 2 + self.core), axis=0)
-        return jnp.concatenate(xor_arrange([half, self.over_core(half)], self.core), axis=1)
-
-    def row_out(self, row):
-        parts = row.reshape(4, -1, 2, row.shape[1] // 2)
-        mine = lax.dynamic_index_in_dim(parts, self.core, 2, keepdims=False)
-        q_here = (self.z % 2) * 2 + self.core
-        got = []
-        for m in range(4):
-            piece = lax.dynamic_index_in_dim(mine, q_here ^ m, 0, keepdims=False)
-            moves = []
-            for d in range(self.dp):
-                for z in range(4):
-                    q = (z % 2) * 2 + d % 2
-                    moves.append((d * 4 + z, (d - d % 2 + z // 2) * 4 + (m ^ q)))
-            got.append(lax.ppermute(piece, ("dp", "seq"), moves))
-        placed = xor_arrange(got, self.z)
-        return jnp.stack([jnp.concatenate(placed[2 * i : 2 * i + 2], axis=1) for i in range(2)])
+        return lax.ppermute(value, "dp", [(i, i ^ 1) for i in range(self.dp)])
 
     def both_cores(self, part):
         part = part.astype(B16)
         return part.astype(F32) + self.over_core(part).astype(F32)
 
 
-def own_columns(array, core, runs=8):
-    split = array.reshape(array.shape[:-1] + (runs // 2, 2, array.shape[-1] // runs))
-    mine = lax.dynamic_index_in_dim(split, core, split.ndim - 2, keepdims=False)
-    return mine.reshape(array.shape[:-1] + (array.shape[-1] // 2,))
-
-
-def lay_side(array):
-    return jnp.concatenate([array[i] for i in range(array.shape[0])], axis=1)
-
-
 class Tree:
     def __init__(self, place):
         self.place = place
 
-    def gather(self, local, x_first):
-        place = self.place
-        pieces = [local] + [place.over_seq(local, j) for j in range(1, 4)]
-        held = jnp.stack(xor_arrange(pieces, place.z))
-        if x_first:
-            held = jnp.stack(xor_arrange([held, place.over_dp(held, 2)], place.x))
-            return jnp.stack(xor_arrange([held, place.over_dp(held, 4)], place.y))
-        held = jnp.stack(xor_arrange([held, place.over_dp(held, 4)], place.y))
-        return jnp.stack(xor_arrange([held, place.over_dp(held, 2)], place.x), axis=1)
-
-    def by_columns(self, local, x_first):
+    def gather(self, flat, columns, rows, tensors, tensors_at):
         core = self.place.core
-        mine = lay_side(own_columns(local, core))
-        other = lay_side(own_columns(local, 1 - core))
-        both = jnp.stack(xor_arrange([mine, self.place.over_core(other)], core))
-        full = self.gather(both, x_first)
-        return full.transpose(0, 1, 3, 2, 4, 5).reshape(-1, full.shape[-1])
-
-    def by_rows(self, local, x_first):
-        return self.gather(local, x_first).reshape(-1, local.shape[-1])
-
-    def sum_chips(self, features, grad, x_first):
-        place = self.place
-        count, size = features.shape
-        quarter = size // 4
-        split = features.reshape(count, 2, 2, quarter)
-        axis, here, mask = (2, place.x, 2) if x_first else (1, place.y, 4)
-        here_two, mask_two = (place.y, 4) if x_first else (place.x, 2)
-
-        def part(index):
-            cut = lax.dynamic_index_in_dim(split, index, axis, keepdims=False)
-            return product_tn(cut.reshape(count, size // 2), grad)
-
-        sent = place.over_dp(part(1 - here).astype(B16), mask)
-        kept = (part(here) + sent.astype(F32)).astype(B16).reshape(2, quarter, grad.shape[1])
-        away = lax.dynamic_index_in_dim(kept, 1 - here_two, 0, keepdims=False)
-        stay = lax.dynamic_index_in_dim(kept, here_two, 0, keepdims=False)
-        return (stay.astype(F32) + place.over_dp(away, mask_two).astype(F32)).astype(B16)
-
-    def sum_z(self, value, axis):
-        place = self.place
-        total = lax.dynamic_index_in_dim(value, place.z, axis, keepdims=False).astype(F32)
-        for j in range(1, 4):
-            piece = lax.dynamic_index_in_dim(value, place.z ^ j, axis, keepdims=False)
-            total = total + place.over_seq(piece, j).astype(F32)
-        return total
-
-    def grad_by_columns(self, features, grad, x_first, parts):
-        place = self.place
-        value = self.sum_chips(features, grad, x_first)
-        rows = value.shape[0] // 8
-        total = self.sum_z(value.reshape(2, 4, rows, value.shape[1]), 1)
-        mine = lax.dynamic_index_in_dim(total, place.core, 0, keepdims=False)
-        other = lax.dynamic_index_in_dim(total, 1 - place.core, 0, keepdims=False).astype(B16)
-        got = place.over_core(other).astype(F32)
-        both = [v.reshape(rows, parts, 4, -1) for v in xor_arrange([mine, got], place.core)]
-        return jnp.stack(both, axis=3).reshape(rows, parts, -1).transpose(1, 0, 2)
-
-    def grad_by_rows(self, features, grad, x_first):
-        value = self.sum_chips(features, grad, x_first)
-        return self.sum_z(value.reshape(4, -1, value.shape[1]), 0)
-
-    def small(self, table, hidden):
-        place = self.place
+        padded = jnp.pad(flat, (0, -flat.shape[0] % 4096)).reshape(16, -1)
+        locals_ = {-1: (padded, padded)}
+        for key, value in columns.items():
+            locals_[key] = (lay_side(own_columns(value, core)), lay_side(own_columns(value, 1 - core)))
+        for key, value in rows.items():
+            locals_[key] = (value, None)
+        keys = sorted(locals_)
+        outs = gather_all([locals_[key] for key in keys], tensors, tensors_at)
+        whole = {key: out for key, out in zip(keys, outs)}
+        small = whole.pop(-1).reshape(32, -1)[:, : flat.shape[0]]
+        weights = {key: value.reshape(-1, value.shape[-1]) for key, value in whole.items()}
+        return small, weights, [out.reshape(-1, out.shape[-1]) for out in outs[len(keys) :]]
+
+    def sums(self, columns, rows, table, hidden, tensors):
         n, m = table.shape[0], hidden.shape[0]
         both = jnp.concatenate(
             [
@@ -431,12 +752,30 @@
             ],
             axis=-1,
         )
-        for here, mask in ((place.y, 4), (place.x, 2)):
-            away = lax.dynamic_index_in_dim(both, 1 - here, 0, keepdims=False)
-            both = lax.dynamic_index_in_dim(both, here, 0, keepdims=False) + place.over_dp(away, mask)
-        flat = self.sum_z(both, 0)
+        size = both.shape[-1]
+        both = jnp.pad(both, ((0, 0), (0, 0), (0, 0), (0, -size % 2048))).reshape(2, 2, 1, 4, 8, -1)
+        grads, keys = [], []
+        for key, (features, grad, _) in columns.items():
+            value = product_tn(features, grad).astype(B16)
+            grads.append(value.reshape(2, 2, 2, 4, value.shape[0] // 32, value.shape[1]))
+            keys.append(key)
+        for key, (features, grad) in rows.items():
+            value = product_tn(features, grad).astype(B16)
+            grads.append(value.reshape(2, 2, 1, 4, value.shape[0] // 16, value.shape[1]))
+            keys.append(key)
+        order = sorted(range(len(keys)), key=lambda k: keys[k])
+        outs = sum_all([grads[k] for k in order] + [both], [t.reshape(4, -1, t.shape[-1]) for t in tensors])
+        result = {}
+        for k, out in zip(order, outs):
+            key = keys[k]
+            if key in columns:
+                parts, r = columns[key][2], out.shape[1]
+                result[key] = out.reshape(2, r, parts, 4, -1).transpose(2, 1, 3, 0, 4).reshape(parts, r, -1)
+            else:
+                result[key] = out
+        flat = outs[len(keys)].reshape(-1)[:size]
         edge = table.shape[1] // 16 * n
-        return flat[:edge].reshape(n, -1), flat[edge:].reshape(m, -1)
+        return result, flat[:edge].reshape(n, -1), flat[edge:].reshape(m, -1), outs[len(keys) + 1 :]
 
 
 class Plain:
@@ -444,14 +783,52 @@
         self.place = place
         self.axes = ("dp", "seq")
 
-    def by_columns(self, local, x_first):
-        full = lax.all_gather(local, self.axes, axis=1, tiled=True)
-        return lay_side(own_columns(full, self.place.core))
-
-    def by_rows(self, local, x_first):
-        full = lax.all_gather(local, self.axes, axis=0, tiled=True)
-        split = full.reshape(4, 2, full.shape[0] // 8, full.shape[1])
-        return lax.dynamic_index_in_dim(split, self.place.core, 1, keepdims=False).reshape(-1, full.shape[1])
+    def row_in(self, array):
+        place = self.place
+        parts = array.reshape(2, array.shape[1], 2, -1)
+        got = []
+        for m in range(4):
+            code = place.z ^ m
+            piece = lax.dynamic_index_in_dim(parts, code // 2, 0, keepdims=False)
+            piece = lax.dynamic_index_in_dim(piece, code % 2, 1, keepdims=False)
+            moves = []
+            for d in range(place.dp):
+                for z in range(4):
+                    q = m ^ z
+                    moves.append((d * 4 + z, (d - d % 2 + q % 2) * 4 + 2 * (d % 2) + q // 2))
+            got.append(lax.ppermute(piece, self.axes, moves))
+        half = jnp.concatenate(xor_arrange(got, (place.z % 2) * 2 + place.core), axis=0)
+        return jnp.concatenate(xor_arrange([half, place.over_core(half)], place.core), axis=1)
+
+    def row_out(self, row):
+        place = self.place
+        parts = row.reshape(4, -1, 2, row.shape[1] // 2)
+        mine = lax.dynamic_index_in_dim(parts, place.core, 2, keepdims=False)
+        q_here = (place.z % 2) * 2 + place.core
+        got = []
+        for m in range(4):
+            piece = lax.dynamic_index_in_dim(mine, q_here ^ m, 0, keepdims=False)
+            moves = []
+            for d in range(place.dp):
+                for z in range(4):
+                    q = (z % 2) * 2 + d % 2
+                    moves.append((d * 4 + z, (d - d % 2 + z // 2) * 4 + (m ^ q)))
+            got.append(lax.ppermute(piece, self.axes, moves))
+        placed = xor_arrange(got, place.z)
+        return jnp.stack([jnp.concatenate(placed[2 * i : 2 * i + 2], axis=1) for i in range(2)])
+
+    def gather(self, flat, columns, rows, tensors, tensors_at):
+        small = lax.all_gather(flat, self.axes, axis=0, tiled=False)
+        weights = {}
+        for key, value in columns.items():
+            full = lax.all_gather(value, self.axes, axis=1, tiled=True)
+            weights[key] = lay_side(own_columns(full, self.place.core))
+        for key, value in rows.items():
+            full = lax.all_gather(value, self.axes, axis=0, tiled=True)
+            split = full.reshape(4, 2, full.shape[0] // 8, full.shape[1])
+            mine = lax.dynamic_index_in_dim(split, self.place.core, 1, keepdims=False)
+            weights[key] = mine.reshape(-1, full.shape[1])
+        return small, weights, [self.row_in(tensor) for tensor in tensors]
 
     def spread(self, half, axis):
         shape = half.shape[:axis] + (4, 1, half.shape[axis] // 4) + half.shape[axis + 1 :]
@@ -462,21 +839,19 @@
         both = jnp.concatenate([first, second], axis=axis + 1)
         return both.reshape(shape[:axis] + (-1,) + shape[axis + 3 :])
 
-    def grad_by_columns(self, features, grad, x_first, parts):
-        full = product_tn(features, grad)
-        full = full.reshape(full.shape[0], parts, -1).transpose(1, 0, 2).astype(B16)
-        full = self.spread(full, 2)
-        return lax.psum_scatter(full, self.axes, scatter_dimension=1, tiled=True).astype(F32)
-
-    def grad_by_rows(self, features, grad, x_first):
-        full = self.spread(product_tn(features, grad).astype(B16), 0)
-        return lax.psum_scatter(full, self.axes, scatter_dimension=0, tiled=True).astype(F32)
-
-    def small(self, table, hidden):
-        return tuple(
-            lax.psum_scatter(self.spread(v, 1), self.axes, scatter_dimension=1, tiled=True)
-            for v in (table, hidden)
-        )
+    def scatter(self, value, axis):
+        return lax.psum_scatter(value, self.axes, scatter_dimension=axis, tiled=True).astype(F32)
+
+    def sums(self, columns, rows, table, hidden, tensors):
+        result = {}
+        for key, (features, grad, parts) in columns.items():
+            full = product_tn(features, grad)
+            full = full.reshape(full.shape[0], parts, -1).transpose(1, 0, 2).astype(B16)
+            result[key] = self.scatter(self.spread(full, 2), 1)
+        for key, (features, grad) in rows.items():
+            result[key] = self.scatter(self.spread(product_tn(features, grad).astype(B16), 0), 0)
+        small = [self.scatter(self.spread(v, 1), 1) for v in (table, hidden)]
+        return result, small[0], small[1], [self.row_out(tensor) for tensor in tensors]
 
 
 def on_device(
@@ -514,8 +889,18 @@
     n_small = langs + gains.shape[0] + biases.shape[0]
     table = jnp.concatenate([lang_table, gains, biases], axis=0)
     flat = jnp.concatenate([table.reshape(-1), ff_biases.reshape(-1)])
-    everything = lax.all_gather(flat, ("dp", "seq"), axis=0, tiled=False)
     edge = table.size
+    everything, weights, tensors = moves.gather(
+        flat,
+        {0: enc_proj, 2: enc_in[None], 4: dec_proj[0:3], 6: dec_proj[3:6], 8: dec_in[None]},
+        {1: enc_oproj, 3: enc_out, 5: dec_oproj[0], 7: dec_oproj[1], 9: dec_out},
+        [src_x, tgt_x, tgt_cot, src_cot],
+        [0, 3, 5, 7],
+    )
+    source, target, target_cot, source_cot = tensors
+    enc_qkv_w, enc_o_w, enc_in_w, enc_out_w, dec_qkv_w, dec_o_w, cross_w, cross_o_w, dec_in_w, dec_out_w = (
+        weights[k] for k in range(10)
+    )
     table = everything[:, :edge].reshape(dp * seq, n_small, -1).transpose(1, 0, 2).reshape(n_small, width)
     ffb = everything[:, edge:].reshape(dp * seq, 2, -1).transpose(1, 0, 2).reshape(2, -1)
     languages = table[:langs]
@@ -540,22 +925,6 @@
     enc_masks = (block_info(False, s_seg, s_seg, t_len), s_seg[None, :], s_seg[:, None])
     dec_masks = (block_info(True, t_seg, t_seg, t_len), t_seg[None, :], t_seg[:, None])
     cross_masks = (block_info(False, t_seg, s_seg, t_len), t_seg[None, :], s_seg[:, None])
-
-    source = place.row_in(src_x)
-    target = place.row_in(tgt_x)
-    target_cot = place.row_in(tgt_cot)
-    source_cot = place.row_in(src_cot)
-
-    enc_qkv_w = moves.by_columns(enc_proj, True)
-    enc_o_w = moves.by_rows(enc_oproj, False)
-    enc_in_w = moves.by_columns(enc_in[None], False)
-    enc_out_w = moves.by_rows(enc_out, True)
-    dec_qkv_w = moves.by_columns(dec_proj[0:3], False)
-    dec_o_w = moves.by_rows(dec_oproj[0], True)
-    cross_w = moves.by_columns(dec_proj[3:6], True)
-    cross_o_w = moves.by_rows(dec_oproj[1], False)
-    dec_in_w = moves.by_columns(dec_in[None], False)
-    dec_out_w = moves.by_rows(dec_out, True)
 
     none = jnp.zeros((half,), F32)
     packed = (0, half // PAIR, 2 * half // PAIR)
@@ -590,8 +959,6 @@
 
     dec_du = (product_nt(target_cot, dec_out_w) * dec_slope.astype(F32)).astype(B16)
     dec_dn3 = place.both_cores(product_nt(dec_du, dec_in_w))
-    dec_out_grad = moves.grad_by_rows(dec_acted, target_cot, True)
-    dec_in_grad = moves.grad_by_columns(dec_n3, dec_du, False, 1)[0]
     target_cot_f = target_cot.astype(F32)
     step, gain_four, shift_14 = norm_backward(dec_h2, gain_f[4], dec_dn3)
     grad_h2 = target_cot_f + step
@@ -604,16 +971,11 @@
     cross_dkv = jnp.concatenate([cross_dk, cross_dv], axis=1)
     grad_memory = place.both_cores(product_nt(cross_dkv, cross_w[:, half:]))
     dec_dn2 = place.both_cores(product_nt(cross_dq, cross_w[:, :half]))
-    cross_o_grad = moves.grad_by_rows(cross_mixed, cross_branch, True)
-    cross_q_grad = moves.grad_by_columns(dec_n2, cross_dq, True, 1)
-    cross_kv_grad = moves.grad_by_columns(memory, cross_dkv, False, 2)
 
     source_cot_f = source_cot.astype(F32) + grad_memory
     enc_ff_branch = source_cot_f.astype(B16)
     enc_du = (product_nt(enc_ff_branch, enc_out_w) * enc_slope.astype(F32)).astype(B16)
     enc_dn2 = place.both_cores(product_nt(enc_du, enc_in_w))
-    enc_out_grad = moves.grad_by_rows(enc_acted, enc_ff_branch, True)
-    enc_in_grad = moves.grad_by_columns(enc_n2, enc_du, False, 1)[0]
 
     step, gain_three, shift_10 = norm_backward(dec_h1, gain_f[3], dec_dn2)
     grad_h1 = grad_h2 + step
@@ -626,8 +988,6 @@
         axis=1,
     )
     dec_dn1 = place.both_cores(product_nt(dec_dqkv, dec_qkv_w))
-    dec_o_grad = moves.grad_by_rows(dec_mixed, self_branch, False)
-    dec_qkv_grad = moves.grad_by_columns(dec_n1, dec_dqkv, True, 3)
     step, gain_two, shift_6 = norm_backward(dec_h0, gain_f[2], dec_dn1)
     target_grad = grad_h1 + step
 
@@ -642,8 +1002,6 @@
         axis=1,
     )
     enc_dn1 = place.both_cores(product_nt(enc_dqkv, enc_qkv_w))
-    enc_o_grad = moves.grad_by_rows(enc_mixed, enc_branch, False)
-    enc_qkv_grad = moves.grad_by_columns(enc_n1, enc_dqkv, True, 3)
     step, gain_zero, shift_0 = norm_backward(enc_h0, gain_f[0], enc_dn1)
     source_grad = grad_e1 + step
 
@@ -678,27 +1036,43 @@
             own(column_sum(target_cot)),
         ]
     )
-    small, ffb_grad = moves.small(
+    grads, small, ffb_grad, outputs = moves.sums(
+        {
+            0: (dec_n3, dec_du, 1),
+            2: (dec_n2, cross_dq, 1),
+            3: (memory, cross_dkv, 2),
+            5: (enc_n2, enc_du, 1),
+            7: (dec_n1, dec_dqkv, 3),
+            9: (enc_n1, enc_dqkv, 3),
+        },
+        {
+            1: (dec_acted, target_cot),
+            4: (cross_mixed, cross_branch),
+            6: (enc_acted, enc_ff_branch),
+            8: (dec_mixed, self_branch),
+            10: (enc_mixed, enc_branch),
+        },
         jnp.concatenate([lang_grad, own(gain_rows), bias_rows], axis=0),
         jnp.stack([column_sum(enc_du), column_sum(dec_du)]),
+        [memory, decoded.astype(B16), source_grad.astype(B16), target_grad.astype(B16)],
     )
     return (
-        place.row_out(memory),
-        place.row_out(decoded.astype(B16)),
-        place.row_out(source_grad.astype(B16)).astype(F32),
-        place.row_out(target_grad.astype(B16)).astype(F32),
+        outputs[0],
+        outputs[1],
+        outputs[2].astype(F32),
+        outputs[3].astype(F32),
         small[:langs],
         small[langs : langs + 5],
         small[langs + 5 :],
         ffb_grad,
-        enc_qkv_grad,
-        enc_o_grad,
-        enc_in_grad,
-        enc_out_grad,
-        jnp.concatenate([dec_qkv_grad, cross_q_grad, cross_kv_grad], axis=0),
-        jnp.stack([dec_o_grad, cross_o_grad]),
-        dec_in_grad,
-        dec_out_grad,
+        grads[9],
+        grads[10],
+        grads[5][0],
+        grads[6],
+        jnp.concatenate([grads[7], grads[2], grads[3]], axis=0),
+        jnp.stack([grads[8], grads[4]]),
+        grads[0][0],
+        grads[1],
     )
 
 

time: 1650 us -> 1220 us (0.74)
  Pallas kernels: 183 us -> 818 us
  waiting for transfers between devices: 542 us -> 2.56 us
  starting transfers between devices: 255 us -> 6.53 us
  local copies, waits for them, and re-layouts: 296 us -> 130 us
  other arithmetic: 173 us -> 77.8 us
    pallas_call x0 -> x2, Pallas kernels: none -> 675 us  [the longest x1 337 us: sum_all(): pl.pallas_call(kernel, in_specs=[hbm] * (count + tensors), out_specs=[vme...]
    ppermute x169 -> x12, waiting for transfers between devices: 467 us -> 2.56 us  [over_core(): return lax.ppermute(value, 'dp', [(i, i ^ 1) for i in range(self.dp)])]
    ppermute x169 -> x12, starting transfers between devices: 255 us -> 6.53 us  [over_core(): return lax.ppermute(value, 'dp', [(i, i ^ 1) for i in range(self.dp)])]
    dynamic_slice x31 -> x0, local copies, waits for them, and re-layouts: 86.3 us -> none  [the longest x20 45.7 us: row_out(): piece = lax.dynamic_index_in_dim(mine, q_here ^ m, 0, keepdims=False)]
    unnamed x2 -> x0, waiting for transfers between devices: 74.6 us -> none
    unnamed x577 -> x301, local copies, waits for them, and re-layouts: 83.8 us -> 34.1 us
    another operation x81 -> x1, other arithmetic: 43.3 us -> 1.75 us  [on_device(): jnp.stack([grads[8], grads[4]])]
    reshape x19 -> x15, local copies, waits for them, and re-layouts: 42.8 us -> 10.4 us  [the longest x10 8.06 us: sums(): out.reshape(2, r, parts, 4, -1).transpose(2, 1, 3, 0, 4)]
  transfers between devices with their start and end apart: 170 -> 12, of which waited for: 53 -> 1; matrix products, arithmetic and copies ran while one was open for 35% -> 17% of each run, Pallas kernels for 10% -> 34%
where the time goes in v2:
time: 1220 us; the launch traced here: 1200 us
  Pallas kernels  818 us (67%)
  matrix products  159 us (13%)
  local copies, waits for them, and re-layouts  130 us (11%)
  other arithmetic  77.8 us (6%)
    pallas_call x1, Pallas kernels, sum_all(): pl.pallas_call(kernel, in_specs=[hbm] * (count + tensors), out_specs=[vme...  337 us
    pallas_call x1, Pallas kernels, gather_all(): pl.pallas_call(kernel, in_specs=[hbm] * len(inputs), out_specs=[hbm] * le...  337 us
    pallas_call x3, Pallas kernels, attend_backward(): pl.pallas_call(functools.partial(backward_kernel, causal), grid_spec=pltp...  85.7 us
    pallas_call x3, Pallas kernels, attend_forward(): pl.pallas_call(functools.partial(forward_kernel, causal), grid_spec=pltpu...  57.9 us
    dot_general x15, matrix products, product_tn(): lax.dot_general(left, right, (((0,), (0,)), ((), ())), preferred_element_...  57.1 us
    dot_general x11, matrix products, product_nt(): lax.dot_general(left, right, (((1,), (1,)), ((), ())), preferred_element_...  54.5 us
    dot_general x13, matrix products, product(): return jnp.dot(left, right, preferred_element_type=F32)  47.6 us
    unnamed x301, local copies, waits for them, and re-layouts  34.1 us
  transfers between devices with their start and end apart: 12, of which 1 were waited for; matrix products, arithmetic and copies ran while one was open for 17% of the time, Pallas kernels for 34%

profile of v2, /device:TPU:0, one launch (start us, length us, event | category | flops | bytes accessed | tf_op | source)
XLA Modules:
  0.0 1197.9 jit_solution(14383589608456039273)
XLA Ops:
  26.2 337.4 %gather_all.1 = (bf16[2,2,2,4,16,256]{5,4,3,2,1,0:T(8,128)(2,1)}, bf16[2,2,2,4,32,1536]{5,4,3,2,1,0:T(8,128)(2,1)}, bf16[2,2,1,4,32,1024]{5,4,3,2,1,0:T(8,128)(2...) custom-call(bf16[16,256]{1,0:T(8,128)(2,1)} %reshape.618.refs_0_.ref, ...), custom_call_target="tpu_custom_call" | custom-call | tf_op jit(solution)/shard_map/gather_all/pallas_call | solution.py:494
  388.9 19.8 %attend.2 = (bf16[1024,512]{1,0:T(8,128)(2,1)S(1)}, f32[4,8,1024]{2,1,0:T(8,128)S(1)}) custom-call(s32[17]{0:T(128)S(1)} %get-tuple-element.290.info_ref, bf16[1024,1536]{1,0:T(8,128)(2,1)S(1)} %add_convert_fusion.q_ref.k_ref.v_ref, bf16[1024,1536]{1,0:T(8,128)(2,1)S(1)} %add_convert_fusion.q_ref.k_ref.v_ref, ...), custom_call_target="tpu_custom_call" | custom-call | flops 4294967296 | bytes 4194304 | tf_op jit(solution)/shard_map/attend/pallas_call | solution.py:236
  414.6 6.8 add_convert_fusion.1.q_ref.k_ref.v_ref
  421.5 17.8 %attend_causal.1 = (bf16[1024,512]{1,0:T(8,128)(2,1)S(1)}, f32[4,8,1024]{2,1,0:T(8,128)S(1)}) custom-call(s32[17]{0:T(128)S(1)} %get-tuple-element.289.info_ref, bf16[1024,1536]{1,0:T(8,128)(2,1)S(1)} %add_convert_fusion.1.q_ref.k_ref.v_ref, bf16[1024,1536]{1,0:T(8,128)(2,1)S(1)} %add_convert_fusion.1.q_ref.k_ref.v_ref, ...), custom_call_target="tpu_custom_call" | custom-call | flops 4294967296 | bytes 4194304 | tf_op jit(solution)/shard_map/attend_causal/pallas_call | solution.py:236
  448.2 8.3 multiply_convert_fusion.3
  456.6 7.1 convolution_convert_fusion.15
  474.5 20.3 %attend.3 = (bf16[1024,512]{1,0:T(8,128)(2,1)S(1)}, f32[4,8,1024]{2,1,0:T(8,128)S(1)}) custom-call(s32[17]{0:T(128)S(1)} %pad_add_fusion.1.info_ref, bf16[1024,512]{1,0:T(8,128)(2,1)S(1)} %add_convert_fusion.10.q_ref, bf16[1024,1024]{1,0:T(8,128)(2,1)S(1)} %add_convert_fusion.4.k_ref.v_ref, bf16[1024,1024]{1,0:T(8,128)(2,1)S(1)} %add_convert_fusion.4.k_ref.v_ref, ...), custom_call_target="tpu_custom_call" | custom-call | flops 4294967296 | bytes 4194304 | tf_op jit(solution)/shard_map/attend/pallas_call | solution.py:236
  518.7 9.4 convert_reduce_fusion
  528.0 7.1 convolution_convert_fusion.13
  535.7 6.6 convolution_convert_fusion.5
  559.4 30.0 %attend_grad.2 = (bf16[1024,512]{1,0:T(8,128)(2,1)S(1)}, bf16[1024,512]{1,0:T(8,128)(2,1)S(1)}, bf16[1024,512]{1,0:T(8,128)(2,1)S(1)}) custom-call(s32[17]{0:T(128)S(1)} %pad_add_fusion.1.info_ref, bf16[1024,512]{1,0:T(8,128)(2,1)S(1)} %copy-done.23, bf16[1024,1024]{1,0:T(8,128)(2,1)S(1)} %copy-done.25, bf16[1024,1024]{1,0:T(8,128)(2,1)S(1)} %copy-done.25, ...), custom_call_target="tpu_custom_call" | custom-call | flops 10737418240 | bytes 8388608 | tf_op jit(solution)/shard_map/attend_grad/pallas_call | solution.py:262
  625.9 26.2 %attend_grad_causal.1 = (bf16[1024,512]{1,0:T(8,128)(2,1)S(1)}, bf16[1024,512]{1,0:T(8,128)(2,1)S(1)}, bf16[1024,512]{1,0:T(8,128)(2,1)S(1)}) custom-call(s32[17]{0:T(128)S(1)} %copy-done.9, bf16[1024,1536]{1,0:T(8,128)(2,1)S(1)} %copy-done.21, bf16[1024,1536]{1,0:T(8,128)(2,1)S(1)} %copy-done.21, bf16[1024,1536]{1,0:T(8,128)(2,1)S(1)} %copy-done.21, ...), custom_call_target="tpu_custom_call" | custom-call | flops 10737418240 | bytes 8388608 | tf_op jit(solution)/shard_map/attend_grad_causal/pallas_call | solution.py:262
  669.0 7.9 convert_reduce_fusion.1
  687.4 9.6 convolution_convert_fusion.2
  697.0 6.7 convolution_convert_fusion.3
  716.0 29.5 %attend_grad.3 = (bf16[1024,512]{1,0:T(8,128)(2,1)S(1)}, bf16[1024,512]{1,0:T(8,128)(2,1)S(1)}, bf16[1024,512]{1,0:T(8,128)(2,1)S(1)}) custom-call(s32[17]{0:T(128)S(1)} %copy-done.7, bf16[1024,1536]{1,0:T(8,128)(2,1)S(1)} %copy-done.19, bf16[1024,1536]{1,0:T(8,128)(2,1)S(1)} %copy-done.19, bf16[1024,1536]{1,0:T(8,128)(2,1)S(1)} %copy-done.19, ...), custom_call_target="tpu_custom_call" | custom-call | flops 10737418240 | bytes 8388608 | tf_op jit(solution)/shard_map/attend_grad/pallas_call | solution.py:262
  751.5 7.8 convolution_convert_fusion.8
  764.4 7.1 fusion.70
  771.5 6.8 reshape.648
  778.2 8.8 dynamic-slice_reduce_fusion
  803.0 7.6 fusion.71
  810.5 6.6 reshape.646
  817.1 8.7 dynamic-slice_reduce_fusion.1
  833.7 337.4 %sum_all.1 = (f32[2,32,2048]{2,1,0:T(8,128)}, f32[128,1024]{1,0:T(8,128)}, f32[2,32,512]{2,1,0:T(8,128)}, f32[2,32,1024]{2,1,0:T(8,128)}, f32[32,1024]{1,0:T(8,1...) custom-call(bf16[2,2,2,4,32,2048]{5,4,3,2,1,0:T(8,128)(2,1)} %bitcas, ...), custom_call_target="tpu_custom_call" | custom-call | tf_op jit(solution)/shard_map/sum_all/pallas_call | solution.py:691
  (544 shorter events, 253.5 us)
Async XLA Ops:
  2.9 373.7 %collective-permute-start = (s32[2,2057]{1,0:T(2,128)}, s32[2,2057]{1,0:T(2,128)}, u32[]{:S(2)}, u32[]{:S(2)}) collective-permute-start(s32[2,2057]{1,0:T(2,128)} %concatenate.110), channel_id=1, source_target_pairs={{0,4},{4,0},{8,12},{12,8},{16,20},{20,16},{24,28},{28,24},{1,5},{5... | collective-permute-start | bytes 49376 | tf_op jit(solution)/shard_map/ppermute | solution.py:720
  369.9 44.7 %copy-start.87 = (f32[1024]{0:T(1024)}, f32[1024]{0:T(1024)S(1)}, u32[]{:S(2)}) copy-start(f32[1024]{0:T(1024)S(1)} %mul.155) | copy-start | bytes 12292
  371.1 74.0 %copy-start.105 = (f32[1024]{0:T(1024)}, f32[1024]{0:T(1024)S(1)}, u32[]{:S(2)}) copy-start(f32[1024]{0:T(1024)S(1)} %add.384) | copy-start | bytes 12292
  372.7 41.9 %copy-start.107 = (f32[1024]{0:T(1024)}, f32[1024]{0:T(1024)S(1)}, u32[]{:S(2)}) copy-start(f32[1024]{0:T(1024)S(1)} %add.354) | copy-start | bytes 12292
  378.7 178.2 %copy-start = (s32[1024,1]{1,0:T(8,128)}, s32[1024,1]{1,0:T(8,128)S(1)}, u32[]{:S(2)}) copy-start(s32[1024,1]{1,0:T(8,128)S(1)} %copy.156.kseg_ref) | copy-start | bytes 12292
  382.2 31.5 %copy-start.33 = (f32[1024,1024]{1,0:T(8,128)}, f32[1024,1024]{1,0:T(8,128)S(1)}, u32[]{:S(2)}) copy-start(f32[1024,1024]{1,0:T(8,128)S(1)} %get-tuple-element.276) | copy-start | bytes 12582916
  382.2 32.4 %copy-start.81 = (f32[1024]{0:T(1024)}, f32[1024]{0:T(1024)S(1)}, u32[]{:S(2)}) copy-start(f32[1024]{0:T(1024)S(1)} %broadcast_multiply_fusion.14) | copy-start | bytes 12292
  384.6 36.9 %copy-start.8 = (s32[17]{0:T(128)}, s32[17]{0:T(128)S(1)}, u32[]{:S(2)}) copy-start(s32[17]{0:T(128)S(1)} %get-tuple-element.289.info_ref) | copy-start | bytes 208
  410.0 30.7 %collective-permute-start.2 = (bf16[1024,1024]{1,0:T(8,128)(2,1)S(1)}, bf16[1024,1024]{1,0:T(8,128)(2,1)}, u32[]{:S(2)}, u32[]{:S(2)}) collective-permute-start(bf16[1024,1024]{1,0:T(8,128)(2,1)S(1)} %convolution_convert_fusion.16), channel_id=1, source_target_pairs={{0,4},{4,0},{8,12},{12,8},{16,20},{20,16},{24,28},{28,24},{1,5},{5... | collective-permute-start | bytes 6291464 | tf_op jit(solution)/shard_map/ppermute | solution.py:720
  440.6 23.8 %collective-permute-start.1 = (bf16[1024,1024]{1,0:T(8,128)(2,1)S(1)}, bf16[1024,1024]{1,0:T(8,128)(2,1)S(1)}, u32[]{:S(2)}, u32[]{:S(2)}) collective-permute-start(bf16[1024,1024]{1,0:T(8,128)(2,1)S(1)} %convolution_convert_fusion.17), channel_id=1, source_target_pairs={{0,4},{4,0},{8,12},{12,8},{16,20},{20,16},{24,28},{28,24},{1,5},{5... | collective-permute-start | bytes 6291464 | tf_op jit(solution)/shard_map/ppermute | solution.py:720
  444.5 26.3 %copy-start.28 = (f32[1024,1024]{1,0:T(8,128)}, f32[1024,1024]{1,0:T(8,128)S(1)}, u32[]{:S(2)}) copy-start(f32[1024,1024]{1,0:T(8,128)S(1)} %get-tuple-element.244) | copy-start | bytes 12582916
  463.6 7.2 collective-permute-start.3
  497.4 4.6 collective-permute-start.4
  535.1 13.5 %collective-permute-start.5 = (bf16[1024,1024]{1,0:T(8,128)(2,1)S(1)}, bf16[1024,1024]{1,0:T(8,128)(2,1)S(1)}, u32[]{:S(2)}, u32[]{:S(2)}) collective-permute-start(bf16[1024,1024]{1,0:T(8,128)(2,1)S(1)} %convolution_convert_fusion.13), channel_id=1, source_target_pairs={{0,4},{4,0},{8,12},{12,8},{16,20},{20,16},{24,28},{28,24},{1,5},{5... | collective-permute-start | bytes 6291464 | tf_op jit(solution)/shard_map/ppermute | solution.py:720
  535.6 16.2 %collective-permute-start.11 = (bf16[1024,1024]{1,0:T(8,128)(2,1)S(1)}, bf16[1024,1024]{1,0:T(8,128)(2,1)S(1)}, u32[]{:S(2)}, u32[]{:S(2)}) collective-permute-start(bf16[1024,1024]{1,0:T(8,128)(2,1)S(1)} %convolution_convert_fusion.6), channel_id=1, source_target_pairs={{0,4},{4,0},{8,12},{12,8},{16,20},{20,16},{24,28},{28,24},{1,5},{5... | collective-permute-start | bytes 6291464 | tf_op jit(solution)/shard_map/ppermute | solution.py:720
  555.7 33.7 %copy-start.39 = (f32[1024,1024]{1,0:T(8,128)}, f32[1024,1024]{1,0:T(8,128)S(1)}, u32[]{:S(2)}) copy-start(f32[1024,1024]{1,0:T(8,128)S(1)} %get-tuple-element.234) | copy-start | bytes 12582916
  593.7 20.8 %collective-permute-start.7 = (bf16[1024,1024]{1,0:T(8,128)(2,1)}, bf16[1024,1024]{1,0:T(8,128)(2,1)}, u32[]{:S(2)}, u32[]{:S(2)}) collective-permute-start(bf16[1024,1024]{1,0:T(8,128)(2,1)} %convolution_convert_fusion.10), channel_id=1, source_target_pairs={{0,4},{4,0},{8,12},{12,8},{16,20},{20,16},{24,28},{28,24},{1,5},{5... | collective-permute-start | bytes 6291464 | tf_op jit(solution)/shard_map/ppermute | solution.py:720
  604.9 60.5 %copy-start.46 = (bf16[1024,1024]{1,0:T(8,128)(2,1)}, bf16[1024,1024]{1,0:T(8,128)(2,1)S(1)}, u32[]{:S(2)}) copy-start(bf16[1024,1024]{1,0:T(8,128)(2,1)S(1)} %convolution_convert_fusion.11) | copy-start | bytes 6291460
  604.9 60.4 %collective-permute-start.6 = (bf16[1024,1024]{1,0:T(8,128)(2,1)S(1)}, bf16[1024,1024]{1,0:T(8,128)(2,1)S(1)}, u32[]{:S(2)}, u32[]{:S(2)}) collective-permute-start(bf16[1024,1024]{1,0:T(8,128)(2,1)S(1)} %convolution_convert_fusion.11), channel_id=1, source_target_pairs={{0,4},{4,0},{8,12},{12,8},{16,20},{20,16},{24,28},{28,24},{1,5},{5... | collective-permute-start | bytes 6291464 | tf_op jit(solution)/shard_map/ppermute | solution.py:720
  622.0 30.9 %copy-start.37 = (f32[1024,1024]{1,0:T(8,128)}, f32[1024,1024]{1,0:T(8,128)S(1)}, u32[]{:S(2)}) copy-start(f32[1024,1024]{1,0:T(8,128)S(1)} %get-tuple-element.236) | copy-start | bytes 12582916
  683.1 20.7 %collective-permute-start.8 = (bf16[1024,1024]{1,0:T(8,128)(2,1)S(1)}, bf16[1024,1024]{1,0:T(8,128)(2,1)}, u32[]{:S(2)}, u32[]{:S(2)}) collective-permute-start(bf16[1024,1024]{1,0:T(8,128)(2,1)S(1)} %convolution_convert_fusion.9), channel_id=1, source_target_pairs={{0,4},{4,0},{8,12},{12,8},{16,20},{20,16},{24,28},{28,24},{1,5},{5... | collective-permute-start | bytes 6291464 | tf_op jit(solution)/shard_map/ppermute | solution.py:720
  687.0 72.4 %collective-permute-start.10 = (bf16[1024,1024]{1,0:T(8,128)(2,1)}, bf16[1024,1024]{1,0:T(8,128)(2,1)}, u32[]{:S(2)}, u32[]{:S(2)}) collective-permute-start(bf16[1024,1024]{1,0:T(8,128)(2,1)} %convolution_convert_fusion.7), channel_id=1, source_target_pairs={{0,4},{4,0},{8,12},{12,8},{16,20},{20,16},{24,28},{28,24},{1,5},{5... | collective-permute-start | bytes 6291464 | tf_op jit(solution)/shard_map/ppermute | solution.py:720
  712.1 33.4 %copy-start.38 = (f32[1024,1024]{1,0:T(8,128)}, f32[1024,1024]{1,0:T(8,128)S(1)}, u32[]{:S(2)}) copy-start(f32[1024,1024]{1,0:T(8,128)S(1)} %get-tuple-element.240) | copy-start | bytes 12582916
  759.3 37.7 %collective-permute-start.9 = (bf16[1024,1024]{1,0:T(8,128)(2,1)}, bf16[1024,1024]{1,0:T(8,128)(2,1)}, u32[]{:S(2)}, u32[]{:S(2)}) collective-permute-start(bf16[1024,1024]{1,0:T(8,128)(2,1)} %convolution_convert_fusion.8), channel_id=1, source_target_pairs={{0,4},{4,0},{8,12},{12,8},{16,20},{20,16},{24,28},{28,24},{1,5},{5... | collective-permute-start | bytes 6291464 | tf_op jit(solution)/shard_map/ppermute | solution.py:720
  (120 other events, 713.6 us)

commit v3 on v2

v3 whole, which is shorter than its diff:
```python
import functools

import jax
import jax.numpy as jnp
from jax import lax
from jax.experimental import pallas as pl
from jax.experimental.pallas import tpu as pltpu
from jax.sharding import Mesh
from jax.sharding import PartitionSpec as P

HEAD_DIM = 64
EPSILON = 1e-05
MASKED = -1000000000.0
BLOCK = 256
HEADS = 4
GROUP = HEADS * HEAD_DIM
B16 = jnp.bfloat16
F32 = jnp.float32


def product(left, right):
    return jnp.dot(left, right, preferred_element_type=F32)


def product_tn(left, right):
    return lax.dot_general(left, right, (((0,), (0,)), ((), ())), preferred_element_type=F32)


def product_nt(left, right):
    return lax.dot_general(left, right, (((1,), (1,)), ((), ())), preferred_element_type=F32)


def column_sum(values):
    return jnp.sum(values.astype(F32), axis=0)


def norm_parts(hidden):
    centred = hidden - jnp.mean(hidden, axis=-1, keepdims=True)
    spread = jnp.mean(centred * centred, axis=-1, keepdims=True)
    scale = lax.rsqrt(spread + EPSILON)
    return centred * scale, scale


def layer_norm(hidden, gain_row, shift_row):
    return (norm_parts(hidden)[0] * gain_row + shift_row).astype(B16)


def norm_backward(hidden, gain_row, grad):
    unit, scale = norm_parts(hidden)
    weighted = grad * gain_row
    grad_hidden = scale * (
        weighted
        - jnp.mean(weighted, axis=-1, keepdims=True)
        - unit * jnp.mean(weighted * unit, axis=-1, keepdims=True)
    )
    return grad_hidden, jnp.sum(grad * unit, axis=0), jnp.sum(grad, axis=0)


def gelu_both(values):
    below = 0.5 * (1.0 + lax.erf(values * (0.5**0.5)))
    density = jnp.exp(-0.5 * values * values) * (0.5 / jnp.pi) ** 0.5
    return (values * below).astype(B16), (below + values * density).astype(B16)


def allowed_block(causal, kseg_ref, qseg, length, key_at, query_at):
    allowed = kseg_ref[key_at : key_at + BLOCK, :] == qseg
    if causal:
        keys = key_at + lax.broadcasted_iota(jnp.int32, (BLOCK, BLOCK), 0)
        queries = query_at + lax.broadcasted_iota(jnp.int32, (BLOCK, BLOCK), 1)
        allowed = allowed & (keys <= queries) & ((keys < length) | (keys == queries))
    return allowed


def dot_nt(left, right):
    return lax.dot_general(left, right, (((1,), (1,)), ((), ())), preferred_element_type=F32)


def head_masked(value):
    lane = lax.broadcasted_iota(jnp.int32, value.shape, 1) // HEAD_DIM
    zero = jnp.zeros_like(value)
    return [jnp.where(lane == h, value, zero) for h in range(HEADS)]


def fold_rows(value, combine):
    return combine(value.reshape(value.shape[0] // 8, 8, value.shape[1]), axis=0)


def forward_kernel(
    causal, info_ref, q_ref, k_ref, v_ref, qseg_ref, kseg_ref, o_ref, lse_ref, vt_ref, s_ref, acc_ref, top_ref, sum_ref
):
    block = pl.program_id(1)
    blocks = k_ref.shape[0] // BLOCK
    length = info_ref[blocks * blocks]

    @pl.when(block == 0)
    def _():
        vt_ref[...] = v_ref[...].T

    qseg = qseg_ref[...]
    heads = head_masked(q_ref[...] * jnp.asarray(HEAD_DIM**-0.5, B16))
    top_ref[...] = jnp.full(top_ref.shape, -1e30, F32)
    sum_ref[...] = jnp.zeros_like(sum_ref)
    acc_ref[...] = jnp.zeros_like(acc_ref)
    for j in range(blocks):

        @pl.when(info_ref[block * blocks + j] > 0)
        def _(j=j):
            keys = k_ref[j * BLOCK : (j + 1) * BLOCK, :]
            allowed = allowed_block(causal, kseg_ref, qseg, length, j * BLOCK, block * BLOCK)
            for h in range(HEADS):
                scores = jnp.where(allowed, dot_nt(keys, heads[h]), MASKED)
                s_ref[h, j * BLOCK : (j + 1) * BLOCK, :] = scores
                top_ref[h] = jnp.maximum(top_ref[h], fold_rows(scores, jnp.max))

    highest = [jnp.max(top_ref[h], axis=0, keepdims=True) for h in range(HEADS)]
    for j in range(blocks):

        @pl.when(info_ref[block * blocks + j] > 0)
        def _(j=j):
            for h in range(HEADS):
                weights = jnp.exp(s_ref[h, j * BLOCK : (j + 1) * BLOCK, :] - highest[h])
                sum_ref[h] += fold_rows(weights, jnp.sum)
                rows = slice(h * HEAD_DIM, (h + 1) * HEAD_DIM)
                acc_ref[rows, :] += jnp.dot(
                    vt_ref[rows, j * BLOCK : (j + 1) * BLOCK],
                    weights.astype(B16),
                    preferred_element_type=F32,
                )

    lse_ref[...] = jnp.zeros_like(lse_ref)
    for h in range(HEADS):
        total = jnp.sum(sum_ref[h], axis=0, keepdims=True)
        rows = slice(h * HEAD_DIM, (h + 1) * HEAD_DIM)
        acc_ref[rows, :] = acc_ref[rows, :] / total
        lse_ref[0, h : h + 1, :] = highest[h] + jnp.log(total)
    o_ref[...] = acc_ref[...].T.astype(B16)


def backward_kernel(
    causal,
    info_ref,
    q_ref,
    k_ref,
    v_ref,
    o_ref,
    do_ref,
    lse_ref,
    qseg_ref,
    kseg_ref,
    *rest,
):
    *outs, kt_ref, dqt_ref, sums_ref, done_ref, sems = rest
    group, block = pl.program_id(0), pl.program_id(1)
    groups = pl.num_programs(0)
    blocks = k_ref.shape[0] // BLOCK
    length = info_ref[blocks * blocks]

    @pl.when(block == 0)
    def _():
        kt_ref[...] = k_ref[...].T
        sums_ref[...] = jnp.zeros_like(sums_ref)

    qseg = qseg_ref[...]
    grads = do_ref[...]
    query_heads = head_masked(q_ref[...] * jnp.asarray(HEAD_DIM**-0.5, B16))
    grad_heads = head_masked(grads)
    queries_down = jnp.concatenate(query_heads, axis=0)
    grads_down = jnp.concatenate(grad_heads, axis=0)
    mixed = grads.astype(F32) * o_ref[...].astype(F32)
    lane = lax.broadcasted_iota(jnp.int32, (8, GROUP), 1) // HEAD_DIM
    picks = (lane == lax.broadcasted_iota(jnp.int32, (8, GROUP), 0)).astype(F32)
    inner = lax.dot_general(
        picks, mixed, (((1,), (1,)), ((), ())), precision=lax.Precision.HIGHEST, preferred_element_type=F32
    )
    dqt_ref[...] = jnp.zeros_like(dqt_ref)
    for j in range(blocks):

        @pl.when(info_ref[block * blocks + j] > 0)
        def _(j=j):
            rows = slice(j * BLOCK, (j + 1) * BLOCK)
            keys = k_ref[rows, :]
            values = v_ref[rows, :]
            allowed = allowed_block(causal, kseg_ref, qseg, length, j * BLOCK, block * BLOCK)
            all_chances, all_scores = [], []
            for h in range(HEADS):
                scores = dot_nt(keys, query_heads[h])
                chances = jnp.where(allowed, jnp.exp(scores - lse_ref[0, h : h + 1, :]), 0.0)
                grad_chances = dot_nt(values, grad_heads[h])
                grad_scores = (chances * (grad_chances - inner[h : h + 1, :])).astype(B16)
                all_chances.append(chances.astype(B16))
                all_scores.append(grad_scores)
                part = slice(h * HEAD_DIM, (h + 1) * HEAD_DIM)
                dqt_ref[part, :] += jnp.dot(kt_ref[part, rows], grad_scores, preferred_element_type=F32)
            sums_ref[0, rows, :] += jnp.dot(
                jnp.concatenate(all_scores, axis=1), queries_down, preferred_element_type=F32
            )
            sums_ref[1, rows, :] += jnp.dot(
                jnp.concatenate(all_chances, axis=1), grads_down, preferred_element_type=F32
            )

    here = pl.ds(pl.multiple_of(block * BLOCK, BLOCK), BLOCK)
    done_ref[0, here, :] = (dqt_ref[...].T * HEAD_DIM**-0.5).astype(B16)

    @pl.when(block == blocks - 1)
    def _():
        done_ref[1] = sums_ref[0].astype(B16)
        done_ref[2] = sums_ref[1].astype(B16)
        width = k_ref.shape[1]
        copies = []
        for k in range(3):
            out, place = (outs[0], k) if len(outs) == 1 else (outs[min(k, 1)], max(k - 1, 0))
            lanes = pl.ds(pl.multiple_of((place * groups + group) * width, width), width)
            copies.append(pltpu.make_async_copy(done_ref.at[k], out.at[:, lanes], sems.at[k]))
        for copy in copies:
            copy.start()
        for copy in copies:
            copy.wait()


def block_info(causal, query_seg, key_seg, length):
    blocks = query_seg.shape[0] // BLOCK
    query_low, query_high = query_seg[::BLOCK], query_seg[BLOCK - 1 :: BLOCK]
    key_low, key_high = key_seg[::BLOCK], key_seg[BLOCK - 1 :: BLOCK]
    meets = (key_low[None, :] <= query_high[:, None]) & (key_high[None, :] >= query_low[:, None])
    if causal:
        at = jnp.arange(blocks)
        meets = meets & (at[None, :] <= at[:, None])
    return jnp.concatenate([meets.astype(jnp.int32).reshape(-1), length[None]])


def attention_specs(count, offsets):
    query = pl.BlockSpec((BLOCK, GROUP), lambda p, i, info: (i, p + offsets[0]))
    key = pl.BlockSpec((count, GROUP), lambda p, i, info: (0, p + offsets[1]))
    value = pl.BlockSpec((count, GROUP), lambda p, i, info: (0, p + offsets[2]))
    plain = pl.BlockSpec((BLOCK, GROUP), lambda p, i, info: (i, p))
    whole = pl.BlockSpec((count, GROUP), lambda p, i, info: (0, p))
    stats = pl.BlockSpec((1, 8, BLOCK), lambda p, i, info: (p, 0, i))
    qseg = pl.BlockSpec((1, BLOCK), lambda p, i, info: (0, i))
    kseg = pl.BlockSpec((count, 1), lambda p, i, info: (0, 0))
    return query, key, value, plain, whole, stats, qseg, kseg


def attend_forward(causal, masks, queries, keys, values, offsets, width):
    info, qseg_row, kseg_column = masks
    count = queries.shape[0]
    groups = width // GROUP
    query, key, value, plain, _, stats, qseg, kseg = attention_specs(count, offsets)
    return pl.pallas_call(
        functools.partial(forward_kernel, causal),
        grid_spec=pltpu.PrefetchScalarGridSpec(
            num_scalar_prefetch=1,
            grid=(groups, count // BLOCK),
            in_specs=[query, key, value, qseg, kseg],
            out_specs=[plain, stats],
            scratch_shapes=[pltpu.VMEM((GROUP, count), B16), pltpu.VMEM((HEADS, count, BLOCK), F32), pltpu.VMEM((GROUP, BLOCK), F32)]
            + [pltpu.VMEM((HEADS, 8, BLOCK), F32)] * 2,
        ),
        out_shape=[
            jax.ShapeDtypeStruct((count, width), B16),
            jax.ShapeDtypeStruct((groups, 8, count), F32),
        ],
        compiler_params=pltpu.CompilerParams(vmem_limit_bytes=24 * 2**20),
        cost_estimate=pl.CostEstimate(
            flops=2 * 2 * count * count * width * 2, bytes_accessed=count * width * 8, transcendentals=0
        ),
        name="attend_causal" if causal else "attend",
    )(info, queries, keys, values, qseg_row, kseg_column)


def attend_backward(causal, masks, queries, keys, values, offsets, width, mixed, lse, grad):
    widths = (3 * width,) if queries is keys else (width, 2 * width)
    info, qseg_row, kseg_column = masks
    count = queries.shape[0]
    groups = width // GROUP
    query, key, value, plain, _, stats, qseg, kseg = attention_specs(count, offsets)
    return pl.pallas_call(
        functools.partial(backward_kernel, causal),
        grid_spec=pltpu.PrefetchScalarGridSpec(
            num_scalar_prefetch=1,
            grid=(groups, count // BLOCK),
            in_specs=[query, key, value, plain, plain, stats, qseg, kseg],
            out_specs=[pl.BlockSpec(memory_space=pl.ANY)] * len(widths),
            scratch_shapes=[
                pltpu.VMEM((GROUP, count), B16),
                pltpu.VMEM((GROUP, BLOCK), F32),
                pltpu.VMEM((2, count, GROUP), F32),
                pltpu.VMEM((3, count, GROUP), B16),
                pltpu.SemaphoreType.DMA((3,)),
            ],
        ),
        out_shape=[jax.ShapeDtypeStruct((count, w), B16) for w in widths],
        compiler_params=pltpu.CompilerParams(vmem_limit_bytes=24 * 2**20),
        cost_estimate=pl.CostEstimate(
            flops=5 * 2 * count * count * width * 2, bytes_accessed=count * width * 16, transcendentals=0
        ),
        name="attend_grad_causal" if causal else "attend_grad",
    )(info, queries, keys, values, mixed, grad, lse, qseg_row, kseg_column)


MESH = pl.DeviceIdType.MESH
GATHER_LAGS = (0, 1, 2, 3)
ROW_LAG = 4
SUM_CUT = 20
SUM_ROWS = [1, 3, 5, 7]


def own_columns(array, core, runs=8):
    split = array.reshape(array.shape[:-1] + (runs // 2, 2, array.shape[-1] // runs))
    mine = lax.dynamic_index_in_dim(split, core, split.ndim - 2, keepdims=False)
    return mine.reshape(array.shape[:-1] + (array.shape[-1] // 2,))


def lay_side(array):
    return jnp.concatenate([array[i] for i in range(array.shape[0])], axis=1)


def lay_wide(arrays):
    return arrays[0] if len(arrays) == 1 else jnp.concatenate(arrays, axis=1)


def xor_arrange(pieces, place):
    pieces, bit = list(pieces), 0
    while 1 << bit < len(pieces):
        odd = ((place >> bit) & 1) == 1
        pieces = [jnp.where(odd, pieces[k ^ (1 << bit)], pieces[k]) for k in range(len(pieces))]
        bit += 1
    return pieces


class Here:
    def __init__(self):
        self.at = lax.axis_index("dp")
        self.c = lax.axis_index("core")
        self.z = lax.axis_index("seq")
        self.x = self.at % 2
        self.y = self.at // 2
        self.core_peer = (self.at, 1 - self.c, self.z)
        self.x_peer = (self.at + 1 - 2 * self.x, self.c, self.z)
        self.y_peer = (self.at + 2 - 4 * self.y, self.c, self.z)
        self.edge = (self.z % 3) == 0
        self.inner = jnp.logical_not(self.edge)

    def z_flip(self, j):
        return (self.z // 2 + j // 2) % 2 * 2 + (self.z % 2 + j % 2) % 2

    def z_peer(self, j):
        return (self.at, self.c, self.z_flip(j))

    def enter(self):
        barrier = pltpu.get_barrier_semaphore()
        peers = [self.x_peer, self.y_peer, self.core_peer]
        for j in range(1, 4):
            peers += [(self.at, self.c, self.z_flip(j)), (self.at, 1 - self.c, self.z_flip(j))]
        for peer in peers:
            pl.semaphore_signal(barrier, inc=1, device_id=peer, device_id_type=MESH)
        pl.semaphore_wait(barrier, len(peers))


def remote(source, target, send_sem, recv_sem, peer):
    return pltpu.make_async_remote_copy(
        src_ref=source,
        dst_ref=target,
        send_sem=send_sem,
        recv_sem=recv_sem,
        device_id=peer,
        device_id_type=MESH,
    )


class GatherItem:
    def __init__(self, here, mine, other, out, start, size, send, recv, local):
        self.here, self.mine, self.other, self.out = here, mine, other, out
        self.send, self.recv, self.local = send, recv, local
        self.all = pl.ds(start, size)
        self.sides = pl.ds(start, size // 2), pl.ds(start + size // 2, size // 2)
        self.core = here.c if other is not None else 0
        self.copies = {}

    def move(self, slot, region, peer, arrive=None):
        recv = self.recv.at[slot if arrive is None else arrive]
        self.copies[slot] = remote(region, region, self.send.at[slot], recv, peer)
        return self.copies[slot]

    def begin(self):
        here = self.here
        block = self.out.at[here.y, here.x, self.core, here.z, :, self.all]
        self.own = pltpu.make_async_copy(self.mine.at[:, self.all], block, self.local)
        self.own.start()
        if self.other is not None:
            other = self.other.at[:, self.all]
            self.copies[0] = remote(other, block, self.send.at[0], self.recv.at[0], here.core_peer)
            self.copies[0].start()

    def stage_z(self):
        here = self.here
        self.own.wait()
        if self.other is not None:
            self.copies[0].wait_recv()
        block = self.out.at[here.y, here.x, :, here.z, :, self.all]
        self.move(1, block, here.z_peer(1)).start()
        self.move(2, block, here.z_peer(2)).start()
        pl.when(here.inner)(self.move(3, block, here.z_peer(3)).start)

    def stage_pass(self):
        here = self.here
        self.copies[2].wait_recv()
        block = self.out.at[here.y, here.x, :, here.z_flip(2), :, self.all]
        pl.when(here.inner)(self.move(8, block, here.z_peer(1), arrive=3).start)

    def stage_one(self):
        here, (a, b) = self.here, self.sides
        self.copies[1].wait_recv()
        self.copies[3].wait_recv()
        self.move(4, self.out.at[here.y, here.x, :, :, :, a], here.x_peer).start()
        self.move(5, self.out.at[here.y, here.x, :, :, :, b], here.y_peer).start()

    def stage_two(self):
        here, (a, b) = self.here, self.sides
        self.copies[4].wait_recv()
        self.move(6, self.out.at[here.y, :, :, :, :, a], here.y_peer).start()
        self.copies[5].wait_recv()
        self.move(7, self.out.at[:, here.x, :, :, :, b], here.x_peer).start()

    def finish(self):
        self.copies[6].wait_recv()
        self.copies[7].wait_recv()
        for slot, copy in self.copies.items():
            if slot in (3, 8):
                pl.when(self.here.inner)(copy.wait_send)
            else:
                copy.wait_send()


class RowIn:
    def __init__(self, here, source, out, send, recv, local):
        self.here, self.source, self.out = here, source, out
        self.send, self.recv, self.local = send, recv, local
        self.half = source.shape[-1] // 2

    def lanes(self, f):
        return pl.ds(f * self.half, self.half) if isinstance(f, int) else pl.ds(pl.multiple_of(f * self.half, 128), self.half)

    def parts(self):
        here = self.here
        for i in range(2):
            for f in range(2):
                source = self.source.at[i, :, self.lanes(f)]
                target = self.out.at[here.z, :, self.lanes(f)]
                self_sent = (2 * here.c + i == here.z) & (here.c == f)
                peer = (here.at, f, 2 * here.c + i)
                away = remote(source, target, self.send.at[2 * i + f], self.recv.at[here.z], peer)
                stay = pltpu.make_async_copy(source, target, self.local)
                yield self_sent, away, stay

    def begin(self):
        for self_sent, away, stay in self.parts():
            pl.when(self_sent)(stay.start)
            pl.when(jnp.logical_not(self_sent))(away.start)

    def across(self):
        here = self.here
        lanes = self.lanes(here.c)
        for k in range(4):
            target = self.out.at[k, :, lanes]
            from_self = (here.z == k) & (here.z // 2 == here.c)
            stay = pltpu.make_async_copy(target, target, self.local)
            away = remote(target, target, self.send.at[0], self.recv.at[k], here.core_peer)
            pl.when(from_self)(stay.wait)
            pl.when(jnp.logical_not(from_self))(away.wait_recv)
        region = self.out.at[:, :, lanes]
        self.copy = remote(region, region, self.send.at[4], self.recv.at[4], here.core_peer)
        self.copy.start()

    def finish(self):
        self.copy.wait()
        for self_sent, away, _ in self.parts():
            pl.when(jnp.logical_not(self_sent))(away.wait_send)


def gather_kernel(kinds, cuts, rows_at, refs):
    here = Here()
    refs = list(refs)
    take = lambda n: [refs.pop(0) for _ in range(n)]
    count = len(kinds)
    ins = [take(2) if columns else take(1) + [None] for columns in kinds]
    row_ins = take(len(rows_at))
    outs = take(count)
    row_outs = take(len(rows_at))
    send, recv, local, row_send, row_recv, row_local = refs
    items = []
    for k, (mine, other) in enumerate(ins):
        size = mine.shape[-1] // cuts[k]
        for cut in range(cuts[k]):
            n = len(items)
            items.append(
                GatherItem(here, mine, other, outs[k], cut * size, size, send.at[n], recv.at[n], local.at[n])
            )
    count = len(items)
    rows = [
        RowIn(here, row_ins[t], row_outs[t], row_send.at[t], row_recv.at[t], row_local.at[t])
        for t in range(len(rows_at))
    ]
    here.enter()
    for item in items:
        item.begin()
    steps = (GatherItem.stage_z, GatherItem.stage_pass, GatherItem.stage_one, GatherItem.stage_two)
    for step in range(count + GATHER_LAGS[-1] + 1):
        for t, start in enumerate(rows_at):
            if start == step:
                rows[t].begin()
            if min(start + ROW_LAG, count + GATHER_LAGS[-1]) == step:
                rows[t].across()
        for stage, lag in zip(steps, GATHER_LAGS):
            if 0 <= step - lag < count:
                stage(items[step - lag])
    for item in items:
        item.finish()
    for row in rows:
        row.finish()


def gather_all(locals_, rows, rows_at):
    kinds = [other is not None for _, other in locals_]
    inputs = [v for pair in locals_ for v in pair if v is not None] + list(rows)
    shapes = [
        jax.ShapeDtypeStruct((2, 2, 2 if other is not None else 1, 4) + mine.shape, mine.dtype)
        for mine, other in locals_
    ] + [jax.ShapeDtypeStruct((4,) + row.shape[1:], row.dtype) for row in rows]
    cuts = [2 if mine.size * (1 + columns) > 2**17 else 1 for (mine, _), columns in zip(locals_, kinds)]
    count, tensors = sum(cuts), len(rows)
    hbm = pl.BlockSpec(memory_space=pl.ANY)

    def kernel(*refs):
        gather_kernel(kinds, cuts, rows_at, refs)

    dma = pltpu.SemaphoreType.DMA
    return pl.pallas_call(
        kernel,
        in_specs=[hbm] * len(inputs),
        out_specs=[hbm] * len(shapes),
        out_shape=shapes,
        scratch_shapes=[
            dma((count, 9)),
            dma((count, 9)),
            dma((count,)),
            dma((tensors, 5)),
            dma((tensors, 5)),
            dma((tensors,)),
        ],
        compiler_params=pltpu.CompilerParams(collective_id=0, has_side_effects=True),
        name="gather_all",
    )(*inputs)


class SumItem:
    def __init__(self, here, source, out, start, scratch, send, recv, local):
        self.here, self.source, self.out = here, source, out
        self.own, self.b1, self.b2, self.b3, self.met = scratch[:5]
        self.columns = source.shape[2] == 2
        if self.columns:
            self.b4, self.b4s = scratch[5:]
        self.send, self.recv, self.local = send, recv, local
        size = self.own.shape[-1]
        self.half = size // 2
        self.sides = pl.ds(0, self.half), pl.ds(self.half, self.half)
        self.cut = slice(start, start + size)
        self.source_sides = pl.ds(start, self.half), pl.ds(start + self.half, self.half)
        self.copies = {}

    def make(self, slot, source, target, peer):
        self.copies[slot] = remote(source, target, self.send.at[slot], self.recv.at[slot], peer)
        return self.copies[slot]

    def go(self, slot, source, target, peer):
        self.make(slot, source, target, peer).start()

    def blocks(self, body):
        cores = self.b2.shape[0]

        def step(k, carry):
            body(k // 4, k % 4)
            return carry

        lax.fori_loop(0, cores * 4, step, 0)

    def stage_one(self):
        here, (a, b), source = self.here, self.sides, self.source
        first, second = self.source_sides
        self.go(0, source.at[:, 1 - here.x, :, :, :, first], self.b1.at[:, :, :, :, a], here.x_peer)
        self.go(1, source.at[1 - here.y, :, :, :, :, second], self.b1.at[:, :, :, :, b], here.y_peer)
        self.loads = [
            pltpu.make_async_copy(source.at[:, here.x, :, :, :, first], self.own.at[:, :, :, :, a], self.local.at[0]),
            pltpu.make_async_copy(source.at[here.y, :, :, :, :, second], self.own.at[:, :, :, :, b], self.local.at[1]),
        ]
        for load in self.loads:
            load.start()

        @pl.when(here.edge)
        def _():
            self.b3[2] = jnp.zeros(self.b3.shape[1:], self.b3.dtype)

    def stage_two(self):
        here = self.here
        for side, near, peer in ((0, here.y, here.y_peer), (1, here.x, here.x_peer)):
            lanes = self.sides[side]
            away = 1 - near
            self.loads[side].wait()
            self.copies[side].wait_recv()

            def add(c, z, away=away, lanes=lanes):
                total = self.own[away, c, z, :, lanes].astype(F32) + self.b1[away, c, z, :, lanes].astype(F32)
                self.own[away, c, z, :, lanes] = total.astype(self.own.dtype)

            self.blocks(add)
            self.go(2 + side, self.own.at[away, :, :, :, lanes], self.b2.at[:, :, :, lanes], peer)

    def stage_three(self):
        here = self.here
        for side, near in ((0, here.y), (1, here.x)):
            lanes = self.sides[side]
            self.copies[2 + side].wait_recv()

            def add(c, z, near=near, lanes=lanes):
                total = self.own[near, c, z, :, lanes].astype(F32) + self.b1[near, c, z, :, lanes].astype(F32)
                total = total + self.b2[c, z, :, lanes].astype(F32)
                self.b2[c, z, :, lanes] = total.astype(self.b2.dtype)

            self.blocks(add)
        piece = lambda j: self.b2.at[:, here.z_flip(j)]
        self.go(4, piece(1), self.b3.at[0], here.z_peer(1))
        pl.when(here.edge)(self.make(5, piece(2), self.b3.at[1], here.z_peer(2)).start)
        pl.when(here.inner)(self.make(6, piece(3), self.b3.at[2], here.z_peer(3)).start)
        pl.when(here.edge)(self.make(8, piece(3), self.met, here.z_peer(1)).start)

    def stage_meet(self):
        here = self.here

        @pl.when(here.inner)
        def _():
            self.copies[8].wait_recv()
            for c in range(self.b2.shape[0]):
                place = here.z_flip(2)
                total = self.b2[c, place].astype(F32) + self.met[c].astype(F32)
                self.b2[c, place] = total.astype(self.b2.dtype)
            self.copies[5].start()

    def total(self, c):
        total = self.b2[c, self.here.z].astype(F32)
        for j in range(3):
            total = total + self.b3[j, c].astype(F32)
        return total

    def stage_four(self):
        here = self.here
        self.copies[4].wait_recv()
        self.copies[5].wait_recv()
        pl.when(here.inner)(self.copies[6].wait_recv)
        if self.columns:
            self.b4s[...] = self.total(1 - here.c).astype(self.b4s.dtype)
            self.go(7, self.b4s, self.b4, here.core_peer)
            self.out[here.c, :, self.cut] = self.total(here.c)
        else:
            self.out[:, self.cut] = self.total(0)

    def finish(self):
        if self.columns:
            self.copies[7].wait_recv()
            self.out[1 - self.here.c, :, self.cut] = self.b4[...].astype(F32)
        for slot, copy in self.copies.items():
            if slot == 6:
                pl.when(self.here.inner)(copy.wait_send)
            elif slot == 8:
                pl.when(self.here.edge)(copy.wait_send)
            else:
                copy.wait_send()


class RowOut:
    def __init__(self, here, source, out, send, recv, local):
        self.here, self.source, self.out = here, source, out
        self.send, self.recv, self.local = send, recv, local
        self.half = source.shape[-1] // 2

    def parts(self):
        here = self.here
        lanes = pl.ds(pl.multiple_of(here.c * self.half, 128), self.half)
        for k in range(4):
            source = self.source.at[k, :, lanes]
            target = self.out.at[here.z % 2, :, lanes]
            self_sent = (here.z == k) & (here.z // 2 == here.c)
            peer = (here.at, here.z // 2, k)
            away = remote(source, target, self.send.at[k], self.recv.at[here.z % 2 * 2 + here.c], peer)
            yield self_sent, away, pltpu.make_async_copy(source, target, self.local)

    def begin(self):
        for self_sent, away, stay in self.parts():
            pl.when(self_sent)(stay.start)
            pl.when(jnp.logical_not(self_sent))(away.start)

    def finish(self):
        here = self.here
        for i in range(2):
            for f in range(2):
                target = self.out.at[i, :, pl.ds(f * self.half, self.half)]
                from_self = (2 * here.c + i == here.z) & (here.c == f)
                away = remote(target, target, self.send.at[0], self.recv.at[2 * i + f], here.core_peer)
                stay = pltpu.make_async_copy(target, target, self.local)
                pl.when(from_self)(stay.wait)
                pl.when(jnp.logical_not(from_self))(away.wait_recv)
        for self_sent, away, _ in self.parts():
            pl.when(jnp.logical_not(self_sent))(away.wait_send)


def sum_kernel(column_flags, cuts, rows_at, refs):
    here = Here()
    refs = list(refs)
    take = lambda n: [refs.pop(0) for _ in range(n)]
    grads, tensors = len(column_flags), len(rows_at)
    sources, row_sources = take(grads), take(tensors)
    outs, row_outs = take(grads), take(tensors)
    scratch = [[take(7 if columns else 5) for _ in range(cut)] for columns, cut in zip(column_flags, cuts)]
    send, recv, local, row_send, row_recv, row_local = refs
    items = []
    for k in range(grads):
        for cut in range(cuts[k]):
            n, start = len(items), cut * (sources[k].shape[-1] // cuts[k])
            items.append(
                SumItem(here, sources[k], outs[k], start, scratch[k][cut], send.at[n], recv.at[n], local.at[n])
            )
    count = len(items)
    rows = [
        RowOut(here, row_sources[t], row_outs[t], row_send.at[t], row_recv.at[t], row_local.at[t])
        for t in range(tensors)
    ]
    here.enter()
    for step in range(count + 5):
        if step < count:
            items[step].stage_one()
        if 0 <= step - 1 < count:
            items[step - 1].stage_two()
        if 0 <= step - 2 < count:
            items[step - 2].stage_three()
        if 0 <= step - 3 < count:
            items[step - 3].stage_meet()
        if 0 <= step - 4 < count:
            items[step - 4].stage_four()
        if 0 <= step - 5 < count:
            items[step - 5].finish()
        for t, start in enumerate(rows_at):
            if start == step:
                rows[t].begin()
    for row in rows:
        row.finish()


def sum_all(grads, rows, rows_at):
    flags = [grad.shape[2] == 2 for grad in grads]
    hbm = pl.BlockSpec(memory_space=pl.ANY)
    vmem = pl.BlockSpec(memory_space=pltpu.VMEM)
    shapes, scratch, cuts = [], [], []
    for grad, columns in zip(grads, flags):
        _, _, cores, places, r, n = grad.shape
        shapes.append(jax.ShapeDtypeStruct((2, r, n) if columns else (r, n), F32))
        cuts.append(2 if grad.size > 2**SUM_CUT else 1)
        n = n // cuts[-1]
        sizes = [(2, cores, places, r, n)] * 2 + [(cores, places, r, n), (3, cores, r, n), (cores, r, n)]
        sizes += [(r, n)] * 2 if columns else []
        scratch += [pltpu.VMEM(size, grad.dtype) for size in sizes] * cuts[-1]
    count, tensors = sum(cuts), len(rows)
    row_shapes = [jax.ShapeDtypeStruct((2,) + row.shape[1:], row.dtype) for row in rows]

    def kernel(*refs):
        sum_kernel(flags, cuts, rows_at, refs)

    dma = pltpu.SemaphoreType.DMA
    return pl.pallas_call(
        kernel,
        in_specs=[hbm] * (len(grads) + tensors),
        out_specs=[vmem] * len(grads) + [hbm] * tensors,
        out_shape=shapes + row_shapes,
        scratch_shapes=scratch
        + [
            dma((count, 9)),
            dma((count, 9)),
            dma((count, 2)),
            dma((tensors, 4)),
            dma((tensors, 4)),
            dma((tensors,)),
        ],
        compiler_params=pltpu.CompilerParams(
            collective_id=1, has_side_effects=True, vmem_limit_bytes=60 * 2**20
        ),
        name="sum_all",
    )(*grads, *rows)


class Place:
    def __init__(self):
        self.core = lax.axis_index("core")
        self.z = lax.axis_index("seq")

    def over_core(self, value):
        return lax.ppermute(value, "core", [(0, 1), (1, 0)])

    def both_cores(self, part):
        part = part.astype(B16)
        return part.astype(F32) + self.over_core(part).astype(F32)


class Tree:
    def __init__(self, place):
        self.place = place

    def gather(self, flat, columns, rows, tensors, tensors_at):
        core = self.place.core
        padded = jnp.pad(flat, (0, -flat.shape[0] % 4096)).reshape(16, -1)
        locals_ = {-1: (padded, padded)}
        for key, value in columns.items():
            locals_[key] = (lay_side(own_columns(value, core)), lay_side(own_columns(value, 1 - core)))
        for key, value in rows.items():
            locals_[key] = (value, None)
        keys = sorted(locals_)
        outs = gather_all([locals_[key] for key in keys], tensors, tensors_at)
        whole = {key: out for key, out in zip(keys, outs)}
        small = whole.pop(-1).reshape(32, -1)[:, : flat.shape[0]]
        weights = {key: value.reshape(-1, value.shape[-1]) for key, value in whole.items()}
        return small, weights, [out.reshape(-1, out.shape[-1]) for out in outs[len(keys) :]]

    def gather_late(self, columns, rows, after):
        core = self.place.core
        mine, other = lay_side(own_columns(columns, core)), lay_side(own_columns(columns, 1 - core))
        both = jnp.stack(xor_arrange([mine, self.place.over_core(other)], core))
        both, rows, _ = lax.optimization_barrier((both, rows, after))
        full = lax.all_gather(both, ("dp", "seq"), axis=0, tiled=False)
        full = full.reshape((4, 4) + both.shape).transpose(0, 2, 1, 3, 4)
        return full.reshape(-1, full.shape[-1]), lax.all_gather(rows, ("dp", "seq"), axis=0, tiled=True)

    def early_columns(self, pairs, parts):
        core = self.place.core
        value = lay_wide([product_tn(features, grad).astype(B16) for features, grad in pairs])
        value = value.reshape(4, 2, 4, -1, value.shape[1]).transpose(0, 2, 1, 3, 4)
        value = value.reshape(16, -1, value.shape[-1])
        total = lax.psum_scatter(value, ("dp", "seq"), scatter_dimension=0, tiled=True)
        total = total.reshape(2, -1, total.shape[-1])
        mine = lax.dynamic_index_in_dim(total, core, 0, keepdims=False)
        other = lax.dynamic_index_in_dim(total, 1 - core, 0, keepdims=False)
        both = jnp.stack(xor_arrange([mine, self.place.over_core(other)], core))
        return self.weave(both, parts)

    def early_both(self, pairs, parts, features, grad):
        core = self.place.core
        values = [product_tn(f, g).astype(B16) for f, g in pairs]
        width = values[0].shape[1]
        cut = [v[:, k : k + width] for v in values for k in range(0, v.shape[1], width)]
        cut = [v.reshape(4, 2, 4, -1, width).transpose(0, 2, 1, 3, 4).reshape(16, -1, width) for v in cut]
        rows = product_tn(features, grad).astype(B16)
        rows = rows.reshape(16, -1, rows.shape[1])
        r = rows.shape[1]
        cut += [rows[:, :, k : k + width] for k in range(0, rows.shape[2], width)]
        total = lax.psum_scatter(jnp.concatenate(cut, axis=1), ("dp", "seq"), scatter_dimension=0, tiled=True)[0]
        columns, rest = total[: 2 * r * parts].reshape(parts, 2, r, width), total[2 * r * parts :]
        mine = lax.dynamic_index_in_dim(columns, core, 1, keepdims=False)
        other = lax.dynamic_index_in_dim(columns, 1 - core, 1, keepdims=False)
        both = jnp.stack(xor_arrange([mine, self.place.over_core(other)], core))
        both = both.astype(F32).reshape(2, parts, r, 4, -1).transpose(1, 2, 3, 0, 4).reshape(parts, r, -1)
        return both, rest.astype(F32).reshape(-1, r, width).transpose(1, 0, 2).reshape(r, -1)

    def early_rows(self, features, grad):
        value = product_tn(features, grad).astype(B16)
        return lax.psum_scatter(value, ("dp", "seq"), scatter_dimension=0, tiled=True).astype(F32)

    def weave(self, both, parts):
        r = both.shape[1]
        both = both.astype(F32).reshape(2, r, parts, 4, -1)
        return both.transpose(2, 1, 3, 0, 4).reshape(parts, r, -1)

    def sums(self, columns, rows, table, hidden, tensors):
        n, m = table.shape[0], hidden.shape[0]
        both = jnp.concatenate(
            [
                table.reshape(n, 2, 2, 4, -1).transpose(1, 2, 3, 0, 4).reshape(2, 2, 4, -1),
                hidden.reshape(m, 2, 2, 4, -1).transpose(1, 2, 3, 0, 4).reshape(2, 2, 4, -1),
            ],
            axis=-1,
        )
        size = both.shape[-1]
        both = jnp.pad(both, ((0, 0), (0, 0), (0, 0), (0, -size % 2048))).reshape(2, 2, 1, 4, 8, -1)
        grads, keys = [], []
        for key, (features, grad, _) in columns.items():
            value = product_tn(features, grad).astype(B16)
            grads.append(value.reshape(2, 2, 2, 4, value.shape[0] // 32, value.shape[1]))
            keys.append(key)
        for key, (features, grad) in rows.items():
            value = product_tn(features, grad).astype(B16)
            grads.append(value.reshape(2, 2, 1, 4, value.shape[0] // 16, value.shape[1]))
            keys.append(key)
        order = sorted(range(len(keys)), key=lambda k: keys[k])
        outs = sum_all([grads[k] for k in order] + [both], [t.reshape(4, -1, t.shape[-1]) for t in tensors], SUM_ROWS)
        result = {}
        for k, out in zip(order, outs):
            key = keys[k]
            if key in columns:
                result[key] = self.weave(out, columns[key][2])
            else:
                result[key] = out
        flat = outs[len(keys)].reshape(-1)[:size]
        edge = table.shape[1] // 16 * n
        return result, flat[:edge].reshape(n, -1), flat[edge:].reshape(m, -1), outs[len(keys) + 1 :]


class Plain:
    def __init__(self, place):
        self.place = place
        self.axes = ("dp", "core", "seq")

    def row_in(self, array):
        place = self.place
        parts = array.reshape(2, array.shape[1], 2, -1)
        got = []
        for m in range(4):
            code = place.z ^ m
            piece = lax.dynamic_index_in_dim(parts, code // 2, 0, keepdims=False)
            piece = lax.dynamic_index_in_dim(piece, code % 2, 1, keepdims=False)
            moves = []
            for c in range(2):
                for z in range(4):
                    q = m ^ z
                    moves.append((c * 4 + z, q % 2 * 4 + 2 * c + q // 2))
            got.append(lax.ppermute(piece, ("core", "seq"), moves))
        half = jnp.concatenate(xor_arrange(got, (place.z % 2) * 2 + place.core), axis=0)
        return jnp.concatenate(xor_arrange([half, place.over_core(half)], place.core), axis=1)

    def row_out(self, row):
        place = self.place
        parts = row.reshape(4, -1, 2, row.shape[1] // 2)
        mine = lax.dynamic_index_in_dim(parts, place.core, 2, keepdims=False)
        q_here = (place.z % 2) * 2 + place.core
        got = []
        for m in range(4):
            piece = lax.dynamic_index_in_dim(mine, q_here ^ m, 0, keepdims=False)
            moves = []
            for c in range(2):
                for z in range(4):
                    q = (z % 2) * 2 + c
                    moves.append((c * 4 + z, z // 2 * 4 + (m ^ q)))
            got.append(lax.ppermute(piece, ("core", "seq"), moves))
        placed = xor_arrange(got, place.z)
        return jnp.stack([jnp.concatenate(placed[2 * i : 2 * i + 2], axis=1) for i in range(2)])

    def gather(self, flat, columns, rows, tensors, tensors_at):
        small = lax.all_gather(flat, self.axes, axis=0, tiled=False)
        weights = {}
        for key, value in columns.items():
            weights[key] = self.whole_columns(value)
        for key, value in rows.items():
            weights[key] = self.whole_rows(value)
        return small, weights, [self.row_in(tensor) for tensor in tensors]

    def whole_columns(self, value):
        full = lax.all_gather(value, self.axes, axis=1, tiled=True)
        return lay_side(own_columns(full, self.place.core))

    def whole_rows(self, value):
        full = lax.all_gather(value, self.axes, axis=0, tiled=True)
        split = full.reshape(4, 2, full.shape[0] // 8, full.shape[1])
        mine = lax.dynamic_index_in_dim(split, self.place.core, 1, keepdims=False)
        return mine.reshape(-1, full.shape[1])

    def gather_late(self, columns, rows, after):
        return self.whole_columns(columns), self.whole_rows(rows)

    def early_columns(self, pairs, parts):
        full = lay_wide([product_tn(features, grad) for features, grad in pairs])
        full = full.reshape(full.shape[0], parts, -1).transpose(1, 0, 2).astype(B16)
        return self.scatter(self.spread(full, 2), 1)

    def early_both(self, pairs, parts, features, grad):
        return self.early_columns(pairs, parts), self.early_rows(features, grad)

    def early_rows(self, features, grad):
        return self.scatter(self.spread(product_tn(features, grad).astype(B16), 0), 0)

    def spread(self, half, axis):
        shape = half.shape[:axis] + (4, 1, half.shape[axis] // 4) + half.shape[axis + 1 :]
        half = half.reshape(shape)
        empty = jnp.zeros_like(half)
        first = jnp.where(self.place.core == 0, half, empty)
        second = jnp.where(self.place.core == 1, half, empty)
        both = jnp.concatenate([first, second], axis=axis + 1)
        return both.reshape(shape[:axis] + (-1,) + shape[axis + 3 :])

    def scatter(self, value, axis):
        return lax.psum_scatter(value, self.axes, scatter_dimension=axis, tiled=True).astype(F32)

    def sums(self, columns, rows, table, hidden, tensors):
        result = {}
        for key, (features, grad, parts) in columns.items():
            result[key] = self.early_columns([(features, grad)], parts)
        for key, (features, grad) in rows.items():
            result[key] = self.early_rows(features, grad)
        small = [self.scatter(self.spread(v, 1), 1) for v in (table, hidden)]
        return result, small[0], small[1], [self.row_out(tensor) for tensor in tensors]


def on_device(
    dp,
    seq,
    src_x,
    tgt_x,
    src_seg,
    tgt_seg,
    tgt_len,
    src_lang,
    tgt_lang,
    lang_table,
    gains,
    biases,
    ff_biases,
    enc_proj,
    enc_oproj,
    enc_in,
    enc_out,
    dec_proj,
    dec_oproj,
    dec_in,
    dec_out,
    src_cot,
    tgt_cot,
):
    place = Place()
    core = place.core
    moves = Tree(place) if (dp, seq) == (4, 4) else Plain(place)
    width = enc_oproj.shape[1]
    half = width // 2
    langs = lang_table.shape[0]

    n_small = langs + gains.shape[0] + biases.shape[0]
    table = jnp.concatenate([lang_table, gains, biases], axis=0)
    flat = jnp.concatenate([table.reshape(-1), ff_biases.reshape(-1)])
    edge = table.size
    everything, weights, tensors = moves.gather(
        flat,
        {0: enc_proj, 2: enc_in[None], 4: dec_proj[0:3], 6: dec_proj[3:6]},
        {1: enc_oproj, 3: enc_out, 5: dec_oproj[0], 7: dec_oproj[1]},
        [src_x, tgt_x, tgt_cot, src_cot],
        [2, 5, 8, 11],
    )
    source, target, target_cot, source_cot = tensors
    enc_qkv_w, enc_o_w, enc_in_w, enc_out_w, dec_qkv_w, dec_o_w, cross_w, cross_o_w = (
        weights[k] for k in range(8)
    )
    dec_in_w, dec_out_w = moves.gather_late(dec_in[None], dec_out, everything)
    table = everything[:, :edge].reshape(2 * dp * seq, n_small, -1).transpose(1, 0, 2).reshape(n_small, width)
    ffb = everything[:, edge:].reshape(2 * dp * seq, 2, -1).transpose(1, 0, 2).reshape(2, -1)
    languages = table[:langs]
    gain_f = table[langs : langs + gains.shape[0]].astype(F32)
    bias_f = table[langs + gains.shape[0] :].astype(F32)
    ffb_own = own_columns(ffb.astype(F32), core)
    bias_own = own_columns(bias_f, core)

    meta = jnp.concatenate([src_seg, tgt_seg, tgt_len[:, None], src_lang, tgt_lang], axis=1)
    rows = jnp.where(place.z // 2 == core, meta, place.over_core(meta))
    row = lax.dynamic_index_in_dim(rows, place.z % 2, 0, keepdims=False)
    count, segs = src_seg.shape[1], src_lang.shape[1]
    s_seg, t_seg, t_len = row[:count], row[count : 2 * count], row[2 * count]
    s_lang, t_lang = row[2 * count + 1 : 2 * count + 1 + segs], row[2 * count + 1 + segs :]

    def onehot(segments, chosen):
        member = segments[:, None] == jnp.arange(segs, dtype=jnp.int32)[None, :]
        token = jnp.sum(jnp.where(member, chosen[None, :], 0), axis=1)
        return (token[:, None] == jnp.arange(langs, dtype=jnp.int32)[None, :]).astype(B16)

    src_hot, tgt_hot = onehot(s_seg, s_lang), onehot(t_seg, t_lang)
    enc_masks = (block_info(False, s_seg, s_seg, t_len), s_seg[None, :], s_seg[:, None])
    dec_masks = (block_info(True, t_seg, t_seg, t_len), t_seg[None, :], t_seg[:, None])
    cross_masks = (block_info(False, t_seg, s_seg, t_len), t_seg[None, :], s_seg[:, None])

    none = jnp.zeros((half,), F32)
    packed = (0, half // GROUP, 2 * half // GROUP)

    enc_h0 = source.astype(F32) + product(src_hot, languages)
    enc_n1 = layer_norm(enc_h0, gain_f[0], bias_f[0])
    enc_qkv_bias = jnp.concatenate([bias_own[1], none, bias_own[2]])
    enc_qkv = (product(enc_n1, enc_qkv_w) + enc_qkv_bias).astype(B16)
    enc_mixed, enc_lse = attend_forward(False, enc_masks, enc_qkv, enc_qkv, enc_qkv, packed, half)
    enc_h1 = enc_h0 + place.both_cores(product(enc_mixed, enc_o_w)) + bias_f[3]
    enc_n2 = layer_norm(enc_h1, gain_f[1], bias_f[4])
    enc_acted, enc_slope = gelu_both(product(enc_n2, enc_in_w) + ffb_own[0])
    encoded = enc_h1 + place.both_cores(product(enc_acted, enc_out_w)) + bias_f[5]
    memory = encoded.astype(B16)

    dec_h0 = target.astype(F32) + product(tgt_hot, languages)
    dec_n1 = layer_norm(dec_h0, gain_f[2], bias_f[6])
    dec_qkv_bias = jnp.concatenate([bias_own[7], none, bias_own[8]])
    dec_qkv = (product(dec_n1, dec_qkv_w) + dec_qkv_bias).astype(B16)
    dec_mixed, dec_lse = attend_forward(True, dec_masks, dec_qkv, dec_qkv, dec_qkv, packed, half)
    dec_h1 = dec_h0 + place.both_cores(product(dec_mixed, dec_o_w)) + bias_f[9]
    dec_n2 = layer_norm(dec_h1, gain_f[3], bias_f[10])
    cross_q = (product(dec_n2, cross_w[:, :half]) + bias_own[11]).astype(B16)
    cross_kv_bias = jnp.concatenate([none, bias_own[12]])
    cross_kv = (product(memory, cross_w[:, half:]) + cross_kv_bias).astype(B16)
    apart = (0, 0, half // GROUP)
    cross_mixed, cross_lse = attend_forward(False, cross_masks, cross_q, cross_kv, cross_kv, apart, half)
    dec_h2 = dec_h1 + place.both_cores(product(cross_mixed, cross_o_w)) + bias_f[13]
    dec_n3 = layer_norm(dec_h2, gain_f[4], bias_f[14])
    dec_acted, dec_slope = gelu_both(product(dec_n3, dec_in_w) + ffb_own[1])
    decoded = dec_h2 + place.both_cores(product(dec_acted, dec_out_w)) + bias_f[15]

    dec_du = (product_nt(target_cot, dec_out_w) * dec_slope.astype(F32)).astype(B16)
    dec_dn3 = place.both_cores(product_nt(dec_du, dec_in_w))
    dec_in_grad = moves.early_columns([(dec_n3, dec_du)], 1)
    dec_out_grad = moves.early_rows(dec_acted, target_cot)
    target_cot_f = target_cot.astype(F32)
    step, gain_four, shift_14 = norm_backward(dec_h2, gain_f[4], dec_dn3)
    grad_h2 = target_cot_f + step

    cross_branch = grad_h2.astype(B16)
    cross_do = product_nt(cross_branch, cross_o_w).astype(B16)
    cross_dq, cross_dkv = attend_backward(
        False, cross_masks, cross_q, cross_kv, cross_kv, apart, half, cross_mixed, cross_lse, cross_do
    )
    grad_memory = place.both_cores(product_nt(cross_dkv, cross_w[:, half:]))
    dec_dn2 = place.both_cores(product_nt(cross_dq, cross_w[:, :half]))

    cross_grad, cross_o_grad = moves.early_both(
        [(dec_n2, cross_dq), (memory, cross_dkv)], 3, cross_mixed, cross_branch
    )

    source_cot_f = source_cot.astype(F32) + grad_memory
    enc_ff_branch = source_cot_f.astype(B16)
    enc_du = (product_nt(enc_ff_branch, enc_out_w) * enc_slope.astype(F32)).astype(B16)
    enc_dn2 = place.both_cores(product_nt(enc_du, enc_in_w))

    step, gain_three, shift_10 = norm_backward(dec_h1, gain_f[3], dec_dn2)
    grad_h1 = grad_h2 + step
    self_branch = grad_h1.astype(B16)
    dec_do = product_nt(self_branch, dec_o_w).astype(B16)
    (dec_dqkv,) = attend_backward(
        True, dec_masks, dec_qkv, dec_qkv, dec_qkv, packed, half, dec_mixed, dec_lse, dec_do
    )
    dec_dn1 = place.both_cores(product_nt(dec_dqkv, dec_qkv_w))
    step, gain_two, shift_6 = norm_backward(dec_h0, gain_f[2], dec_dn1)
    target_grad = grad_h1 + step

    step, gain_one, shift_4 = norm_backward(enc_h1, gain_f[1], enc_dn2)
    grad_e1 = source_cot_f + step
    enc_branch = grad_e1.astype(B16)
    enc_do = product_nt(enc_branch, enc_o_w).astype(B16)
    (enc_dqkv,) = attend_backward(
        False, enc_masks, enc_qkv, enc_qkv, enc_qkv, packed, half, enc_mixed, enc_lse, enc_do
    )
    enc_dn1 = place.both_cores(product_nt(enc_dqkv, enc_qkv_w))
    step, gain_zero, shift_0 = norm_backward(enc_h0, gain_f[0], enc_dn1)
    source_grad = grad_e1 + step

    source_high, target_high = source_grad.astype(B16), target_grad.astype(B16)
    lang_grad = 0.0
    for hot, value, high in ((src_hot, source_grad, source_high), (tgt_hot, target_grad, target_high)):
        low = (value - high.astype(F32)).astype(B16)
        lang_grad = lang_grad + product_tn(hot, high) + product_tn(hot, low)
    own = functools.partial(own_columns, core=core)
    gain_rows = jnp.stack([gain_zero, gain_one, gain_two, gain_three, gain_four])
    enc_qkv_sum, dec_qkv_sum = column_sum(enc_dqkv), column_sum(dec_dqkv)
    bias_rows = jnp.stack(
        [
            own(shift_0),
            enc_qkv_sum[:half],
            enc_qkv_sum[2 * half :],
            own(column_sum(enc_branch)),
            own(shift_4),
            own(column_sum(enc_ff_branch)),
            own(shift_6),
            dec_qkv_sum[:half],
            dec_qkv_sum[2 * half :],
            own(column_sum(self_branch)),
            own(shift_10),
            column_sum(cross_dq),
            column_sum(cross_dkv[:, half:]),
            own(column_sum(cross_branch)),
            own(shift_14),
            own(column_sum(target_cot)),
        ]
    )
    grads, small, ffb_grad, outputs = moves.sums(
        {
            1: (dec_n1, dec_dqkv, 3),
            2: (enc_n2, enc_du, 1),
            4: (enc_n1, enc_dqkv, 3),
        },
        {
            0: (dec_mixed, self_branch),
            3: (enc_acted, enc_ff_branch),
            5: (enc_mixed, enc_branch),
        },
        jnp.concatenate([own(lang_grad), own(gain_rows), bias_rows], axis=0),
        jnp.stack([column_sum(enc_du), column_sum(dec_du)]),
        [memory, decoded.astype(B16), source_high, target_high],
    )
    return (
        outputs[0],
        outputs[1],
        outputs[2].astype(F32),
        outputs[3].astype(F32),
        small[:langs],
        small[langs : langs + 5],
        small[langs + 5 :],
        ffb_grad,
        grads[4],
        grads[5],
        grads[2][0],
        grads[3],
        jnp.concatenate([grads[1], cross_grad], axis=0),
        jnp.stack([grads[0], cross_o_grad]),
        dec_in_grad[0],
        dec_out_grad,
    )


def solution(mesh):
    dp, seq = mesh.shape["dp"] // 2, mesh.shape["seq"]
    pairs = Mesh(mesh.devices.reshape(dp, 2, seq), ("dp", "core", "seq"))
    both, every = ("dp", "core"), ("dp", "core", "seq")
    rows = P(both, "seq", None)
    columns = P(None, every)
    middle = P(None, every, None)
    first = P(every, None)
    weights = (columns, columns, columns, columns, middle, first, first, first, middle, middle, first, first)
    return jax.shard_map(
        functools.partial(on_device, dp, seq),
        mesh=pairs,
        in_specs=(rows, rows, P(both, None), P(both, None), P(both), P(both, None), P(both, None))
        + weights
        + (rows, rows),
        out_specs=(rows, rows, rows, rows) + weights,
        check_vma=False,
    )
```

time: 1220 us -> 1020 us (0.84)
  Pallas kernels: 818 us -> 571 us
  waiting for transfers between devices: 2.56 us -> 29.3 us
  other arithmetic: 77.8 us -> 91.9 us
  between operations: 3.18 us -> 16.8 us
  local copies, waits for them, and re-layouts: 130 us -> 117 us
    pallas_call x1, Pallas kernels: 337 us -> 196 us  [sum_all(): pl.pallas_call(kernel, in_specs=[hbm] * (len(grads) + tensors), out_specs...]
    pallas_call x1, Pallas kernels: 337 us -> 239 us  [gather_all(): pl.pallas_call(kernel, in_specs=[hbm] * len(inputs), out_specs=[hbm] * le...]
    all_gather x0 -> x2, waiting for transfers between devices: none -> 24.9 us  [the longest x1 24.9 us: gather_late(): lax.all_gather(rows, ('dp', 'seq'), axis=0, tiled=True)]
    dynamic_slice x15 -> x13, local copies, waits for them, and re-layouts: 21.9 us -> 5.1 us  [own_columns(): mine = lax.dynamic_index_in_dim(split, core, split.ndim - 2, keepdims=False)]
    pallas_call x3, Pallas kernels: 57.9 us -> 41.2 us  [attend_forward(): pl.pallas_call(functools.partial(forward_kernel, causal), grid_spec=pltpu...]
    unnamed x301 -> x314, local copies, waits for them, and re-layouts: 34.1 us -> 43.3 us
  transfers between devices with their start and end apart: 12 -> 20, of which waited for: 1 -> 3; matrix products, arithmetic and copies ran while one was open for 17% -> 32% of each run, Pallas kernels for 34% -> 57%
where the time goes in v3:
time: 1020 us; the launch traced here: 1000 us
  Pallas kernels  571 us (56%)
  matrix products  170 us (17%)
  local copies, waits for them, and re-layouts  117 us (11%)
  other arithmetic  91.9 us (9%)
  waiting for transfers between devices  29.3 us (3%)
  between operations  16.8 us (2%)
    pallas_call x1, Pallas kernels, gather_all(): pl.pallas_call(kernel, in_specs=[hbm] * len(inputs), out_specs=[hbm] * le...  239 us
    pallas_call x1, Pallas kernels, sum_all(): pl.pallas_call(kernel, in_specs=[hbm] * (len(grads) + tensors), out_specs...  196 us
    pallas_call x3, Pallas kernels, attend_backward(): pl.pallas_call(functools.partial(backward_kernel, causal), grid_spec=pltp...  95.4 us
    dot_general x15, matrix products, product_tn(): lax.dot_general(left, right, (((0,), (0,)), ((), ())), preferred_element_...  59.3 us
    dot_general x13, matrix products, product(): return jnp.dot(left, right, preferred_element_type=F32)  56.8 us
    dot_general x11, matrix products, product_nt(): lax.dot_general(left, right, (((1,), (1,)), ((), ())), preferred_element_...  54.4 us
    unnamed x314, local copies, waits for them, and re-layouts  43.3 us
    pallas_call x3, Pallas kernels, attend_forward(): pl.pallas_call(functools.partial(forward_kernel, causal), grid_spec=pltpu...  41.2 us
  transfers between devices with their start and end apart: 20, of which 3 were waited for; matrix products, arithmetic and copies ran while one was open for 32% of the time, Pallas kernels for 57%

profile of v3, /device:TPU:0, one launch (start us, length us, event | category | flops | bytes accessed | tf_op | source)
XLA Modules:
  0.0 1000.2 jit_solution(8241411791371151865)
XLA Ops:
  29.2 238.6 %gather_all.1 = (bf16[2,2,2,4,16,256]{5,4,3,2,1,0:T(8,128)(2,1)}, bf16[2,2,2,4,32,1536]{5,4,3,2,1,0:T(8,128)(2,1)}, bf16[2,2,1,4,32,1024]{5,4,3,2,1,0:T(8,128)(2...) custom-call(bf16[16,256]{1,0:T(8,128)(2,1)} %reshape.663.refs_0_.ref, ...), custom_call_target="tpu_custom_call" | custom-call | tf_op jit(solution)/shard_map/gather_all/pallas_call | solution.py:537
  287.8 8.4 add_convert_fusion.q_ref.k_ref.v_ref
  300.1 13.5 %attend.2 = (bf16[1024,512]{1,0:T(8,128)(2,1)S(1)}, f32[2,8,1024]{2,1,0:T(8,128)S(1)}) custom-call(s32[17]{0:T(128)S(1)} %get-tuple-element.306.info_ref, bf16[1024,1536]{1,0:T(8,128)(2,1)S(1)} %copy-done.17, bf16[1024,1536]{1,0:T(8,128)(2,1)S(1)} %copy-done.17, bf16[1024,1536]{1,0:T(8,128)(2,1)S(1)} %copy-done.17, ...), custom_call_target="tpu_custom_call" | custom-call | flops 4294967296 | bytes 4194304 | tf_op jit(solution)/shard_map/attend/pallas_call | solution.py:248
  319.2 6.9 add_convert_fusion.1.q_ref.k_ref.v_ref
  326.1 13.9 %attend_causal.1 = (bf16[1024,512]{1,0:T(8,128)(2,1)S(1)}, f32[2,8,1024]{2,1,0:T(8,128)S(1)}) custom-call(s32[17]{0:T(128)S(1)} %get-tuple-element.305.info_ref, bf16[1024,1536]{1,0:T(8,128)(2,1)S(1)} %add_convert_fusion.1.q_ref.k_ref.v_ref, bf16[1024,1536]{1,0:T(8,128)(2,1)S(1)} %add_convert_fusion.1.q_ref.k_ref.v_ref, ...), custom_call_target="tpu_custom_call" | custom-call | flops 4294967296 | bytes 4194304 | tf_op jit(solution)/shard_map/attend_causal/pallas_call | solution.py:248
  350.3 8.0 multiply_convert_fusion.3
  380.4 13.8 %attend.3 = (bf16[1024,512]{1,0:T(8,128)(2,1)S(1)}, f32[2,8,1024]{2,1,0:T(8,128)S(1)}) custom-call(s32[17]{0:T(128)S(1)} %pad_add_fusion.1.info_ref, bf16[1024,512]{1,0:T(8,128)(2,1)S(1)} %add_convert_fusion.10.q_ref, bf16[1024,1024]{1,0:T(8,128)(2,1)S(1)} %add_convert_fusion.4.k_ref.v_ref, bf16[1024,1024]{1,0:T(8,128)(2,1)S(1)} %add_convert_fusion.4.k_ref.v_ref, ...), custom_call_target="tpu_custom_call" | custom-call | flops 4294967296 | bytes 4194304 | tf_op jit(solution)/shard_map/attend/pallas_call | solution.py:248
  411.0 8.3 multiply_convert_fusion
  419.3 24.9 %all-gather.4.cloned.1.call-done = bf16[2048,1024]{1,0:T(8,128)(2,1)} async-done(((bf16[128,1024]{1,0:T(8,128)(2,1)}), bf16[2048,1024]{1,0:T(8,128)(2,1)}) %all-gather.4.cloned.1.call-update) | async-done | bytes 4194320 | tf_op jit(solution)/shard_map/all_gather | solution.py:836
  444.2 10.2 %convert_reduce_fusion = (f32[2048]{0:T(1024)S(1)}, bf16[1024,2048]{1,0:T(8,128)(2,1)S(1)}) fusion(f32[1024,2048]{1,0:T(8,128)} %get-tuple-element.298, f32[2048]{0:T(1024)S(1)} %bitcast.379, bf16[1024,1024]{1,0:T(8,128)(2,1)S(1)} %bitcast.276, bf16[2048,1024]{1,0:T(8,128)(2,1)} %all-gather.4.cloned.1.call-done), kind=kOutput, calls=%fused_computation.13 | convolution fusion | flops 4326422528 | bytes 18890752 | tf_op jit(solution)/shard_map/dot_general | solution.py:30
  454.5 5.8 convolution_convert_fusion.3
  462.7 8.1 convolution_convert_fusion.13
  470.9 6.2 convolution_convert_fusion.2
  477.2 9.3 convolution_convert_fusion.7
  495.5 5.8 convert_reduce_fusion.5
  505.1 31.9 %attend_grad.2 = (bf16[1024,512]{1,0:T(8,128)(2,1)S(1)}, bf16[1024,1024]{1,0:T(8,128)(2,1)S(1)}) custom-call(s32[17]{0:T(128)S(1)} %pad_add_fusion.1.info_ref, bf16[1024,512]{1,0:T(8,128)(2,1)S(1)} %copy-done.22, bf16[1024,1024]{1,0:T(8,128)(2,1)S(1)} %copy-done.24, bf16[1024,1024]{1,0:T(8,128)(2,1)S(1)} %copy-done.24, bf16[1024,512]{1,0:T(8,128)(2,1)S(1)} %copy-done.16, ...), custom_call_target="tpu_custom_call" | custom-call | flops 10737418240 | bytes 8388608 | tf_op jit(solution)/shard_map/attend_grad/pallas_call | solution.py:276
  580.8 32.1 %attend_grad_causal.1 = bf16[1024,1536]{1,0:T(8,128)(2,1)S(1)} custom-call(s32[17]{0:T(128)S(1)} %copy-done.9, bf16[1024,1536]{1,0:T(8,128)(2,1)S(1)} %copy-done.20, bf16[1024,1536]{1,0:T(8,128)(2,1)S(1)} %copy-done.20, bf16[1024,1536]{1,0:T(8,128)(2,1)S(1)} %copy-done.20, bf16[1024,512]{1,0:T(8,128)(2,1)S(1)} %copy-done.14, ...), custom_call_target="tpu_custom_call" | custom-call | flops 10737418240 | bytes 8388608 | tf_op jit(solution)/shard_map/attend_grad_causal/pallas_call | solution.py:276
  630.0 8.9 convert_reduce_fusion.1
  638.9 7.0 convolution_convert_fusion.10
  651.3 9.5 convolution_convert_fusion.4
  660.9 6.9 convolution_convert_fusion.5
  680.3 31.3 %attend_grad.3 = bf16[1024,1536]{1,0:T(8,128)(2,1)S(1)} custom-call(s32[17]{0:T(128)S(1)} %copy-done.7, bf16[1024,1536]{1,0:T(8,128)(2,1)S(1)} %copy-done.18, bf16[1024,1536]{1,0:T(8,128)(2,1)S(1)} %copy-done.18, bf16[1024,1536]{1,0:T(8,128)(2,1)S(1)} %copy-done.18, bf16[1024,512]{1,0:T(8,128)(2,1)S(1)} %copy-done.11, ...), custom_call_target="tpu_custom_call" | custom-call | flops 10737418240 | bytes 8388608 | tf_op jit(solution)/shard_map/attend_grad/pallas_call | solution.py:276
  751.5 5.7 fusion.67
  768.7 196.3 %sum_all.1 = (f32[32,1024]{1,0:T(8,128)}, f32[2,32,1536]{2,1,0:T(8,128)}, f32[2,32,2048]{2,1,0:T(8,128)}, f32[128,1024]{1,0:T(8,128)}, f32[2,32,1536]{2,1,0:T(8,...) custom-call(bf16[2,2,1,4,32,1024]{5,4,3,2,1,0:T(8,128)(2,1)} %bitcas, ...), custom_call_target="tpu_custom_call" | custom-call | tf_op jit(solution)/shard_map/sum_all/pallas_call | solution.py:776
  (593 shorter events, 271.9 us)
Async XLA Ops:
  7.2 399.2 %all-gather.6.cloned.1.call-start = ((), (), s32[]{:S(2)}) async-start(), calls=%async_computation.7 | async-start | bytes 4456448 | tf_op jit(solution)/shard_map/all_gather | solution.py:834
  9.5 271.7 %collective-permute-start = (s32[2,2057]{1,0:T(2,128)}, s32[2,2057]{1,0:T(2,128)}, u32[]{:S(2)}, u32[]{:S(2)}) collective-permute-start(s32[2,2057]{1,0:T(2,128)} %concatenate.104), channel_id=1, source_target_pairs={{0,4},{4,0},{1,5},{5,1},{2,6},{6,2},{3,7},{7,3},{8,12},{12,8},{9,1... | collective-permute-start | bytes 49376 | tf_op jit(solution)/shard_map/ppermute | solution.py:803
  16.8 269.2 %collective-permute-start.5 = (bf16[32,2048]{1,0:T(8,128)(2,1)}, bf16[32,2048]{1,0:T(8,128)(2,1)}, u32[]{:S(2)}, u32[]{:S(2)}) collective-permute-start(bf16[32,2048]{1,0:T(8,128)(2,1)} %bitcast.151), channel_id=1, source_target_pairs={{0,4},{4,0},{1,5},{5,1},{2,6},{6,2},{3,7},{7,3},{8,12},{12,8},{9,1... | collective-permute-start | bytes 393224 | tf_op jit(solution)/shard_map/ppermute | solution.py:803
  276.8 70.3 %copy-start.112 = (f32[1024]{0:T(1024)}, f32[1024]{0:T(1024)S(1)}, u32[]{:S(2)}) copy-start(f32[1024]{0:T(1024)S(1)} %add.391) | copy-start | bytes 12292
  276.9 70.3 %copy-start.96 = (f32[1024]{0:T(1024)}, f32[1024]{0:T(1024)S(1)}, u32[]{:S(2)}) copy-start(f32[1024]{0:T(1024)S(1)} %mul.329) | copy-start | bytes 12292
  278.5 40.6 %copy-start.114 = (f32[1024]{0:T(1024)}, f32[1024]{0:T(1024)S(1)}, u32[]{:S(2)}) copy-start(f32[1024]{0:T(1024)S(1)} %add.361) | copy-start | bytes 12292
  287.7 156.5 %all-gather.4.cloned.1.call-start = ((), (), s32[]{:S(2)}) async-start(), calls=%async_computation.3 | async-start | bytes 4456448 | tf_op jit(solution)/shard_map/all_gather | solution.py:836
  297.5 205.2 %copy-start = (s32[1024,1]{1,0:T(8,128)}, s32[1024,1]{1,0:T(8,128)S(1)}, u32[]{:S(2)}) copy-start(s32[1024,1]{1,0:T(8,128)S(1)} %copy.263.kseg_ref) | copy-start | bytes 12292
  314.9 27.8 %collective-permute-start.2 = (bf16[1024,1024]{1,0:T(8,128)(2,1)S(1)}, bf16[1024,1024]{1,0:T(8,128)(2,1)}, u32[]{:S(2)}, u32[]{:S(2)}) collective-permute-start(bf16[1024,1024]{1,0:T(8,128)(2,1)S(1)} %convolution_convert_fusion.16), channel_id=1, source_target_pairs={{0,4},{4,0},{1,5},{5,1},{2,6},{6,2},{3,7},{7,3},{8,12},{12,8},{9,1... | collective-permute-start | bytes 6291464 | tf_op jit(solution)/shard_map/ppermute | solution.py:803
  342.6 21.8 %collective-permute-start.1 = (bf16[1024,1024]{1,0:T(8,128)(2,1)}, bf16[1024,1024]{1,0:T(8,128)(2,1)}, u32[]{:S(2)}, u32[]{:S(2)}) collective-permute-start(bf16[1024,1024]{1,0:T(8,128)(2,1)} %convolution_convert_fusion.17), channel_id=1, source_target_pairs={{0,4},{4,0},{1,5},{5,1},{2,6},{6,2},{3,7},{7,3},{8,12},{12,8},{9,1... | collective-permute-start | bytes 6291464 | tf_op jit(solution)/shard_map/ppermute | solution.py:803
  363.0 11.1 %collective-permute-start.3 = (bf16[1024,1024]{1,0:T(8,128)(2,1)S(1)}, bf16[1024,1024]{1,0:T(8,128)(2,1)}, u32[]{:S(2)}, u32[]{:S(2)}) collective-permute-start(bf16[1024,1024]{1,0:T(8,128)(2,1)S(1)} %convolution_convert_fusion.15), channel_id=1, source_target_pairs={{0,4},{4,0},{1,5},{5,1},{2,6},{6,2},{3,7},{7,3},{8,12},{12,8},{9,1... | collective-permute-start | bytes 6291464 | tf_op jit(solution)/shard_map/ppermute | solution.py:803
  364.3 602.7 %reduce-scatter.6.cloned.1.call-start = ((), (), s32[]{:S(2)}) async-start(), calls=%async_computation.5 | async-start | bytes 4456448 | tf_op jit(solution)/shard_map/reduce_scatter | solution.py:843
  395.5 4.4 collective-permute-start.4
  462.6 516.6 %reduce-scatter.8.cloned.1.call-start = ((), (), s32[]{:S(2)}) async-start(), calls=%async_computation.6 | async-start | bytes 4456448 | tf_op jit(solution)/shard_map/reduce_scatter | solution.py:870
  470.8 19.2 %collective-permute-start.6 = (bf16[1024,1024]{1,0:T(8,128)(2,1)S(1)}, bf16[1024,1024]{1,0:T(8,128)(2,1)}, u32[]{:S(2)}, u32[]{:S(2)}) collective-permute-start(bf16[1024,1024]{1,0:T(8,128)(2,1)S(1)} %convolution_convert_fusion.13), channel_id=1, source_target_pairs={{0,4},{4,0},{1,5},{5,1},{2,6},{6,2},{3,7},{7,3},{8,12},{12,8},{9,1... | collective-permute-start | bytes 6291464 | tf_op jit(solution)/shard_map/ppermute | solution.py:803
  477.1 507.4 %reduce-scatter.4.cloned.1.call-start = ((), (), s32[]{:S(2)}) async-start(), calls=%async_computation.4 | async-start | bytes 4456448 | tf_op jit(solution)/shard_map/reduce_scatter | solution.py:860
  486.5 9.0 collective-permute-start.12
  548.0 19.0 %collective-permute-start.7 = (bf16[1024,1024]{1,0:T(8,128)(2,1)}, bf16[1024,1024]{1,0:T(8,128)(2,1)}, u32[]{:S(2)}, u32[]{:S(2)}) collective-permute-start(bf16[1024,1024]{1,0:T(8,128)(2,1)} %convolution_convert_fusion.12), channel_id=1, source_target_pairs={{0,4},{4,0},{1,5},{5,1},{2,6},{6,2},{3,7},{7,3},{8,12},{12,8},{9,1... | collective-permute-start | bytes 6291464 | tf_op jit(solution)/shard_map/ppermute | solution.py:803
  551.8 74.2 %collective-permute-start.8 = (bf16[1024,1024]{1,0:T(8,128)(2,1)}, bf16[1024,1024]{1,0:T(8,128)(2,1)}, u32[]{:S(2)}, u32[]{:S(2)}) collective-permute-start(bf16[1024,1024]{1,0:T(8,128)(2,1)} %convolution_convert_fusion.11), channel_id=1, source_target_pairs={{0,4},{4,0},{1,5},{5,1},{2,6},{6,2},{3,7},{7,3},{8,12},{12,8},{9,1... | collective-permute-start | bytes 6291464 | tf_op jit(solution)/shard_map/ppermute | solution.py:803
  645.9 21.8 %collective-permute-start.9 = (bf16[1024,1024]{1,0:T(8,128)(2,1)S(1)}, bf16[1024,1024]{1,0:T(8,128)(2,1)}, u32[]{:S(2)}, u32[]{:S(2)}) collective-permute-start(bf16[1024,1024]{1,0:T(8,128)(2,1)S(1)} %convolution_convert_fusion.10), channel_id=1, source_target_pairs={{0,4},{4,0},{1,5},{5,1},{2,6},{6,2},{3,7},{7,3},{8,12},{12,8},{9,1... | collective-permute-start | bytes 6291464 | tf_op jit(solution)/shard_map/ppermute | solution.py:803
  646.0 70.9 %collective-permute-start.11 = (bf16[1024,1024]{1,0:T(8,128)(2,1)}, bf16[1024,1024]{1,0:T(8,128)(2,1)}, u32[]{:S(2)}, u32[]{:S(2)}) collective-permute-start(bf16[1024,1024]{1,0:T(8,128)(2,1)} %convolution_convert_fusion.8), channel_id=1, source_target_pairs={{0,4},{4,0},{1,5},{5,1},{2,6},{6,2},{3,7},{7,3},{8,12},{12,8},{9,1... | collective-permute-start | bytes 6291464 | tf_op jit(solution)/shard_map/ppermute | solution.py:803
  716.8 29.6 %collective-permute-start.10 = (bf16[1024,1024]{1,0:T(8,128)(2,1)}, bf16[1024,1024]{1,0:T(8,128)(2,1)}, u32[]{:S(2)}, u32[]{:S(2)}) collective-permute-start(bf16[1024,1024]{1,0:T(8,128)(2,1)} %convolution_convert_fusion.9), channel_id=1, source_target_pairs={{0,4},{4,0},{1,5},{5,1},{2,6},{6,2},{3,7},{7,3},{8,12},{12,8},{9,1... | collective-permute-start | bytes 6291464 | tf_op jit(solution)/shard_map/ppermute | solution.py:803
  968.7 12.9 %collective-permute-start.14 = (bf16[32,2048]{1,0:T(8,128)(2,1)}, bf16[32,2048]{1,0:T(8,128)(2,1)}, u32[]{:S(2)}, u32[]{:S(2)}) collective-permute-start(bf16[32,2048]{1,0:T(8,128)(2,1)} %dynamic-slice_bitcast_fusion), channel_id=1, source_target_pairs={{0,4},{4,0},{1,5},{5,1},{2,6},{6,2},{3,7},{7,3},{8,12},{12,8},{9,1... | collective-permute-start | bytes 393224 | tf_op jit(solution)/shard_map/ppermute | solution.py:803
  986.7 1.5 collective-permute-start.13
  (136 other events, 1108.1 us)
Sparse Core Ops, SparseCore 0:
  287.8 74.9 all-gather.5
  365.5 78.6 all-gather.3
  462.7 94.9 reduce-scatter.5
  559.9 94.6 reduce-scatter.7
  656.7 94.6 reduce-scatter.3

commit v4 on v3

--- a/solution.py
+++ b/solution.py
@@ -45,15 +45,59 @@
     return (norm_parts(hidden)[0] * gain_row + shift_row).astype(B16)
 
 
-def norm_backward(hidden, gain_row, grad):
-    unit, scale = norm_parts(hidden)
-    weighted = grad * gain_row
-    grad_hidden = scale * (
+def norm_backward_kernel(last, h_ref, mine_ref, other_ref, grad_ref, gain_ref, *rest):
+    if last:
+        hot_ref, low_ref, sums_ref, lang_ref = rest
+    else:
+        full_ref, low_ref, sums_ref = rest
+    unit, scale = norm_parts(h_ref[...])
+    down = mine_ref[...].astype(F32) + other_ref[...].astype(F32)
+    weighted = down * gain_ref[...]
+    step = scale * (
         weighted
         - jnp.mean(weighted, axis=-1, keepdims=True)
         - unit * jnp.mean(weighted * unit, axis=-1, keepdims=True)
     )
-    return grad_hidden, jnp.sum(grad * unit, axis=0), jnp.sum(grad, axis=0)
+    full = grad_ref[...].astype(F32) + step
+    low = full.astype(B16)
+    low_ref[...] = low
+
+    @pl.when(pl.program_id(0) == 0)
+    def _():
+        sums_ref[...] = jnp.zeros_like(sums_ref)
+        if last:
+            lang_ref[...] = jnp.zeros_like(lang_ref)
+
+    for k, value in enumerate((down * unit, down, low.astype(F32))):
+        sums_ref[k : k + 1, :] += jnp.sum(value, axis=0, keepdims=True)
+    if last:
+        hot = hot_ref[...]
+        rest_low = (full - low.astype(F32)).astype(B16)
+        lang_ref[...] += product_tn(hot, low) + product_tn(hot, rest_low)
+    else:
+        full_ref[...] = full
+
+
+def norm_backward(hidden, gain_row, parts, grad, hot=None):
+    count, width = hidden.shape
+    last = hot is not None
+    block = pl.BlockSpec((BLOCK, width), lambda i: (i, 0))
+    still = lambda rows: pl.BlockSpec((rows, width), lambda i: (0, 0))
+    inputs = [hidden, parts[0], parts[1], grad, gain_row] + ([hot] if last else [])
+    outs = [(count, B16, block), (8, F32, still(8))]
+    outs = outs + [(hot.shape[1], F32, still(hot.shape[1]))] if last else [(count, F32, block)] + outs
+    return pl.pallas_call(
+        functools.partial(norm_backward_kernel, last),
+        grid=(count // BLOCK,),
+        in_specs=[block] * 4
+        + [still(1)]
+        + ([pl.BlockSpec((BLOCK, hot.shape[1]), lambda i: (i, 0))] if last else []),
+        out_specs=[spec for _, _, spec in outs],
+        out_shape=[jax.ShapeDtypeStruct((rows, width), kind) for rows, kind, _ in outs],
+        compiler_params=pltpu.CompilerParams(vmem_limit_bytes=28 * 2**20),
+        cost_estimate=pl.CostEstimate(flops=30 * count * width, bytes_accessed=18 * count * width, transcendentals=0),
+        name="norm_last" if last else "norm_grad",
+    )(*inputs)
 
 
 def gelu_both(values):
@@ -75,18 +119,36 @@
     return lax.dot_general(left, right, (((1,), (1,)), ((), ())), preferred_element_type=F32)
 
 
-def head_masked(value):
-    lane = lax.broadcasted_iota(jnp.int32, value.shape, 1) // HEAD_DIM
+def head_masked(value, axis=1):
+    lane = lax.broadcasted_iota(jnp.int32, value.shape, axis) // HEAD_DIM
     zero = jnp.zeros_like(value)
     return [jnp.where(lane == h, value, zero) for h in range(HEADS)]
 
 
+def dot_nn(left, right):
+    return jnp.dot(left, right, preferred_element_type=F32)
+
+
 def fold_rows(value, combine):
     return combine(value.reshape(value.shape[0] // 8, 8, value.shape[1]), axis=0)
 
 
 def forward_kernel(
-    causal, info_ref, q_ref, k_ref, v_ref, qseg_ref, kseg_ref, o_ref, lse_ref, vt_ref, s_ref, acc_ref, top_ref, sum_ref
+    causal,
+    info_ref,
+    q_ref,
+    k_ref,
+    v_ref,
+    qseg_ref,
+    kseg_ref,
+    o_ref,
+    lse_ref,
+    vt_ref,
+    s_ref,
+    acc_ref,
+    top_ref,
+    sum_ref,
+    qt_ref,
 ):
     block = pl.program_id(1)
     blocks = k_ref.shape[0] // BLOCK
@@ -97,7 +159,8 @@
         vt_ref[...] = v_ref[...].T
 
     qseg = qseg_ref[...]
-    heads = head_masked(q_ref[...] * jnp.asarray(HEAD_DIM**-0.5, B16))
+    for h, head in enumerate(head_masked((q_ref[...] * jnp.asarray(HEAD_DIM**-0.5, B16)).T, 0)):
+        qt_ref[h] = head
     top_ref[...] = jnp.full(top_ref.shape, -1e30, F32)
     sum_ref[...] = jnp.zeros_like(sum_ref)
     acc_ref[...] = jnp.zeros_like(acc_ref)
@@ -108,7 +171,7 @@
             keys = k_ref[j * BLOCK : (j + 1) * BLOCK, :]
             allowed = allowed_block(causal, kseg_ref, qseg, length, j * BLOCK, block * BLOCK)
             for h in range(HEADS):
-                scores = jnp.where(allowed, dot_nt(keys, heads[h]), MASKED)
+                scores = jnp.where(allowed, dot_nn(keys, qt_ref[h]), MASKED)
                 s_ref[h, j * BLOCK : (j + 1) * BLOCK, :] = scores
                 top_ref[h] = jnp.maximum(top_ref[h], fold_rows(scores, jnp.max))
 
@@ -149,7 +212,7 @@
     kseg_ref,
     *rest,
 ):
-    *outs, kt_ref, dqt_ref, sums_ref, done_ref, sems = rest
+    *outs, kt_ref, dqt_ref, sums_ref, done_ref, qt_ref, dot_ref, sems = rest
     group, block = pl.program_id(0), pl.program_id(1)
     groups = pl.num_programs(0)
     blocks = k_ref.shape[0] // BLOCK
@@ -162,16 +225,19 @@
 
     qseg = qseg_ref[...]
     grads = do_ref[...]
-    query_heads = head_masked(q_ref[...] * jnp.asarray(HEAD_DIM**-0.5, B16))
-    grad_heads = head_masked(grads)
-    queries_down = jnp.concatenate(query_heads, axis=0)
-    grads_down = jnp.concatenate(grad_heads, axis=0)
-    mixed = grads.astype(F32) * o_ref[...].astype(F32)
-    lane = lax.broadcasted_iota(jnp.int32, (8, GROUP), 1) // HEAD_DIM
-    picks = (lane == lax.broadcasted_iota(jnp.int32, (8, GROUP), 0)).astype(F32)
-    inner = lax.dot_general(
-        picks, mixed, (((1,), (1,)), ((), ())), precision=lax.Precision.HIGHEST, preferred_element_type=F32
-    )
+    scaled = q_ref[...] * jnp.asarray(HEAD_DIM**-0.5, B16)
+    grads_up = grads.T
+    for h, head in enumerate(head_masked(scaled.T, 0)):
+        qt_ref[h] = head
+    for h, head in enumerate(head_masked(grads_up, 0)):
+        dot_ref[h] = head
+    queries_down = jnp.concatenate(head_masked(scaled), axis=0)
+    grads_down = jnp.concatenate(head_masked(grads), axis=0)
+    mixed = grads_up.astype(F32) * o_ref[...].T.astype(F32)
+    inner = [
+        jnp.sum(fold_rows(mixed[h * HEAD_DIM : (h + 1) * HEAD_DIM], jnp.sum), axis=0, keepdims=True)
+        for h in range(HEADS)
+    ]
     dqt_ref[...] = jnp.zeros_like(dqt_ref)
     for j in range(blocks):
 
@@ -183,10 +249,10 @@
             allowed = allowed_block(causal, kseg_ref, qseg, length, j * BLOCK, block * BLOCK)
             all_chances, all_scores = [], []
             for h in range(HEADS):
-                scores = dot_nt(keys, query_heads[h])
+                scores = dot_nn(keys, qt_ref[h])
                 chances = jnp.where(allowed, jnp.exp(scores - lse_ref[0, h : h + 1, :]), 0.0)
-                grad_chances = dot_nt(values, grad_heads[h])
-                grad_scores = (chances * (grad_chances - inner[h : h + 1, :])).astype(B16)
+                grad_chances = dot_nn(values, dot_ref[h])
+                grad_scores = (chances * (grad_chances - inner[h])).astype(B16)
                 all_chances.append(chances.astype(B16))
                 all_scores.append(grad_scores)
                 part = slice(h * HEAD_DIM, (h + 1) * HEAD_DIM)
@@ -253,7 +319,8 @@
             in_specs=[query, key, value, qseg, kseg],
             out_specs=[plain, stats],
             scratch_shapes=[pltpu.VMEM((GROUP, count), B16), pltpu.VMEM((HEADS, count, BLOCK), F32), pltpu.VMEM((GROUP, BLOCK), F32)]
-            + [pltpu.VMEM((HEADS, 8, BLOCK), F32)] * 2,
+            + [pltpu.VMEM((HEADS, 8, BLOCK), F32)] * 2
+            + [pltpu.VMEM((HEADS, GROUP, BLOCK), B16)],
         ),
         out_shape=[
             jax.ShapeDtypeStruct((count, width), B16),
@@ -285,6 +352,8 @@
                 pltpu.VMEM((GROUP, BLOCK), F32),
                 pltpu.VMEM((2, count, GROUP), F32),
                 pltpu.VMEM((3, count, GROUP), B16),
+                pltpu.VMEM((HEADS, GROUP, BLOCK), B16),
+                pltpu.VMEM((HEADS, GROUP, BLOCK), B16),
                 pltpu.SemaphoreType.DMA((3,)),
             ],
         ),
@@ -304,10 +373,10 @@
 SUM_ROWS = [1, 3, 5, 7]
 
 
-def own_columns(array, core, runs=8):
-    split = array.reshape(array.shape[:-1] + (runs // 2, 2, array.shape[-1] // runs))
-    mine = lax.dynamic_index_in_dim(split, core, split.ndim - 2, keepdims=False)
-    return mine.reshape(array.shape[:-1] + (array.shape[-1] // 2,))
+def own_columns(array, core):
+    w = array.shape[-1] // 8
+    runs = [array[..., k * w : (k + 1) * w] for k in range(8)]
+    return jnp.concatenate([jnp.where(core == 0, runs[k], runs[k + 1]) for k in range(0, 8, 2)], axis=-1)
 
 
 def lay_side(array):
@@ -368,12 +437,15 @@
 
 
 class GatherItem:
-    def __init__(self, here, mine, other, out, start, size, send, recv, local):
-        self.here, self.mine, self.other, self.out = here, mine, other, out
+    def __init__(self, here, source, first, kind, out, start, size, send, recv, local):
+        self.here, self.source, self.first, self.kind, self.out = here, source, first, kind, out
         self.send, self.recv, self.local = send, recv, local
+        self.start, self.size = start, size
         self.all = pl.ds(start, size)
-        self.sides = pl.ds(start, size // 2), pl.ds(start + size // 2, size // 2)
-        self.core = here.c if other is not None else 0
+        self.sides = [pl.ds(start, size // 2), pl.ds(start + size // 2, size // 2)]
+        if kind == "small":
+            self.sides = [self.all]
+        self.core = 0 if kind == "rows" else here.c
         self.copies = {}
 
     def move(self, slot, region, peer, arrive=None):
@@ -381,20 +453,34 @@
         self.copies[slot] = remote(region, region, self.send.at[slot], recv, peer)
         return self.copies[slot]
 
+    def runs(self, core):
+        w = self.source.shape[-1] // 8
+        for q in range(self.start // w, (self.start + self.size) // w):
+            lanes = pl.ds(pl.multiple_of((q % 4 * 2 + core) * w, 128), w)
+            yield self.source.at[self.first + q // 4, :, lanes], pl.ds(q * w, w)
+
     def begin(self):
         here = self.here
+        place = self.out.at[here.y, here.x, self.core, here.z]
         block = self.out.at[here.y, here.x, self.core, here.z, :, self.all]
-        self.own = pltpu.make_async_copy(self.mine.at[:, self.all], block, self.local)
-        self.own.start()
-        if self.other is not None:
-            other = self.other.at[:, self.all]
-            self.copies[0] = remote(other, block, self.send.at[0], self.recv.at[0], here.core_peer)
-            self.copies[0].start()
+        self.own = pltpu.make_async_copy(block, block, self.local)
+        if self.kind == "columns":
+            for source, lanes in self.runs(here.c):
+                pltpu.make_async_copy(source, place.at[:, lanes], self.local).start()
+            for source, lanes in self.runs(1 - here.c):
+                remote(source, place.at[:, lanes], self.send.at[0], self.recv.at[0], here.core_peer).start()
+        else:
+            source = self.source.at[self.first, :, self.all]
+            pltpu.make_async_copy(source, block, self.local).start()
+            if self.kind == "small":
+                remote(source, block, self.send.at[0], self.recv.at[0], here.core_peer).start()
+        if self.kind != "rows":
+            self.copies[0] = remote(block, block, self.send.at[0], self.recv.at[0], here.core_peer)
 
     def stage_z(self):
         here = self.here
         self.own.wait()
-        if self.other is not None:
+        if self.kind != "rows":
             self.copies[0].wait_recv()
         block = self.out.at[here.y, here.x, :, here.z, :, self.all]
         self.move(1, block, here.z_peer(1)).start()
@@ -408,22 +494,23 @@
         pl.when(here.inner)(self.move(8, block, here.z_peer(1), arrive=3).start)
 
     def stage_one(self):
-        here, (a, b) = self.here, self.sides
+        here = self.here
         self.copies[1].wait_recv()
         self.copies[3].wait_recv()
-        self.move(4, self.out.at[here.y, here.x, :, :, :, a], here.x_peer).start()
-        self.move(5, self.out.at[here.y, here.x, :, :, :, b], here.y_peer).start()
+        for k, peer in list(enumerate((here.x_peer, here.y_peer)))[: len(self.sides)]:
+            self.move(4 + k, self.out.at[here.y, here.x, :, :, :, self.sides[k]], peer).start()
 
     def stage_two(self):
-        here, (a, b) = self.here, self.sides
+        here = self.here
         self.copies[4].wait_recv()
-        self.move(6, self.out.at[here.y, :, :, :, :, a], here.y_peer).start()
-        self.copies[5].wait_recv()
-        self.move(7, self.out.at[:, here.x, :, :, :, b], here.x_peer).start()
+        self.move(6, self.out.at[here.y, :, :, :, :, self.sides[0]], here.y_peer).start()
+        if len(self.sides) == 2:
+            self.copies[5].wait_recv()
+            self.move(7, self.out.at[:, here.x, :, :, :, self.sides[1]], here.x_peer).start()
 
     def finish(self):
-        self.copies[6].wait_recv()
-        self.copies[7].wait_recv()
+        for k in range(len(self.sides)):
+            self.copies[6 + k].wait_recv()
         for slot, copy in self.copies.items():
             if slot in (3, 8):
                 pl.when(self.here.inner)(copy.wait_send)
@@ -482,19 +569,18 @@
     refs = list(refs)
     take = lambda n: [refs.pop(0) for _ in range(n)]
     count = len(kinds)
-    ins = [take(2) if columns else take(1) + [None] for columns in kinds]
+    ins = take(count)
     row_ins = take(len(rows_at))
     outs = take(count)
     row_outs = take(len(rows_at))
     send, recv, local, row_send, row_recv, row_local = refs
     items = []
-    for k, (mine, other) in enumerate(ins):
-        size = mine.shape[-1] // cuts[k]
+    for k, (first, kind) in enumerate(kinds):
+        size = outs[k].shape[-1] // cuts[k]
         for cut in range(cuts[k]):
             n = len(items)
-            items.append(
-                GatherItem(here, mine, other, outs[k], cut * size, size, send.at[n], recv.at[n], local.at[n])
-            )
+            sems = send.at[n], recv.at[n], local.at[n]
+            items.append(GatherItem(here, ins[k], first, kind, outs[k], cut * size, size, *sems))
     count = len(items)
     rows = [
         RowIn(here, row_ins[t], row_outs[t], row_send.at[t], row_recv.at[t], row_local.at[t])
@@ -519,14 +605,16 @@
         row.finish()
 
 
-def gather_all(locals_, rows, rows_at):
-    kinds = [other is not None for _, other in locals_]
-    inputs = [v for pair in locals_ for v in pair if v is not None] + list(rows)
-    shapes = [
-        jax.ShapeDtypeStruct((2, 2, 2 if other is not None else 1, 4) + mine.shape, mine.dtype)
-        for mine, other in locals_
-    ] + [jax.ShapeDtypeStruct((4,) + row.shape[1:], row.dtype) for row in rows]
-    cuts = [2 if mine.size * (1 + columns) > 2**17 else 1 for (mine, _), columns in zip(locals_, kinds)]
+def gather_all(sources, rows, rows_at):
+    kinds = [(first, kind) for _, first, _, kind in sources]
+    inputs = [source[0] for source in sources] + list(rows)
+    shapes, cuts = [], []
+    for array, _, number, kind in sources:
+        _, r, n = array.shape
+        n = number * n // 2 if kind == "columns" else n
+        shapes.append(jax.ShapeDtypeStruct((2, 2, 1 if kind == "rows" else 2, 4, r, n), array.dtype))
+        cuts.append(2 if r * n * (2 if kind == "columns" else 1) > 2**16 else 1)
+    shapes += [jax.ShapeDtypeStruct((4,) + row.shape[1:], row.dtype) for row in rows]
     count, tensors = sum(cuts), len(rows)
     hbm = pl.BlockSpec(memory_space=pl.ANY)
 
@@ -650,6 +738,13 @@
             total = total + self.b3[j, c].astype(F32)
         return total
 
+    def place(self, value, core):
+        w = self.out.shape[-1] // 8
+        for k in range(value.shape[1] // w):
+            q = self.cut.start // w + k
+            lanes = pl.ds(pl.multiple_of((q % 4 * 2 + core) * w, 128), w)
+            self.out[q // 4, :, lanes] = value[:, k * w : (k + 1) * w]
+
     def stage_four(self):
         here = self.here
         self.copies[4].wait_recv()
@@ -658,14 +753,14 @@
         if self.columns:
             self.b4s[...] = self.total(1 - here.c).astype(self.b4s.dtype)
             self.go(7, self.b4s, self.b4, here.core_peer)
-            self.out[here.c, :, self.cut] = self.total(here.c)
+            self.place(self.total(here.c), here.c)
         else:
             self.out[:, self.cut] = self.total(0)
 
     def finish(self):
         if self.columns:
             self.copies[7].wait_recv()
-            self.out[1 - self.here.c, :, self.cut] = self.b4[...].astype(F32)
+            self.place(self.b4[...].astype(F32), 1 - self.here.c)
         for slot, copy in self.copies.items():
             if slot == 6:
                 pl.when(self.here.inner)(copy.wait_send)
@@ -753,14 +848,14 @@
         row.finish()
 
 
-def sum_all(grads, rows, rows_at):
+def sum_all(grads, parts, rows, rows_at):
     flags = [grad.shape[2] == 2 for grad in grads]
     hbm = pl.BlockSpec(memory_space=pl.ANY)
     vmem = pl.BlockSpec(memory_space=pltpu.VMEM)
     shapes, scratch, cuts = [], [], []
-    for grad, columns in zip(grads, flags):
+    for grad, columns, number in zip(grads, flags, parts):
         _, _, cores, places, r, n = grad.shape
-        shapes.append(jax.ShapeDtypeStruct((2, r, n) if columns else (r, n), F32))
+        shapes.append(jax.ShapeDtypeStruct((number, r, 2 * n // number) if columns else (r, n), F32))
         cuts.append(2 if grad.size > 2**SUM_CUT else 1)
         n = n // cuts[-1]
         sizes = [(2, cores, places, r, n)] * 2 + [(cores, places, r, n), (3, cores, r, n), (cores, r, n)]
@@ -802,42 +897,60 @@
     def over_core(self, value):
         return lax.ppermute(value, "core", [(0, 1), (1, 0)])
 
+    def both_parts(self, part):
+        part = part.astype(B16)
+        return part, self.over_core(part)
+
     def both_cores(self, part):
-        part = part.astype(B16)
-        return part.astype(F32) + self.over_core(part).astype(F32)
+        mine, other = self.both_parts(part)
+        return mine.astype(F32) + other.astype(F32)
 
 
 class Tree:
     def __init__(self, place):
         self.place = place
 
-    def gather(self, flat, columns, rows, tensors, tensors_at):
-        core = self.place.core
-        padded = jnp.pad(flat, (0, -flat.shape[0] % 4096)).reshape(16, -1)
-        locals_ = {-1: (padded, padded)}
+    def gather(self, table, ffb, columns, rows, tensors, tensors_at):
+        n, r = table.shape
+        small = jnp.pad(table, ((0, 128 - n), (0, 0))).T
+        small = jnp.concatenate([small, jnp.pad(ffb, ((0, 16 - ffb.shape[0]), (0, 0)))], axis=0)
+        sources = {-1: (small[None], 0, 1, "small")}
         for key, value in columns.items():
-            locals_[key] = (lay_side(own_columns(value, core)), lay_side(own_columns(value, 1 - core)))
+            sources[key] = value + ("columns",)
         for key, value in rows.items():
-            locals_[key] = (value, None)
-        keys = sorted(locals_)
-        outs = gather_all([locals_[key] for key in keys], tensors, tensors_at)
+            sources[key] = value + ("rows",)
+        keys = sorted(sources)
+        outs = gather_all([sources[key] for key in keys], tensors, tensors_at)
         whole = {key: out for key, out in zip(keys, outs)}
-        small = whole.pop(-1).reshape(32, -1)[:, : flat.shape[0]]
+        small = whole.pop(-1)
+        table = small[..., :r, :].reshape(-1, 128).astype(F32).T
+        ffb = small[..., r : r + ffb.shape[0], :].reshape(32, ffb.shape[0], -1).transpose(1, 0, 2)
         weights = {key: value.reshape(-1, value.shape[-1]) for key, value in whole.items()}
-        return small, weights, [out.reshape(-1, out.shape[-1]) for out in outs[len(keys) :]]
+        return table, ffb.reshape(ffb.shape[0], -1), weights, [out.reshape(-1, out.shape[-1]) for out in outs[len(keys) :]]
 
     def gather_late(self, columns, rows, after):
         core = self.place.core
         mine, other = lay_side(own_columns(columns, core)), lay_side(own_columns(columns, 1 - core))
         both = jnp.stack(xor_arrange([mine, self.place.over_core(other)], core))
-        both, rows, _ = lax.optimization_barrier((both, rows, after))
-        full = lax.all_gather(both, ("dp", "seq"), axis=0, tiled=False)
-        full = full.reshape((4, 4) + both.shape).transpose(0, 2, 1, 3, 4)
-        return full.reshape(-1, full.shape[-1]), lax.all_gather(rows, ("dp", "seq"), axis=0, tiled=True)
-
-    def early_columns(self, pairs, parts):
+        width = rows.shape[1]
+        wide = both.shape[2] // width
+        parts = [both[:, :, k * width : (k + 1) * width].reshape(-1, width) for k in range(wide)]
+        local = jnp.concatenate(parts + [rows], axis=0)
+        local, _ = lax.optimization_barrier((local, after))
+        full = lax.all_gather(local, ("dp", "seq"), axis=0, tiled=False)
+        r = parts[0].shape[0]
+        first = [full[:, k * r : (k + 1) * r].reshape(4, 4, 2, -1, width) for k in range(wide)]
+        first = [part.transpose(0, 2, 1, 3, 4).reshape(-1, width) for part in first]
+        return lay_wide(first), full[:, wide * r :].reshape(-1, width)
+
+    def full_columns(self, pairs):
+        return lay_wide([product_tn(features, grad).astype(B16) for features, grad in pairs])
+
+    def full_rows(self, features, grad):
+        return product_tn(features, grad).astype(B16)
+
+    def early_columns(self, value, parts):
         core = self.place.core
-        value = lay_wide([product_tn(features, grad).astype(B16) for features, grad in pairs])
         value = value.reshape(4, 2, 4, -1, value.shape[1]).transpose(0, 2, 1, 3, 4)
         value = value.reshape(16, -1, value.shape[-1])
         total = lax.psum_scatter(value, ("dp", "seq"), scatter_dimension=0, tiled=True)
@@ -850,7 +963,7 @@
     def early_both(self, pairs, parts, features, grad):
         core = self.place.core
         values = [product_tn(f, g).astype(B16) for f, g in pairs]
-        width = values[0].shape[1]
+        width = min([v.shape[1] for v in values] + [grad.shape[1]])
         cut = [v[:, k : k + width] for v in values for k in range(0, v.shape[1], width)]
         cut = [v.reshape(4, 2, 4, -1, width).transpose(0, 2, 1, 3, 4).reshape(16, -1, width) for v in cut]
         rows = product_tn(features, grad).astype(B16)
@@ -858,15 +971,17 @@
         r = rows.shape[1]
         cut += [rows[:, :, k : k + width] for k in range(0, rows.shape[2], width)]
         total = lax.psum_scatter(jnp.concatenate(cut, axis=1), ("dp", "seq"), scatter_dimension=0, tiled=True)[0]
-        columns, rest = total[: 2 * r * parts].reshape(parts, 2, r, width), total[2 * r * parts :]
+        pieces, small = len(cut) - rows.shape[2] // width, cut[0].shape[1]
+        columns, rest = total[: small * pieces].reshape(pieces, 2, small // 2, width), total[small * pieces :]
         mine = lax.dynamic_index_in_dim(columns, core, 1, keepdims=False)
         other = lax.dynamic_index_in_dim(columns, 1 - core, 1, keepdims=False)
         both = jnp.stack(xor_arrange([mine, self.place.over_core(other)], core))
-        both = both.astype(F32).reshape(2, parts, r, 4, -1).transpose(1, 2, 3, 0, 4).reshape(parts, r, -1)
+        both = both.astype(F32).reshape(2, parts, pieces // parts, small // 2, width)
+        both = both.transpose(0, 1, 3, 2, 4).reshape(2, parts, small // 2, 4, -1)
+        both = both.transpose(1, 2, 3, 0, 4).reshape(parts, small // 2, -1)
         return both, rest.astype(F32).reshape(-1, r, width).transpose(1, 0, 2).reshape(r, -1)
 
-    def early_rows(self, features, grad):
-        value = product_tn(features, grad).astype(B16)
+    def early_rows(self, value):
         return lax.psum_scatter(value, ("dp", "seq"), scatter_dimension=0, tiled=True).astype(F32)
 
     def weave(self, both, parts):
@@ -895,14 +1010,11 @@
             grads.append(value.reshape(2, 2, 1, 4, value.shape[0] // 16, value.shape[1]))
             keys.append(key)
         order = sorted(range(len(keys)), key=lambda k: keys[k])
-        outs = sum_all([grads[k] for k in order] + [both], [t.reshape(4, -1, t.shape[-1]) for t in tensors], SUM_ROWS)
+        parts = [columns[keys[k]][2] if keys[k] in columns else 1 for k in order] + [1]
+        outs = sum_all([grads[k] for k in order] + [both], parts, [t.reshape(4, -1, t.shape[-1]) for t in tensors], SUM_ROWS)
         result = {}
         for k, out in zip(order, outs):
-            key = keys[k]
-            if key in columns:
-                result[key] = self.weave(out, columns[key][2])
-            else:
-                result[key] = out
+            result[keys[k]] = out
         flat = outs[len(keys)].reshape(-1)[:size]
         edge = table.shape[1] // 16 * n
         return result, flat[:edge].reshape(n, -1), flat[edge:].reshape(m, -1), outs[len(keys) + 1 :]
@@ -947,14 +1059,15 @@
         placed = xor_arrange(got, place.z)
         return jnp.stack([jnp.concatenate(placed[2 * i : 2 * i + 2], axis=1) for i in range(2)])
 
-    def gather(self, flat, columns, rows, tensors, tensors_at):
-        small = lax.all_gather(flat, self.axes, axis=0, tiled=False)
+    def gather(self, table, ffb, columns, rows, tensors, tensors_at):
+        table = lax.all_gather(table, self.axes, axis=1, tiled=True).astype(F32)
+        ffb = lax.all_gather(ffb, self.axes, axis=1, tiled=True)
         weights = {}
-        for key, value in columns.items():
-            weights[key] = self.whole_columns(value)
-        for key, value in rows.items():
-            weights[key] = self.whole_rows(value)
-        return small, weights, [self.row_in(tensor) for tensor in tensors]
+        for key, (value, first, number) in columns.items():
+            weights[key] = self.whole_columns(value[first : first + number])
+        for key, (value, first, _) in rows.items():
+            weights[key] = self.whole_rows(value[first])
+        return table, ffb, weights, [self.row_in(tensor) for tensor in tensors]
 
     def whole_columns(self, value):
         full = lax.all_gather(value, self.axes, axis=1, tiled=True)
@@ -969,16 +1082,21 @@
     def gather_late(self, columns, rows, after):
         return self.whole_columns(columns), self.whole_rows(rows)
 
-    def early_columns(self, pairs, parts):
-        full = lay_wide([product_tn(features, grad) for features, grad in pairs])
+    def full_columns(self, pairs):
+        return lay_wide([product_tn(features, grad).astype(B16) for features, grad in pairs])
+
+    def full_rows(self, features, grad):
+        return product_tn(features, grad).astype(B16)
+
+    def early_columns(self, full, parts):
         full = full.reshape(full.shape[0], parts, -1).transpose(1, 0, 2).astype(B16)
         return self.scatter(self.spread(full, 2), 1)
 
     def early_both(self, pairs, parts, features, grad):
-        return self.early_columns(pairs, parts), self.early_rows(features, grad)
-
-    def early_rows(self, features, grad):
-        return self.scatter(self.spread(product_tn(features, grad).astype(B16), 0), 0)
+        return self.early_columns(self.full_columns(pairs), parts), self.early_rows(self.full_rows(features, grad))
+
+    def early_rows(self, full):
+        return self.scatter(self.spread(full, 0), 0)
 
     def spread(self, half, axis):
         shape = half.shape[:axis] + (4, 1, half.shape[axis] // 4) + half.shape[axis + 1 :]
@@ -995,9 +1113,9 @@
     def sums(self, columns, rows, table, hidden, tensors):
         result = {}
         for key, (features, grad, parts) in columns.items():
-            result[key] = self.early_columns([(features, grad)], parts)
+            result[key] = self.early_columns(self.full_columns([(features, grad)]), parts)
         for key, (features, grad) in rows.items():
-            result[key] = self.early_rows(features, grad)
+            result[key] = self.early_rows(self.full_rows(features, grad))
         small = [self.scatter(self.spread(v, 1), 1) for v in (table, hidden)]
         return result, small[0], small[1], [self.row_out(tensor) for tensor in tensors]
 
@@ -1034,14 +1152,12 @@
     half = width // 2
     langs = lang_table.shape[0]
 
-    n_small = langs + gains.shape[0] + biases.shape[0]
     table = jnp.concatenate([lang_table, gains, biases], axis=0)
-    flat = jnp.concatenate([table.reshape(-1), ff_biases.reshape(-1)])
-    edge = table.size
-    everything, weights, tensors = moves.gather(
-        flat,
-        {0: enc_proj, 2: enc_in[None], 4: dec_proj[0:3], 6: dec_proj[3:6]},
-        {1: enc_oproj, 3: enc_out, 5: dec_oproj[0], 7: dec_oproj[1]},
+    table, ffb, weights, tensors = moves.gather(
+        table,
+        ff_biases,
+        {0: (enc_proj, 0, 3), 2: (enc_in[None], 0, 1), 4: (dec_proj, 0, 3), 6: (dec_proj, 3, 3)},
+        {1: (enc_oproj[None], 0, 1), 3: (enc_out[None], 0, 1), 5: (dec_oproj, 0, 1), 7: (dec_oproj, 1, 1)},
         [src_x, tgt_x, tgt_cot, src_cot],
         [2, 5, 8, 11],
     )
@@ -1049,14 +1165,13 @@
     enc_qkv_w, enc_o_w, enc_in_w, enc_out_w, dec_qkv_w, dec_o_w, cross_w, cross_o_w = (
         weights[k] for k in range(8)
     )
-    dec_in_w, dec_out_w = moves.gather_late(dec_in[None], dec_out, everything)
-    table = everything[:, :edge].reshape(2 * dp * seq, n_small, -1).transpose(1, 0, 2).reshape(n_small, width)
-    ffb = everything[:, edge:].reshape(2 * dp * seq, 2, -1).transpose(1, 0, 2).reshape(2, -1)
-    languages = table[:langs]
-    gain_f = table[langs : langs + gains.shape[0]].astype(F32)
-    bias_f = table[langs + gains.shape[0] :].astype(F32)
-    ffb_own = own_columns(ffb.astype(F32), core)
-    bias_own = own_columns(bias_f, core)
+    dec_in_w, dec_out_w = moves.gather_late(dec_in[None], dec_out, ffb)
+    table, ffb_own = lax.optimization_barrier((table, own_columns(ffb, core).astype(F32)))
+    languages = table[: langs + -langs % 16].astype(B16)
+    gain_f = [table[langs + k : langs + k + 1] for k in range(5)]
+    bias_f = [table[langs + 5 + k : langs + 6 + k] for k in range(16)]
+    table_own = own_columns(table, core)
+    bias_own = [table_own[langs + 5 + k : langs + 6 + k] for k in range(16)]
 
     meta = jnp.concatenate([src_seg, tgt_seg, tgt_len[:, None], src_lang, tgt_lang], axis=1)
     rows = jnp.where(place.z // 2 == core, meta, place.over_core(meta))
@@ -1068,59 +1183,59 @@
     def onehot(segments, chosen):
         member = segments[:, None] == jnp.arange(segs, dtype=jnp.int32)[None, :]
         token = jnp.sum(jnp.where(member, chosen[None, :], 0), axis=1)
-        return (token[:, None] == jnp.arange(langs, dtype=jnp.int32)[None, :]).astype(B16)
+        return (token[:, None] == jnp.arange(langs + -langs % 16, dtype=jnp.int32)[None, :]).astype(B16)
 
     src_hot, tgt_hot = onehot(s_seg, s_lang), onehot(t_seg, t_lang)
     enc_masks = (block_info(False, s_seg, s_seg, t_len), s_seg[None, :], s_seg[:, None])
     dec_masks = (block_info(True, t_seg, t_seg, t_len), t_seg[None, :], t_seg[:, None])
     cross_masks = (block_info(False, t_seg, s_seg, t_len), t_seg[None, :], s_seg[:, None])
 
-    none = jnp.zeros((half,), F32)
+    none = jnp.zeros((1, half), F32)
     packed = (0, half // GROUP, 2 * half // GROUP)
 
     enc_h0 = source.astype(F32) + product(src_hot, languages)
     enc_n1 = layer_norm(enc_h0, gain_f[0], bias_f[0])
-    enc_qkv_bias = jnp.concatenate([bias_own[1], none, bias_own[2]])
+    enc_qkv_bias = jnp.concatenate([bias_own[1], none, bias_own[2]], axis=1)
     enc_qkv = (product(enc_n1, enc_qkv_w) + enc_qkv_bias).astype(B16)
     enc_mixed, enc_lse = attend_forward(False, enc_masks, enc_qkv, enc_qkv, enc_qkv, packed, half)
     enc_h1 = enc_h0 + place.both_cores(product(enc_mixed, enc_o_w)) + bias_f[3]
     enc_n2 = layer_norm(enc_h1, gain_f[1], bias_f[4])
-    enc_acted, enc_slope = gelu_both(product(enc_n2, enc_in_w) + ffb_own[0])
+    enc_acted, enc_slope = gelu_both(product(enc_n2, enc_in_w) + ffb_own[0:1])
     encoded = enc_h1 + place.both_cores(product(enc_acted, enc_out_w)) + bias_f[5]
     memory = encoded.astype(B16)
 
     dec_h0 = target.astype(F32) + product(tgt_hot, languages)
     dec_n1 = layer_norm(dec_h0, gain_f[2], bias_f[6])
-    dec_qkv_bias = jnp.concatenate([bias_own[7], none, bias_own[8]])
+    dec_qkv_bias = jnp.concatenate([bias_own[7], none, bias_own[8]], axis=1)
     dec_qkv = (product(dec_n1, dec_qkv_w) + dec_qkv_bias).astype(B16)
     dec_mixed, dec_lse = attend_forward(True, dec_masks, dec_qkv, dec_qkv, dec_qkv, packed, half)
     dec_h1 = dec_h0 + place.both_cores(product(dec_mixed, dec_o_w)) + bias_f[9]
     dec_n2 = layer_norm(dec_h1, gain_f[3], bias_f[10])
     cross_q = (product(dec_n2, cross_w[:, :half]) + bias_own[11]).astype(B16)
-    cross_kv_bias = jnp.concatenate([none, bias_own[12]])
+    cross_kv_bias = jnp.concatenate([none, bias_own[12]], axis=1)
     cross_kv = (product(memory, cross_w[:, half:]) + cross_kv_bias).astype(B16)
     apart = (0, 0, half // GROUP)
     cross_mixed, cross_lse = attend_forward(False, cross_masks, cross_q, cross_kv, cross_kv, apart, half)
     dec_h2 = dec_h1 + place.both_cores(product(cross_mixed, cross_o_w)) + bias_f[13]
     dec_n3 = layer_norm(dec_h2, gain_f[4], bias_f[14])
-    dec_acted, dec_slope = gelu_both(product(dec_n3, dec_in_w) + ffb_own[1])
+    dec_acted, dec_slope = gelu_both(product(dec_n3, dec_in_w) + ffb_own[1:2])
     decoded = dec_h2 + place.both_cores(product(dec_acted, dec_out_w)) + bias_f[15]
 
     dec_du = (product_nt(target_cot, dec_out_w) * dec_slope.astype(F32)).astype(B16)
-    dec_dn3 = place.both_cores(product_nt(dec_du, dec_in_w))
-    dec_in_grad = moves.early_columns([(dec_n3, dec_du)], 1)
-    dec_out_grad = moves.early_rows(dec_acted, target_cot)
-    target_cot_f = target_cot.astype(F32)
-    step, gain_four, shift_14 = norm_backward(dec_h2, gain_f[4], dec_dn3)
-    grad_h2 = target_cot_f + step
-
-    cross_branch = grad_h2.astype(B16)
+    dec_dn3 = place.both_parts(product_nt(dec_du, dec_in_w))
+    dec_out_full = moves.full_rows(dec_acted, target_cot)
+    dec_in_full = moves.full_columns([(dec_n3, dec_du)])
+    dec_out_grad = moves.early_rows(dec_out_full)
+    dec_in_grad = moves.early_columns(dec_in_full, 1)
+    grad_h2, cross_branch, cross_rows = norm_backward(dec_h2, gain_f[4], dec_dn3, target_cot)
+    cross_branch, _, _ = lax.optimization_barrier((cross_branch, dec_out_full, dec_in_full))
+
     cross_do = product_nt(cross_branch, cross_o_w).astype(B16)
     cross_dq, cross_dkv = attend_backward(
         False, cross_masks, cross_q, cross_kv, cross_kv, apart, half, cross_mixed, cross_lse, cross_do
     )
     grad_memory = place.both_cores(product_nt(cross_dkv, cross_w[:, half:]))
-    dec_dn2 = place.both_cores(product_nt(cross_dq, cross_w[:, :half]))
+    dec_dn2 = place.both_parts(product_nt(cross_dq, cross_w[:, :half]))
 
     cross_grad, cross_o_grad = moves.early_both(
         [(dec_n2, cross_dq), (memory, cross_dkv)], 3, cross_mixed, cross_branch
@@ -1129,58 +1244,35 @@
     source_cot_f = source_cot.astype(F32) + grad_memory
     enc_ff_branch = source_cot_f.astype(B16)
     enc_du = (product_nt(enc_ff_branch, enc_out_w) * enc_slope.astype(F32)).astype(B16)
-    enc_dn2 = place.both_cores(product_nt(enc_du, enc_in_w))
-
-    step, gain_three, shift_10 = norm_backward(dec_h1, gain_f[3], dec_dn2)
-    grad_h1 = grad_h2 + step
-    self_branch = grad_h1.astype(B16)
+    enc_dn2 = place.both_parts(product_nt(enc_du, enc_in_w))
+
+    grad_h1, self_branch, self_rows = norm_backward(dec_h1, gain_f[3], dec_dn2, grad_h2)
     dec_do = product_nt(self_branch, dec_o_w).astype(B16)
     (dec_dqkv,) = attend_backward(
         True, dec_masks, dec_qkv, dec_qkv, dec_qkv, packed, half, dec_mixed, dec_lse, dec_do
     )
-    dec_dn1 = place.both_cores(product_nt(dec_dqkv, dec_qkv_w))
-    step, gain_two, shift_6 = norm_backward(dec_h0, gain_f[2], dec_dn1)
-    target_grad = grad_h1 + step
-
-    step, gain_one, shift_4 = norm_backward(enc_h1, gain_f[1], enc_dn2)
-    grad_e1 = source_cot_f + step
-    enc_branch = grad_e1.astype(B16)
+    dec_dn1 = place.both_parts(product_nt(dec_dqkv, dec_qkv_w))
+    target_high, target_rows, target_lang = norm_backward(dec_h0, gain_f[2], dec_dn1, grad_h1, tgt_hot)
+
+    grad_e1, enc_branch, enc_rows = norm_backward(enc_h1, gain_f[1], enc_dn2, source_cot_f)
     enc_do = product_nt(enc_branch, enc_o_w).astype(B16)
     (enc_dqkv,) = attend_backward(
         False, enc_masks, enc_qkv, enc_qkv, enc_qkv, packed, half, enc_mixed, enc_lse, enc_do
     )
-    enc_dn1 = place.both_cores(product_nt(enc_dqkv, enc_qkv_w))
-    step, gain_zero, shift_0 = norm_backward(enc_h0, gain_f[0], enc_dn1)
-    source_grad = grad_e1 + step
-
-    source_high, target_high = source_grad.astype(B16), target_grad.astype(B16)
-    lang_grad = 0.0
-    for hot, value, high in ((src_hot, source_grad, source_high), (tgt_hot, target_grad, target_high)):
-        low = (value - high.astype(F32)).astype(B16)
-        lang_grad = lang_grad + product_tn(hot, high) + product_tn(hot, low)
-    own = functools.partial(own_columns, core=core)
-    gain_rows = jnp.stack([gain_zero, gain_one, gain_two, gain_three, gain_four])
-    enc_qkv_sum, dec_qkv_sum = column_sum(enc_dqkv), column_sum(dec_dqkv)
-    bias_rows = jnp.stack(
-        [
-            own(shift_0),
-            enc_qkv_sum[:half],
-            enc_qkv_sum[2 * half :],
-            own(column_sum(enc_branch)),
-            own(shift_4),
-            own(column_sum(enc_ff_branch)),
-            own(shift_6),
-            dec_qkv_sum[:half],
-            dec_qkv_sum[2 * half :],
-            own(column_sum(self_branch)),
-            own(shift_10),
-            column_sum(cross_dq),
-            column_sum(cross_dkv[:, half:]),
-            own(column_sum(cross_branch)),
-            own(shift_14),
-            own(column_sum(target_cot)),
-        ]
-    )
+    enc_dn1 = place.both_parts(product_nt(enc_dqkv, enc_qkv_w))
+    source_high, source_rows, source_lang = norm_backward(enc_h0, gain_f[0], enc_dn1, grad_e1, src_hot)
+
+    ff_sums = jnp.stack([column_sum(enc_ff_branch), column_sum(target_cot)])
+    wide = [rows[:3] for rows in (source_rows, enc_rows, target_rows, self_rows, cross_rows)]
+    wide = own_columns(jnp.concatenate([source_lang + target_lang] + wide + [ff_sums], axis=0), core)
+    enc_sum, dec_sum = column_sum(enc_dqkv)[None], column_sum(dec_dqkv)[None]
+    narrow = [enc_sum[:, :half], enc_sum[:, 2 * half :], dec_sum[:, :half], dec_sum[:, 2 * half :]]
+    narrow += [column_sum(cross_dq)[None], column_sum(cross_dkv)[None, half:]]
+    small_table = jnp.concatenate([wide] + narrow, axis=0)
+    at = src_hot.shape[1]
+    gain_places = [at, at + 3, at + 6, at + 9, at + 12]
+    bias_places = [at + k for k in (1, 17, 18, 5, 4, 15, 7, 19, 20, 11, 10, 21, 22, 14, 13, 16)]
+
     grads, small, ffb_grad, outputs = moves.sums(
         {
             1: (dec_n1, dec_dqkv, 3),
@@ -1192,18 +1284,19 @@
             3: (enc_acted, enc_ff_branch),
             5: (enc_mixed, enc_branch),
         },
-        jnp.concatenate([own(lang_grad), own(gain_rows), bias_rows], axis=0),
+        small_table,
         jnp.stack([column_sum(enc_du), column_sum(dec_du)]),
         [memory, decoded.astype(B16), source_high, target_high],
     )
+    picked = lambda places: jnp.concatenate([small[k : k + 1] for k in places], axis=0)
     return (
         outputs[0],
         outputs[1],
         outputs[2].astype(F32),
         outputs[3].astype(F32),
         small[:langs],
-        small[langs : langs + 5],
-        small[langs + 5 :],
+        picked(gain_places),
+        picked(bias_places),
         ffb_grad,
         grads[4],
         grads[5],

time: 1020 us -> 916 us (0.90); the launches traced: 1000 us -> 908 us
  other arithmetic: 91.9 us -> 40.5 us
  local copies, waits for them, and re-layouts: 117 us -> 81.9 us
  waiting for transfers between devices: 29.3 us -> 10.4 us
  Pallas kernels: 571 us -> 589 us
    pallas_call x0 -> x5, Pallas kernels: none -> 30.3 us  [norm_backward(): pl.pallas_call(functools.partial(norm_backward_kernel, last), grid=(count...]
    reduce_sum x5 -> x0, other arithmetic: 23.3 us -> none  [norm_backward(): return (grad_hidden, jnp.sum(grad * unit, axis=0), jnp.sum(grad, axis=0))]
    all_gather x2 -> x1, waiting for transfers between devices: 24.9 us -> 5.92 us  [gather_late(): full = lax.all_gather(local, ('dp', 'seq'), axis=0, tiled=False)]
    reduce_sum x9 -> x6, other arithmetic: 21.7 us -> 5.8 us  [column_sum(): return jnp.sum(values.astype(F32), axis=0)]
    pallas_call x3, Pallas kernels: 95.4 us -> 83.2 us  [attend_backward(): pl.pallas_call(functools.partial(backward_kernel, causal), grid_spec=pltp...]
    dot_general x15 -> x11, matrix products: 59.3 us -> 52.4 us  [product_tn(): lax.dot_general(left, right, (((0,), (0,)), ((), ())), preferred_element_...]
    unnamed x314 -> x284, local copies, waits for them, and re-layouts: 43.3 us -> 49.8 us
  transfers between devices with their start and end apart: 20 -> 19, of which waited for: 3 -> 3; matrix products, arithmetic and copies ran while one was open for 32% -> 23% of each run, Pallas kernels for 57% -> 65%
where the time goes in v4:
time: 916 us; the launch traced here: 908 us
  Pallas kernels  589 us (64%)
  matrix products  166 us (18%)
  local copies, waits for them, and re-layouts  81.9 us (9%)
  other arithmetic  40.5 us (4%)
  between operations  16.1 us (2%)
  waiting for transfers between devices  10.4 us (1%)
    pallas_call x1, Pallas kernels, gather_all(): pl.pallas_call(kernel, in_specs=[hbm] * len(inputs), out_specs=[hbm] * le...  235 us
    pallas_call x1, Pallas kernels, sum_all(): pl.pallas_call(kernel, in_specs=[hbm] * (len(grads) + tensors), out_specs...  199 us
    pallas_call x3, Pallas kernels, attend_backward(): pl.pallas_call(functools.partial(backward_kernel, causal), grid_spec=pltp...  83.2 us
    dot_general x13, matrix products, product(): return jnp.dot(left, right, preferred_element_type=F32)  58.5 us
    dot_general x11, matrix products, product_nt(): lax.dot_general(left, right, (((1,), (1,)), ((), ())), preferred_element_...  55 us
    dot_general x11, matrix products, product_tn(): lax.dot_general(left, right, (((0,), (0,)), ((), ())), preferred_element_...  52.4 us
    unnamed x284, local copies, waits for them, and re-layouts  49.8 us
    pallas_call x3, Pallas kernels, attend_forward(): pl.pallas_call(functools.partial(forward_kernel, causal), grid_spec=pltpu...  41.3 us
  transfers between devices with their start and end apart: 19, of which 3 were waited for; matrix products, arithmetic and copies ran while one was open for 23% of the time, Pallas kernels for 65%

profile of v4, /device:TPU:0, one launch (start us, length us, event | category | flops | bytes accessed | tf_op | source)
XLA Modules:
  0.0 908.1 jit_solution(12283415557484415377)
XLA Ops:
  13.9 235.0 %gather_all.1 = (bf16[2,2,2,4,48,128]{5,4,3,2,1,0:T(8,128)(2,1)}, bf16[2,2,2,4,32,1536]{5,4,3,2,1,0:T(8,128)(2,1)}, bf16[2,2,1,4,32,1024]{5,4,3,2,1,0:T(8,128)(2...) custom-call(bf16[1,48,128]{2,1,0:T(8,128)(2,1)} %fusion.27.refs_0_, ...), custom_call_target="tpu_custom_call" | custom-call | tf_op jit(solution)/shard_map/gather_all/pallas_call | solution.py:625
  260.3 6.9 add_convert_fusion.q_ref.k_ref.v_ref
  267.2 13.8 %attend.2 = (bf16[1024,512]{1,0:T(8,128)(2,1)S(1)}, f32[2,8,1024]{2,1,0:T(8,128)S(1)}) custom-call(s32[17]{0:T(128)S(1)} %get-tuple-element.272.info_ref, bf16[1024,1536]{1,0:T(8,128)(2,1)S(1)} %add_convert_fusion.q_ref.k_ref.v_ref, bf16[1024,1536]{1,0:T(8,128)(2,1)S(1)} %add_convert_fusion.q_ref.k_ref.v_ref, ...), custom_call_target="tpu_custom_call" | custom-call | flops 4294967296 | bytes 4194304 | tf_op jit(solution)/shard_map/attend/pallas_call | solution.py:314
  287.5 7.3 add_convert_fusion.1.q_ref.k_ref.v_ref
  294.8 13.8 %attend_causal.1 = (bf16[1024,512]{1,0:T(8,128)(2,1)S(1)}, f32[2,8,1024]{2,1,0:T(8,128)S(1)}) custom-call(s32[17]{0:T(128)S(1)} %get-tuple-element.271.info_ref, bf16[1024,1536]{1,0:T(8,128)(2,1)S(1)} %add_convert_fusion.1.q_ref.k_ref.v_ref, bf16[1024,1536]{1,0:T(8,128)(2,1)S(1)} %add_convert_fusion.1.q_ref.k_ref.v_ref, ...), custom_call_target="tpu_custom_call" | custom-call | flops 4294967296 | bytes 4194304 | tf_op jit(solution)/shard_map/attend_causal/pallas_call | solution.py:314
  318.2 8.5 multiply_convert_fusion.3
  326.8 7.1 convolution_convert_fusion.14
  345.2 13.7 %attend.3 = (bf16[1024,512]{1,0:T(8,128)(2,1)S(1)}, f32[2,8,1024]{2,1,0:T(8,128)S(1)}) custom-call(s32[17]{0:T(128)S(1)} %pad_add_fusion.1.info_ref, bf16[1024,512]{1,0:T(8,128)(2,1)S(1)} %add_convert_fusion.10.q_ref, bf16[1024,1024]{1,0:T(8,128)(2,1)S(1)} %add_convert_fusion.4.k_ref.v_ref, bf16[1024,1024]{1,0:T(8,128)(2,1)S(1)} %add_convert_fusion.4.k_ref.v_ref, ...), custom_call_target="tpu_custom_call" | custom-call | flops 4294967296 | bytes 4194304 | tf_op jit(solution)/shard_map/attend/pallas_call | solution.py:314
  383.5 7.2 multiply_convert_fusion.1
  390.6 9.9 %convert_reduce_fusion = (f32[2048]{0:T(1024)}, bf16[1024,2048]{1,0:T(8,128)(2,1)}) fusion(f32[1024,2048]{1,0:T(8,128)S(1)} %get-tuple-element.266, f32[2048]{0:T(1024)S(1)} %bitcast.327, bf16[1024,1024]{1,0:T(8,128)(2,1)S(1)} %bitcast.242, bf16[2048,1024]{1,0:T(8,128)(2,1)S(1)} %bitcast.275), kind=kOutput, calls=%fused_computation.12 | convolution fusion | flops 4326422528 | bytes 18890752 | tf_op jit(solution)/shard_map/dot_general | solution.py:30
  400.5 7.3 convolution_convert_fusion.4
  410.2 8.4 convolution_convert_fusion.5
  418.9 9.4 %fusion.12.mine_ref = bf16[1024,1024]{1,0:T(8,128)(2,1)} fusion(bf16[1024,2048]{1,0:T(8,128)(2,1)} %get-tuple-element.268, bf16[1024,1024]{1,0:T(8,128)(2,1)} %bitcast.294, bf16[1024,1024]{1,0:T(8,128)(2,1)} %bitcast.292), kind=kOutput, calls=%fused_computation.57 | convolution fusion | flops 4304404480 | bytes 10485760 | tf_op jit(solution)/shard_map/dot_general | solution.py:30
  430.4 9.5 %convolution_convert_fusion.7 = bf16[1024,1024]{1,0:T(8,128)(2,1)} fusion(bf16[1024,2048]{1,0:T(8,128)(2,1)} %get-tuple-element.265, bf16[2048,1024]{1,0:T(8,128)(2,1)} %bitcast.276), kind=kOutput, calls=%fused_computation.59 | convolution fusion | flops 4296015872 | bytes 10485760 | tf_op jit(solution)/shard_map/dot_general | solution.py:22
  451.1 27.7 %attend_grad.2 = (bf16[1024,512]{1,0:T(8,128)(2,1)S(1)}, bf16[1024,1024]{1,0:T(8,128)(2,1)S(1)}) custom-call(s32[17]{0:T(128)S(1)} %pad_add_fusion.1.info_ref, bf16[1024,512]{1,0:T(8,128)(2,1)S(1)} %copy-done.59, bf16[1024,1024]{1,0:T(8,128)(2,1)S(1)} %copy-done.61, bf16[1024,1024]{1,0:T(8,128)(2,1)S(1)} %copy-done.61, bf16[1024,512]{1,0:T(8,128)(2,1)S(1)} %copy-done.35, ...), custom_call_target="tpu_custom_call" | custom-call | flops 10737418240 | bytes 8388608 | tf_op jit(solution)/shard_map/attend_grad/pallas_call | solution.py:343
  520.4 27.9 %attend_grad_causal.1 = bf16[1024,1536]{1,0:T(8,128)(2,1)S(1)} custom-call(s32[17]{0:T(128)S(1)} %copy-done.53, bf16[1024,1536]{1,0:T(8,128)(2,1)S(1)} %copy-done.57, bf16[1024,1536]{1,0:T(8,128)(2,1)S(1)} %copy-done.57, bf16[1024,1536]{1,0:T(8,128)(2,1)S(1)} %copy-done.57, bf16[1024,512]{1,0:T(8,128)(2,1)S(1)} %copy-done.33, ...), custom_call_target="tpu_custom_call" | custom-call | flops 10737418240 | bytes 8388608 | tf_op jit(solution)/shard_map/attend_grad_causal/pallas_call | solution.py:343
  556.9 6.3 convolution_convert_fusion.2
  563.3 9.1 %convert_reduce_fusion.1 = (f32[2048]{0:T(1024)S(1)}, bf16[1024,2048]{1,0:T(8,128)(2,1)}) fusion(f32[1024,2048]{1,0:T(8,128)S(1)} %bitcast.360, f32[2048]{0:T(1024)S(1)} %bitcast.325, bf16[2048,1024]{1,0:T(8,128)(2,1)S(1)} %bitcast.343, f32[1024,1024]{1,0:T(8,128)S(1)} %get-tuple-element.173.grad_ref), kind=kOutput, calls=%fused_computation.13 | convolution fusion | flops 4327471104 | bytes 20987904 | tf_op jit(solution)/shard_map/dot_general | solution.py:30
  572.4 7.1 convolution_convert_fusion.10.mine_ref
  586.1 6.7 convolution_convert_fusion.3
  602.0 27.5 %attend_grad.3 = bf16[1024,1536]{1,0:T(8,128)(2,1)S(1)} custom-call(s32[17]{0:T(128)S(1)} %copy-done.51, bf16[1024,1536]{1,0:T(8,128)(2,1)S(1)} %copy-done.55, bf16[1024,1536]{1,0:T(8,128)(2,1)S(1)} %copy-done.55, bf16[1024,1536]{1,0:T(8,128)(2,1)S(1)} %copy-done.55, bf16[1024,512]{1,0:T(8,128)(2,1)S(1)} %copy-done.30, ...), custom_call_target="tpu_custom_call" | custom-call | flops 10737418240 | bytes 8388608 | tf_op jit(solution)/shard_map/attend_grad/pallas_call | solution.py:343
  648.2 6.8 norm_last.3
  663.9 6.8 norm_last.2
  674.6 198.8 %sum_all.1 = (f32[32,1024]{1,0:T(8,128)}, f32[3,32,1024]{2,1,0:T(8,128)}, f32[1,32,4096]{2,1,0:T(8,128)}, f32[128,1024]{1,0:T(8,128)}, f32[3,32,1024]{2,1,0:T(8,...) custom-call(bf16[2,2,1,4,32,1024]{5,4,3,2,1,0:T(8,128)(2,1)} %bitcas, ...), custom_call_target="tpu_custom_call" | custom-call | tf_op jit(solution)/shard_map/sum_all/pallas_call | solution.py:871
  (488 shorter events, 209.3 us)
Async XLA Ops:
  7.2 366.6 %all-gather.3.cloned.1.call-start = ((), (), s32[]{:S(2)}) async-start(), calls=%async_computation.6 | async-start | bytes 8912896 | tf_op jit(solution)/shard_map/all_gather | solution.py:940
  8.8 243.1 %collective-permute-start = (s32[2,2057]{1,0:T(2,128)S(1)}, s32[2,2057]{1,0:T(2,128)S(1)}, u32[]{:S(2)}, u32[]{:S(2)}) collective-permute-start(s32[2,2057]{1,0:T(2,128)S(1)} %concatenate.93), channel_id=1, source_target_pairs={{0,4},{4,0},{1,5},{5,1},{2,6},{6,2},{3,7},{7,3},{8,12},{12,8},{9,1... | collective-permute-start | bytes 49376 | tf_op jit(solution)/shard_map/ppermute | solution.py:898
  10.2 248.1 %collective-permute-start.5 = (bf16[32,2048]{1,0:T(8,128)(2,1)S(1)}, bf16[32,2048]{1,0:T(8,128)(2,1)S(1)}, u32[]{:S(2)}, u32[]{:S(2)}) collective-permute-start(bf16[32,2048]{1,0:T(8,128)(2,1)S(1)} %maximum_bitcast_fusion), channel_id=1, source_target_pairs={{0,4},{4,0},{1,5},{5,1},{2,6},{6,2},{3,7},{7,3},{8,12},{12,8},{9,1... | collective-permute-start | bytes 393224 | tf_op jit(solution)/shard_map/ppermute | solution.py:898
  251.7 35.8 %copy-start.109 = (f32[1,1024]{1,0:T(1,128)}, f32[1,1024]{1,0:T(1,128)S(1)}, u32[]{:S(2)}) copy-start(f32[1,1024]{1,0:T(1,128)S(1)} %get-tuple-element.197) | copy-start | bytes 12292
  251.7 63.5 %copy-start.46 = (f32[1,1024]{1,0:T(1,128)}, f32[1,1024]{1,0:T(1,128)S(1)}, u32[]{:S(2)}) copy-start(f32[1,1024]{1,0:T(1,128)S(1)} %get-tuple-element.187.gain_ref) | copy-start | bytes 12292
  251.7 63.5 %copy-start.107 = (f32[1,1024]{1,0:T(1,128)}, f32[1,1024]{1,0:T(1,128)S(1)}, u32[]{:S(2)}) copy-start(f32[1,1024]{1,0:T(1,128)S(1)} %get-tuple-element.186) | copy-start | bytes 12292
  251.7 63.4 %copy-start.102 = (f32[1,2048]{1,0:T(1,128)}, f32[1,2048]{1,0:T(1,128)S(1)}, u32[]{:S(2)}) copy-start(f32[1,2048]{1,0:T(1,128)S(1)} %get-tuple-element.245) | copy-start | bytes 24580
  259.2 624.0 %reduce-scatter.6.cloned.1.call-start = ((), (), s32[]{:S(2)}) async-start(), calls=%async_computation.4 | async-start | bytes 4456448 | tf_op jit(solution)/shard_map/reduce_scatter | solution.py:956
  260.2 84.9 %copy-start.37 = (s32[1024,1]{1,0:T(8,128)}, s32[1024,1]{1,0:T(8,128)S(1)}, u32[]{:S(2)}) copy-start(s32[1024,1]{1,0:T(8,128)S(1)} %copy.100.kseg_ref) | copy-start | bytes 12292
  283.6 27.0 %collective-permute-start.2 = (bf16[1024,1024]{1,0:T(8,128)(2,1)}, bf16[1024,1024]{1,0:T(8,128)(2,1)}, u32[]{:S(2)}, u32[]{:S(2)}) collective-permute-start(bf16[1024,1024]{1,0:T(8,128)(2,1)} %convolution_convert_fusion.15), channel_id=1, source_target_pairs={{0,4},{4,0},{1,5},{5,1},{2,6},{6,2},{3,7},{7,3},{8,12},{12,8},{9,1... | collective-permute-start | bytes 6291464 | tf_op jit(solution)/shard_map/ppermute | solution.py:898
  310.0 25.2 %collective-permute-start.1 = (bf16[1024,1024]{1,0:T(8,128)(2,1)S(1)}, bf16[1024,1024]{1,0:T(8,128)(2,1)S(1)}, u32[]{:S(2)}, u32[]{:S(2)}) collective-permute-start(bf16[1024,1024]{1,0:T(8,128)(2,1)S(1)} %convolution_convert_fusion.16), channel_id=1, source_target_pairs={{0,4},{4,0},{1,5},{5,1},{2,6},{6,2},{3,7},{7,3},{8,12},{12,8},{9,1... | collective-permute-start | bytes 6291464 | tf_op jit(solution)/shard_map/ppermute | solution.py:898
  333.9 7.6 collective-permute-start.3
  360.2 4.2 collective-permute-start.4
  410.2 474.7 %reduce-scatter.8.cloned.1.call-start = ((), (), s32[]{:S(2)}) async-start(), calls=%async_computation.5 | async-start | bytes 4456448 | tf_op jit(solution)/shard_map/reduce_scatter | solution.py:985
  418.7 471.2 %reduce-scatter.4.cloned.1.call-start = ((), (), s32[]{:S(2)}) async-start(), calls=%async_computation.3 | async-start | bytes 4456448 | tf_op jit(solution)/shard_map/reduce_scatter | solution.py:973
  428.3 12.1 %collective-permute-start.6 = (bf16[1024,1024]{1,0:T(8,128)(2,1)}, bf16[1024,1024]{1,0:T(8,128)(2,1)}, u32[]{:S(2)}, u32[]{:S(2)}) collective-permute-start(bf16[1024,1024]{1,0:T(8,128)(2,1)} %fusion.12.mine_ref), channel_id=1, source_target_pairs={{0,4},{4,0},{1,5},{5,1},{2,6},{6,2},{3,7},{7,3},{8,12},{12,8},{9,1... | collective-permute-start | bytes 6291464 | tf_op jit(solution)/shard_map/ppermute | solution.py:898
  439.9 63.4 %collective-permute-start.12 = (bf16[1024,1024]{1,0:T(8,128)(2,1)}, bf16[1024,1024]{1,0:T(8,128)(2,1)}, u32[]{:S(2)}, u32[]{:S(2)}) collective-permute-start(bf16[1024,1024]{1,0:T(8,128)(2,1)} %convolution_convert_fusion.7), channel_id=1, source_target_pairs={{0,4},{4,0},{1,5},{5,1},{2,6},{6,2},{3,7},{7,3},{8,12},{12,8},{9,1... | collective-permute-start | bytes 6291464 | tf_op jit(solution)/shard_map/ppermute | solution.py:898
  492.8 16.8 %collective-permute-start.7 = (bf16[1024,1024]{1,0:T(8,128)(2,1)}, bf16[1024,1024]{1,0:T(8,128)(2,1)}, u32[]{:S(2)}, u32[]{:S(2)}) collective-permute-start(bf16[1024,1024]{1,0:T(8,128)(2,1)} %convolution_convert_fusion.12.mine_ref), channel_id=1, source_target_pairs={{0,4},{4,0},{1,5},{5,1},{2,6},{6,2},{3,7},{7,3},{8,12},{12,8},{9,1... | collective-permute-start | bytes 6291464 | tf_op jit(solution)/shard_map/ppermute | solution.py:898
  496.6 57.0 %collective-permute-start.8 = (bf16[1024,1024]{1,0:T(8,128)(2,1)}, bf16[1024,1024]{1,0:T(8,128)(2,1)S(1)}, u32[]{:S(2)}, u32[]{:S(2)}) collective-permute-start(bf16[1024,1024]{1,0:T(8,128)(2,1)} %convolution_convert_fusion.11), channel_id=1, source_target_pairs={{0,4},{4,0},{1,5},{5,1},{2,6},{6,2},{3,7},{7,3},{8,12},{12,8},{9,1... | collective-permute-start | bytes 6291464 | tf_op jit(solution)/shard_map/ppermute | solution.py:898
  579.6 13.3 %collective-permute-start.9 = (bf16[1024,1024]{1,0:T(8,128)(2,1)S(1)}, bf16[1024,1024]{1,0:T(8,128)(2,1)S(1)}, u32[]{:S(2)}, u32[]{:S(2)}) collective-permute-start(bf16[1024,1024]{1,0:T(8,128)(2,1)S(1)} %convolution_convert_fusion.10.mine_ref), channel_id=1, source_target_pairs={{0,4},{4,0},{1,5},{5,1},{2,6},{6,2},{3,7},{7,3},{8,12},{12,8},{9,1... | collective-permute-start | bytes 6291464 | tf_op jit(solution)/shard_map/ppermute | solution.py:898
  580.4 62.4 %collective-permute-start.11 = (bf16[1024,1024]{1,0:T(8,128)(2,1)}, bf16[1024,1024]{1,0:T(8,128)(2,1)}, u32[]{:S(2)}, u32[]{:S(2)}) collective-permute-start(bf16[1024,1024]{1,0:T(8,128)(2,1)} %convolution_convert_fusion.8.mine_ref), channel_id=1, source_target_pairs={{0,4},{4,0},{1,5},{5,1},{2,6},{6,2},{3,7},{7,3},{8,12},{12,8},{9,1... | collective-permute-start | bytes 6291464 | tf_op jit(solution)/shard_map/ppermute | solution.py:898
  634.3 29.6 %collective-permute-start.10 = (bf16[1024,1024]{1,0:T(8,128)(2,1)}, bf16[1024,1024]{1,0:T(8,128)(2,1)}, u32[]{:S(2)}, u32[]{:S(2)}) collective-permute-start(bf16[1024,1024]{1,0:T(8,128)(2,1)} %convolution_convert_fusion.9.mine_ref), channel_id=1, source_target_pairs={{0,4},{4,0},{1,5},{5,1},{2,6},{6,2},{3,7},{7,3},{8,12},{12,8},{9,1... | collective-permute-start | bytes 6291464 | tf_op jit(solution)/shard_map/ppermute | solution.py:898
  884.2 2.5 collective-permute-start.14
  892.0 1.5 collective-permute-start.13
  (130 other events, 951.9 us)
Sparse Core Ops, SparseCore 0:
  259.3 114.3 all-gather.2
  410.3 99.4 reduce-scatter.5
  512.1 94.6 reduce-scatter.7
  609.0 94.6 reduce-scatter.3

commit v5 on v4

--- a/solution.py
+++ b/solution.py
@@ -12,6 +12,7 @@
 EPSILON = 1e-05
 MASKED = -1000000000.0
 BLOCK = 256
+ROWS = 32
 HEADS = 4
 GROUP = HEADS * HEAD_DIM
 B16 = jnp.bfloat16
@@ -42,7 +43,7 @@
 
 
 def layer_norm(hidden, gain_row, shift_row):
-    return (norm_parts(hidden)[0] * gain_row + shift_row).astype(B16)
+    return lax.optimization_barrier((norm_parts(hidden)[0] * gain_row + shift_row).astype(B16))
 
 
 def norm_backward_kernel(last, h_ref, mine_ref, other_ref, grad_ref, gain_ref, *rest):
@@ -94,7 +95,7 @@
         + ([pl.BlockSpec((BLOCK, hot.shape[1]), lambda i: (i, 0))] if last else []),
         out_specs=[spec for _, _, spec in outs],
         out_shape=[jax.ShapeDtypeStruct((rows, width), kind) for rows, kind, _ in outs],
-        compiler_params=pltpu.CompilerParams(vmem_limit_bytes=28 * 2**20),
+        compiler_params=pltpu.CompilerParams(vmem_limit_bytes=20 * 2**20),
         cost_estimate=pl.CostEstimate(flops=30 * count * width, bytes_accessed=18 * count * width, transcendentals=0),
         name="norm_last" if last else "norm_grad",
     )(*inputs)
@@ -106,11 +107,11 @@
     return (values * below).astype(B16), (below + values * density).astype(B16)
 
 
-def allowed_block(causal, kseg_ref, qseg, length, key_at, query_at):
-    allowed = kseg_ref[key_at : key_at + BLOCK, :] == qseg
+def allowed_rows(causal, kseg_ref, qseg, length, key_at, query_at):
+    allowed = kseg_ref[key_at : key_at + ROWS, :] == qseg
     if causal:
-        keys = key_at + lax.broadcasted_iota(jnp.int32, (BLOCK, BLOCK), 0)
-        queries = query_at + lax.broadcasted_iota(jnp.int32, (BLOCK, BLOCK), 1)
+        keys = key_at + lax.broadcasted_iota(jnp.int32, (ROWS, BLOCK), 0)
+        queries = query_at + lax.broadcasted_iota(jnp.int32, (ROWS, BLOCK), 1)
         allowed = allowed & (keys <= queries) & ((keys < length) | (keys == queries))
     return allowed
 
@@ -149,6 +150,7 @@
     top_ref,
     sum_ref,
     qt_ref,
+    e_ref,
 ):
     block = pl.program_id(1)
     blocks = k_ref.shape[0] // BLOCK
@@ -169,11 +171,17 @@
         @pl.when(info_ref[block * blocks + j] > 0)
         def _(j=j):
             keys = k_ref[j * BLOCK : (j + 1) * BLOCK, :]
-            allowed = allowed_block(causal, kseg_ref, qseg, length, j * BLOCK, block * BLOCK)
             for h in range(HEADS):
-                scores = jnp.where(allowed, dot_nn(keys, qt_ref[h]), MASKED)
-                s_ref[h, j * BLOCK : (j + 1) * BLOCK, :] = scores
-                top_ref[h] = jnp.maximum(top_ref[h], fold_rows(scores, jnp.max))
+                s_ref[h, j * BLOCK : (j + 1) * BLOCK, :] = dot_nn(keys, qt_ref[h])
+            top = [top_ref[h] for h in range(HEADS)]
+            for at in range(j * BLOCK, (j + 1) * BLOCK, ROWS):
+                allowed = allowed_rows(causal, kseg_ref, qseg, length, at, block * BLOCK)
+                for h in range(HEADS):
+                    scores = jnp.where(allowed, s_ref[h, at : at + ROWS, :], MASKED)
+                    s_ref[h, at : at + ROWS, :] = scores
+                    top[h] = jnp.maximum(top[h], fold_rows(scores, jnp.max))
+            for h in range(HEADS):
+                top_ref[h] = top[h]
 
     highest = [jnp.max(top_ref[h], axis=0, keepdims=True) for h in range(HEADS)]
     for j in range(blocks):
@@ -181,14 +189,14 @@
         @pl.when(info_ref[block * blocks + j] > 0)
         def _(j=j):
             for h in range(HEADS):
-                weights = jnp.exp(s_ref[h, j * BLOCK : (j + 1) * BLOCK, :] - highest[h])
-                sum_ref[h] += fold_rows(weights, jnp.sum)
+                total = sum_ref[h]
+                for at in range(0, BLOCK, ROWS):
+                    weights = jnp.exp(s_ref[h, j * BLOCK + at : j * BLOCK + at + ROWS, :] - highest[h])
+                    total = total + fold_rows(weights, jnp.sum)
+                    e_ref[h, at : at + ROWS, :] = weights.astype(B16)
+                sum_ref[h] = total
                 rows = slice(h * HEAD_DIM, (h + 1) * HEAD_DIM)
-                acc_ref[rows, :] += jnp.dot(
-                    vt_ref[rows, j * BLOCK : (j + 1) * BLOCK],
-                    weights.astype(B16),
-                    preferred_element_type=F32,
-                )
+                acc_ref[rows, :] += dot_nn(vt_ref[rows, j * BLOCK : (j + 1) * BLOCK], e_ref[h])
 
     lse_ref[...] = jnp.zeros_like(lse_ref)
     for h in range(HEADS):
@@ -212,7 +220,7 @@
     kseg_ref,
     *rest,
 ):
-    *outs, kt_ref, dqt_ref, sums_ref, done_ref, qt_ref, dot_ref, sems = rest
+    *outs, kt_ref, dqt_ref, sums_ref, done_ref, qt_ref, dot_ref, s_ref, dp_ref, p_ref, ds_ref, sems = rest
     group, block = pl.program_id(0), pl.program_id(1)
     groups = pl.num_programs(0)
     blocks = k_ref.shape[0] // BLOCK
@@ -246,23 +254,22 @@
             rows = slice(j * BLOCK, (j + 1) * BLOCK)
             keys = k_ref[rows, :]
             values = v_ref[rows, :]
-            allowed = allowed_block(causal, kseg_ref, qseg, length, j * BLOCK, block * BLOCK)
-            all_chances, all_scores = [], []
             for h in range(HEADS):
-                scores = dot_nn(keys, qt_ref[h])
-                chances = jnp.where(allowed, jnp.exp(scores - lse_ref[0, h : h + 1, :]), 0.0)
-                grad_chances = dot_nn(values, dot_ref[h])
-                grad_scores = (chances * (grad_chances - inner[h])).astype(B16)
-                all_chances.append(chances.astype(B16))
-                all_scores.append(grad_scores)
+                s_ref[h] = dot_nn(keys, qt_ref[h])
+                dp_ref[h] = dot_nn(values, dot_ref[h])
+            for at in range(0, BLOCK, ROWS):
+                here = slice(at, at + ROWS)
+                allowed = allowed_rows(causal, kseg_ref, qseg, length, j * BLOCK + at, block * BLOCK)
+                for h in range(HEADS):
+                    lanes = slice(h * BLOCK, (h + 1) * BLOCK)
+                    chances = jnp.where(allowed, jnp.exp(s_ref[h, here, :] - lse_ref[0, h : h + 1, :]), 0.0)
+                    p_ref[here, lanes] = chances.astype(B16)
+                    ds_ref[here, lanes] = (chances * (dp_ref[h, here, :] - inner[h])).astype(B16)
+            for h in range(HEADS):
                 part = slice(h * HEAD_DIM, (h + 1) * HEAD_DIM)
-                dqt_ref[part, :] += jnp.dot(kt_ref[part, rows], grad_scores, preferred_element_type=F32)
-            sums_ref[0, rows, :] += jnp.dot(
-                jnp.concatenate(all_scores, axis=1), queries_down, preferred_element_type=F32
-            )
-            sums_ref[1, rows, :] += jnp.dot(
-                jnp.concatenate(all_chances, axis=1), grads_down, preferred_element_type=F32
-            )
+                dqt_ref[part, :] += dot_nn(kt_ref[part, rows], ds_ref[:, h * BLOCK : (h + 1) * BLOCK])
+            sums_ref[0, rows, :] += dot_nn(ds_ref[...], queries_down)
+            sums_ref[1, rows, :] += dot_nn(p_ref[...], grads_down)
 
     here = pl.ds(pl.multiple_of(block * BLOCK, BLOCK), BLOCK)
     done_ref[0, here, :] = (dqt_ref[...].T * HEAD_DIM**-0.5).astype(B16)
@@ -320,13 +327,13 @@
             out_specs=[plain, stats],
             scratch_shapes=[pltpu.VMEM((GROUP, count), B16), pltpu.VMEM((HEADS, count, BLOCK), F32), pltpu.VMEM((GROUP, BLOCK), F32)]
             + [pltpu.VMEM((HEADS, 8, BLOCK), F32)] * 2
-            + [pltpu.VMEM((HEADS, GROUP, BLOCK), B16)],
+            + [pltpu.VMEM((HEADS, GROUP, BLOCK), B16), pltpu.VMEM((HEADS, BLOCK, BLOCK), B16)],
         ),
         out_shape=[
             jax.ShapeDtypeStruct((count, width), B16),
             jax.ShapeDtypeStruct((groups, 8, count), F32),
         ],
-        compiler_params=pltpu.CompilerParams(vmem_limit_bytes=24 * 2**20),
+        compiler_params=pltpu.CompilerParams(vmem_limit_bytes=20 * 2**20),
         cost_estimate=pl.CostEstimate(
             flops=2 * 2 * count * count * width * 2, bytes_accessed=count * width * 8, transcendentals=0
         ),
@@ -354,11 +361,15 @@
                 pltpu.VMEM((3, count, GROUP), B16),
                 pltpu.VMEM((HEADS, GROUP, BLOCK), B16),
                 pltpu.VMEM((HEADS, GROUP, BLOCK), B16),
+                pltpu.VMEM((HEADS, BLOCK, BLOCK), F32),
+                pltpu.VMEM((HEADS, BLOCK, BLOCK), F32),
+                pltpu.VMEM((BLOCK, HEADS * BLOCK), B16),
+                pltpu.VMEM((BLOCK, HEADS * BLOCK), B16),
                 pltpu.SemaphoreType.DMA((3,)),
             ],
         ),
         out_shape=[jax.ShapeDtypeStruct((count, w), B16) for w in widths],
-        compiler_params=pltpu.CompilerParams(vmem_limit_bytes=24 * 2**20),
+        compiler_params=pltpu.CompilerParams(vmem_limit_bytes=20 * 2**20),
         cost_estimate=pl.CostEstimate(
             flops=5 * 2 * count * count * width * 2, bytes_accessed=count * width * 16, transcendentals=0
         ),

time: 916 us -> 900 us (0.983)
  Pallas kernels: 589 us -> 569 us
  matrix products: 166 us -> 152 us
  waiting for transfers between devices: 10.4 us -> 23.7 us
    pallas_call x3, Pallas kernels: 83.2 us -> 58.5 us  [attend_backward(): pl.pallas_call(functools.partial(backward_kernel, causal), grid_spec=pltp...]
    all_gather x1, waiting for transfers between devices: 5.92 us -> 19.6 us  [gather_late(): full = lax.all_gather(local, ('dp', 'seq'), axis=0, tiled=False)]
    dot_general x13, matrix products: 58.5 us -> 48.1 us  [product(): return jnp.dot(left, right, preferred_element_type=F32)]
    unnamed x284 -> x254, local copies, waits for them, and re-layouts: 49.8 us -> 53.1 us
  transfers between devices with their start and end apart: 19 -> 19, of which waited for: 3 -> 3; matrix products, arithmetic and copies ran while one was open for 23% -> 22% of each run, Pallas kernels for 65% -> 64%
where the time goes in v5:
time: 900 us; the launch traced here: 892 us
  Pallas kernels  569 us (63%)
  matrix products  152 us (17%)
  local copies, waits for them, and re-layouts  83.9 us (9%)
  other arithmetic  43.5 us (5%)
  waiting for transfers between devices  23.7 us (3%)
  between operations  16 us (2%)
    pallas_call x1, Pallas kernels, gather_all(): pl.pallas_call(kernel, in_specs=[hbm] * len(inputs), out_specs=[hbm] * le...  235 us
    pallas_call x1, Pallas kernels, sum_all(): pl.pallas_call(kernel, in_specs=[hbm] * (len(grads) + tensors), out_specs...  206 us
    pallas_call x3, Pallas kernels, attend_backward(): pl.pallas_call(functools.partial(backward_kernel, causal), grid_spec=pltp...  58.5 us
    unnamed x254, local copies, waits for them, and re-layouts  53.1 us
    dot_general x11, matrix products, product_nt(): lax.dot_general(left, right, (((1,), (1,)), ((), ())), preferred_element_...  52.3 us
    dot_general x11, matrix products, product_tn(): lax.dot_general(left, right, (((0,), (0,)), ((), ())), preferred_element_...  52 us
    dot_general x13, matrix products, product(): return jnp.dot(left, right, preferred_element_type=F32)  48.1 us
    pallas_call x3, Pallas kernels, attend_forward(): pl.pallas_call(functools.partial(forward_kernel, causal), grid_spec=pltpu...  38.3 us
  transfers between devices with their start and end apart: 19, of which 3 were waited for; matrix products, arithmetic and copies ran while one was open for 22% of the time, Pallas kernels for 64%

profile of v5, /device:TPU:0, one launch (start us, length us, event | category | flops | bytes accessed | tf_op | source)
XLA Modules:
  0.0 892.4 jit_solution(10770992853856251617)
XLA Ops:
  13.9 235.0 %gather_all.1 = (bf16[2,2,2,4,48,128]{5,4,3,2,1,0:T(8,128)(2,1)}, bf16[2,2,2,4,32,1536]{5,4,3,2,1,0:T(8,128)(2,1)}, bf16[2,2,1,4,32,1024]{5,4,3,2,1,0:T(8,128)(2...) custom-call(bf16[1,48,128]{2,1,0:T(8,128)(2,1)} %fusion.27.refs_0_, ...), custom_call_target="tpu_custom_call" | custom-call | tf_op jit(solution)/shard_map/gather_all/pallas_call | solution.py:636
  269.0 13.3 %attend.2 = (bf16[1024,512]{1,0:T(8,128)(2,1)S(1)}, f32[2,8,1024]{2,1,0:T(8,128)S(1)}) custom-call(s32[17]{0:T(128)S(1)} %get-tuple-element.272.info_ref, bf16[1024,1536]{1,0:T(8,128)(2,1)S(1)} %copy-done.58, bf16[1024,1536]{1,0:T(8,128)(2,1)S(1)} %copy-done.58, bf16[1024,1536]{1,0:T(8,128)(2,1)S(1)} %copy-done.58, ...), custom_call_target="tpu_custom_call" | custom-call | flops 4294967296 | bytes 4194304 | tf_op jit(solution)/shard_map/attend/pallas_call | solution.py:321
  292.9 11.4 %attend_causal.1 = (bf16[1024,512]{1,0:T(8,128)(2,1)S(1)}, f32[2,8,1024]{2,1,0:T(8,128)S(1)}) custom-call(s32[17]{0:T(128)S(1)} %get-tuple-element.271.info_ref, bf16[1024,1536]{1,0:T(8,128)(2,1)S(1)} %add_convert_fusion.1.q_ref.k_ref.v_ref, bf16[1024,1536]{1,0:T(8,128)(2,1)S(1)} %add_convert_fusion.1.q_ref.k_ref.v_ref, ...), custom_call_target="tpu_custom_call" | custom-call | flops 4294967296 | bytes 4194304 | tf_op jit(solution)/shard_map/attend_causal/pallas_call | solution.py:321
  312.2 7.2 multiply_convert_fusion.3
  335.5 13.6 %attend.3 = (bf16[1024,512]{1,0:T(8,128)(2,1)S(1)}, f32[2,8,1024]{2,1,0:T(8,128)S(1)}) custom-call(s32[17]{0:T(128)S(1)} %pad_add_fusion.1.info_ref, bf16[1024,512]{1,0:T(8,128)(2,1)S(1)} %add_convert_fusion.10.q_ref, bf16[1024,1024]{1,0:T(8,128)(2,1)S(1)} %add_convert_fusion.4.k_ref.v_ref, bf16[1024,1024]{1,0:T(8,128)(2,1)S(1)} %add_convert_fusion.4.k_ref.v_ref, ...), custom_call_target="tpu_custom_call" | custom-call | flops 4294967296 | bytes 4194304 | tf_op jit(solution)/shard_map/attend/pallas_call | solution.py:321
  359.6 19.6 %all-gather.3.cloned.1.call-done = bf16[4096,1024]{1,0:T(8,128)(2,1)} async-done(((bf16[256,1024]{1,0:T(8,128)(2,1)}), bf16[4096,1024]{1,0:T(8,128)(2,1)}) %all-gather.3.cloned.1.call-update) | async-done | bytes 8388624 | tf_op jit(solution)/shard_map/all_gather | solution.py:951
  387.5 7.2 multiply_convert_fusion.1
  394.8 7.9 convert_reduce_fusion
  410.1 8.8 convolution_convert_fusion.5
  418.9 9.3 %fusion.12.mine_ref = bf16[1024,1024]{1,0:T(8,128)(2,1)} fusion(bf16[1024,2048]{1,0:T(8,128)(2,1)} %copy-done.118, bf16[1024,1024]{1,0:T(8,128)(2,1)} %bitcast.298, bf16[1024,1024]{1,0:T(8,128)(2,1)} %bitcast.296), kind=kOutput, calls=%fused_computation.57 | convolution fusion | flops 4304404480 | bytes 10485760 | tf_op jit(solution)/shard_map/dot_general | solution.py:31
  430.3 9.4 %convolution_convert_fusion.7 = bf16[1024,1024]{1,0:T(8,128)(2,1)} fusion(bf16[1024,2048]{1,0:T(8,128)(2,1)} %get-tuple-element.265, bf16[2048,1024]{1,0:T(8,128)(2,1)} %bitcast.280), kind=kOutput, calls=%fused_computation.59 | convolution fusion | flops 4296015872 | bytes 10485760 | tf_op jit(solution)/shard_map/dot_general | solution.py:23
  440.2 5.8 norm_grad.3
  450.7 20.5 %attend_grad.2 = (bf16[1024,512]{1,0:T(8,128)(2,1)S(1)}, bf16[1024,1024]{1,0:T(8,128)(2,1)S(1)}) custom-call(s32[17]{0:T(128)S(1)} %pad_add_fusion.1.info_ref, bf16[1024,512]{1,0:T(8,128)(2,1)S(1)} %copy-done.63, bf16[1024,1024]{1,0:T(8,128)(2,1)S(1)} %copy-done.65, bf16[1024,1024]{1,0:T(8,128)(2,1)S(1)} %copy-done.65, bf16[1024,512]{1,0:T(8,128)(2,1)S(1)} %copy-done.37, ...), custom_call_target="tpu_custom_call" | custom-call | flops 10737418240 | bytes 8388608 | tf_op jit(solution)/shard_map/attend_grad/pallas_call | solution.py:350
  493.7 6.1 add_convert_fusion.2
  503.7 11.2 %convert_reduce_fusion.1 = (f32[2048]{0:T(1024)S(1)}, bf16[1024,2048]{1,0:T(8,128)(2,1)S(1)}) fusion(f32[1024,2048]{1,0:T(8,128)} %get-tuple-element.264, f32[2048]{0:T(1024)S(1)} %bitcast.333, bf16[2048,1024]{1,0:T(8,128)(2,1)S(1)} %bitcast.343, f32[1024,1024]{1,0:T(8,128)S(1)} %get-tuple-element.173.grad_ref), kind=kOutput, calls=%fused_computation.13 | convolution fusion | flops 4327471104 | bytes 20987904 | tf_op jit(solution)/shard_map/dot_general | solution.py:31
  520.9 6.3 convolution_convert_fusion.3
  527.2 5.8 norm_grad.4
  537.6 17.7 %attend_grad_causal.1 = bf16[1024,1536]{1,0:T(8,128)(2,1)S(1)} custom-call(s32[17]{0:T(128)S(1)} %copy-done.57, bf16[1024,1536]{1,0:T(8,128)(2,1)S(1)} %copy-done.61, bf16[1024,1536]{1,0:T(8,128)(2,1)S(1)} %copy-done.61, bf16[1024,1536]{1,0:T(8,128)(2,1)S(1)} %copy-done.61, bf16[1024,512]{1,0:T(8,128)(2,1)S(1)} %copy-done.35, ...), custom_call_target="tpu_custom_call" | custom-call | flops 10737418240 | bytes 8388608 | tf_op jit(solution)/shard_map/attend_grad_causal/pallas_call | solution.py:350
  569.1 8.6 convolution_convert_fusion.2
  577.7 6.0 norm_grad.5
  588.4 20.3 %attend_grad.3 = bf16[1024,1536]{1,0:T(8,128)(2,1)S(1)} custom-call(s32[17]{0:T(128)S(1)} %copy-done.55, bf16[1024,1536]{1,0:T(8,128)(2,1)S(1)} %copy-done.59, bf16[1024,1536]{1,0:T(8,128)(2,1)S(1)} %copy-done.59, bf16[1024,1536]{1,0:T(8,128)(2,1)S(1)} %copy-done.59, bf16[1024,512]{1,0:T(8,128)(2,1)S(1)} %copy-done.32, ...), custom_call_target="tpu_custom_call" | custom-call | flops 10737418240 | bytes 8388608 | tf_op jit(solution)/shard_map/attend_grad/pallas_call | solution.py:350
  625.4 6.5 norm_last.3
  641.0 6.7 norm_last.2
  651.5 206.1 %sum_all.1 = (f32[32,1024]{1,0:T(8,128)}, f32[3,32,1024]{2,1,0:T(8,128)}, f32[1,32,4096]{2,1,0:T(8,128)}, f32[128,1024]{1,0:T(8,128)}, f32[3,32,1024]{2,1,0:T(8,...) custom-call(bf16[2,2,1,4,32,1024]{5,4,3,2,1,0:T(8,128)(2,1)} %bitcas, ...), custom_call_target="tpu_custom_call" | custom-call | tf_op jit(solution)/shard_map/sum_all/pallas_call | solution.py:882
  (461 shorter events, 206.0 us)
Async XLA Ops:
  7.2 372.1 %all-gather.3.cloned.1.call-start = ((), (), s32[]{:S(2)}) async-start(), calls=%async_computation.6 | async-start | bytes 8912896 | tf_op jit(solution)/shard_map/all_gather | solution.py:951
  8.8 243.1 %collective-permute-start = (s32[2,2057]{1,0:T(2,128)S(1)}, s32[2,2057]{1,0:T(2,128)S(1)}, u32[]{:S(2)}, u32[]{:S(2)}) collective-permute-start(s32[2,2057]{1,0:T(2,128)S(1)} %concatenate.93), channel_id=1, source_target_pairs={{0,4},{4,0},{1,5},{5,1},{2,6},{6,2},{3,7},{7,3},{8,12},{12,8},{9,1... | collective-permute-start | bytes 49376 | tf_op jit(solution)/shard_map/ppermute | solution.py:909
  10.2 253.7 %collective-permute-start.5 = (bf16[32,2048]{1,0:T(8,128)(2,1)S(1)}, bf16[32,2048]{1,0:T(8,128)(2,1)S(1)}, u32[]{:S(2)}, u32[]{:S(2)}) collective-permute-start(bf16[32,2048]{1,0:T(8,128)(2,1)S(1)} %maximum_bitcast_fusion), channel_id=1, source_target_pairs={{0,4},{4,0},{1,5},{5,1},{2,6},{6,2},{3,7},{7,3},{8,12},{12,8},{9,1... | collective-permute-start | bytes 393224 | tf_op jit(solution)/shard_map/ppermute | solution.py:909
  251.7 34.1 %copy-start.46 = (f32[1,1024]{1,0:T(1,128)}, f32[1,1024]{1,0:T(1,128)S(1)}, u32[]{:S(2)}) copy-start(f32[1,1024]{1,0:T(1,128)S(1)} %get-tuple-element.198.gain_ref) | copy-start | bytes 12292
  251.7 56.8 %copy-start.48 = (f32[1,1024]{1,0:T(1,128)}, f32[1,1024]{1,0:T(1,128)S(1)}, u32[]{:S(2)}) copy-start(f32[1,1024]{1,0:T(1,128)S(1)} %get-tuple-element.187.gain_ref) | copy-start | bytes 12292
  251.7 75.3 %copy-start.50 = (f32[1,1024]{1,0:T(1,128)}, f32[1,1024]{1,0:T(1,128)S(1)}, u32[]{:S(2)}) copy-start(f32[1,1024]{1,0:T(1,128)S(1)} %get-tuple-element.192.gain_ref) | copy-start | bytes 12292
  264.8 602.7 %reduce-scatter.6.cloned.1.call-start = ((), (), s32[]{:S(2)}) async-start(), calls=%async_computation.4 | async-start | bytes 4456448 | tf_op jit(solution)/shard_map/reduce_scatter | solution.py:967
  266.1 69.3 %copy-start.39 = (s32[1024,1]{1,0:T(8,128)}, s32[1024,1]{1,0:T(8,128)S(1)}, u32[]{:S(2)}) copy-start(s32[1024,1]{1,0:T(8,128)S(1)} %copy.100.kseg_ref) | copy-start | bytes 12292
  283.6 22.1 %collective-permute-start.2 = (bf16[1024,1024]{1,0:T(8,128)(2,1)S(1)}, bf16[1024,1024]{1,0:T(8,128)(2,1)S(1)}, u32[]{:S(2)}, u32[]{:S(2)}) collective-permute-start(bf16[1024,1024]{1,0:T(8,128)(2,1)S(1)} %convolution_convert_fusion.15), channel_id=1, source_target_pairs={{0,4},{4,0},{1,5},{5,1},{2,6},{6,2},{3,7},{7,3},{8,12},{12,8},{9,1... | collective-permute-start | bytes 6291464 | tf_op jit(solution)/shard_map/ppermute | solution.py:909
  285.1 40.3 %copy-start.3 = (f32[1024,1024]{1,0:T(8,128)}, f32[1024,1024]{1,0:T(8,128)S(1)}, u32[]{:S(2)}) copy-start(f32[1024,1024]{1,0:T(8,128)S(1)} %get-tuple-element.260.h_ref) | copy-start | bytes 12582916
  305.7 19.8 %collective-permute-start.1 = (bf16[1024,1024]{1,0:T(8,128)(2,1)S(1)}, bf16[1024,1024]{1,0:T(8,128)(2,1)S(1)}, u32[]{:S(2)}, u32[]{:S(2)}) collective-permute-start(bf16[1024,1024]{1,0:T(8,128)(2,1)S(1)} %convolution_convert_fusion.16), channel_id=1, source_target_pairs={{0,4},{4,0},{1,5},{5,1},{2,6},{6,2},{3,7},{7,3},{8,12},{12,8},{9,1... | collective-permute-start | bytes 6291464 | tf_op jit(solution)/shard_map/ppermute | solution.py:909
  324.6 7.2 collective-permute-start.3
  350.4 4.3 collective-permute-start.4
  410.0 459.1 %reduce-scatter.8.cloned.1.call-start = ((), (), s32[]{:S(2)}) async-start(), calls=%async_computation.5 | async-start | bytes 4456448 | tf_op jit(solution)/shard_map/reduce_scatter | solution.py:996
  418.9 455.2 %reduce-scatter.4.cloned.1.call-start = ((), (), s32[]{:S(2)}) async-start(), calls=%async_computation.3 | async-start | bytes 4456448 | tf_op jit(solution)/shard_map/reduce_scatter | solution.py:984
  428.3 12.0 %collective-permute-start.6 = (bf16[1024,1024]{1,0:T(8,128)(2,1)}, bf16[1024,1024]{1,0:T(8,128)(2,1)}, u32[]{:S(2)}, u32[]{:S(2)}) collective-permute-start(bf16[1024,1024]{1,0:T(8,128)(2,1)} %fusion.12.mine_ref), channel_id=1, source_target_pairs={{0,4},{4,0},{1,5},{5,1},{2,6},{6,2},{3,7},{7,3},{8,12},{12,8},{9,1... | collective-permute-start | bytes 6291464 | tf_op jit(solution)/shard_map/ppermute | solution.py:909
  439.7 54.0 %collective-permute-start.12 = (bf16[1024,1024]{1,0:T(8,128)(2,1)}, bf16[1024,1024]{1,0:T(8,128)(2,1)}, u32[]{:S(2)}, u32[]{:S(2)}) collective-permute-start(bf16[1024,1024]{1,0:T(8,128)(2,1)} %convolution_convert_fusion.7), channel_id=1, source_target_pairs={{0,4},{4,0},{1,5},{5,1},{2,6},{6,2},{3,7},{7,3},{8,12},{12,8},{9,1... | collective-permute-start | bytes 6291464 | tf_op jit(solution)/shard_map/ppermute | solution.py:909
  485.6 14.2 %collective-permute-start.8 = (bf16[1024,1024]{1,0:T(8,128)(2,1)}, bf16[1024,1024]{1,0:T(8,128)(2,1)}, u32[]{:S(2)}, u32[]{:S(2)}) collective-permute-start(bf16[1024,1024]{1,0:T(8,128)(2,1)} %convolution_convert_fusion.11), channel_id=1, source_target_pairs={{0,4},{4,0},{1,5},{5,1},{2,6},{6,2},{3,7},{7,3},{8,12},{12,8},{9,1... | collective-permute-start | bytes 6291464 | tf_op jit(solution)/shard_map/ppermute | solution.py:909
  487.1 40.1 %collective-permute-start.7 = (bf16[1024,1024]{1,0:T(8,128)(2,1)S(1)}, bf16[1024,1024]{1,0:T(8,128)(2,1)}, u32[]{:S(2)}, u32[]{:S(2)}) collective-permute-start(bf16[1024,1024]{1,0:T(8,128)(2,1)S(1)} %convolution_convert_fusion.12.mine_ref), channel_id=1, source_target_pairs={{0,4},{4,0},{1,5},{5,1},{2,6},{6,2},{3,7},{7,3},{8,12},{12,8},{9,1... | collective-permute-start | bytes 6291464 | tf_op jit(solution)/shard_map/ppermute | solution.py:909
  520.8 57.0 %collective-permute-start.9 = (bf16[1024,1024]{1,0:T(8,128)(2,1)}, bf16[1024,1024]{1,0:T(8,128)(2,1)}, u32[]{:S(2)}, u32[]{:S(2)}) collective-permute-start(bf16[1024,1024]{1,0:T(8,128)(2,1)} %convolution_convert_fusion.10.mine_ref), channel_id=1, source_target_pairs={{0,4},{4,0},{1,5},{5,1},{2,6},{6,2},{3,7},{7,3},{8,12},{12,8},{9,1... | collective-permute-start | bytes 6291464 | tf_op jit(solution)/shard_map/ppermute | solution.py:909
  564.3 55.1 %collective-permute-start.11 = (bf16[1024,1024]{1,0:T(8,128)(2,1)}, bf16[1024,1024]{1,0:T(8,128)(2,1)}, u32[]{:S(2)}, u32[]{:S(2)}) collective-permute-start(bf16[1024,1024]{1,0:T(8,128)(2,1)} %convolution_convert_fusion.8.mine_ref), channel_id=1, source_target_pairs={{0,4},{4,0},{1,5},{5,1},{2,6},{6,2},{3,7},{7,3},{8,12},{12,8},{9,1... | collective-permute-start | bytes 6291464 | tf_op jit(solution)/shard_map/ppermute | solution.py:909
  613.4 27.5 %collective-permute-start.10 = (bf16[1024,1024]{1,0:T(8,128)(2,1)}, bf16[1024,1024]{1,0:T(8,128)(2,1)}, u32[]{:S(2)}, u32[]{:S(2)}) collective-permute-start(bf16[1024,1024]{1,0:T(8,128)(2,1)} %convolution_convert_fusion.9.mine_ref), channel_id=1, source_target_pairs={{0,4},{4,0},{1,5},{5,1},{2,6},{6,2},{3,7},{7,3},{8,12},{12,8},{9,1... | collective-permute-start | bytes 6291464 | tf_op jit(solution)/shard_map/ppermute | solution.py:909
  868.4 2.5 collective-permute-start.14
  876.2 1.5 collective-permute-start.13
  (115 other events, 754.1 us)
Sparse Core Ops, SparseCore 0:
  264.9 114.2 all-gather.2
  410.1 94.5 reduce-scatter.5
  507.0 94.6 reduce-scatter.7
  603.8 109.5 reduce-scatter.3

commit v6 on v5

--- a/solution.py
+++ b/solution.py
@@ -105,6 +105,57 @@
     below = 0.5 * (1.0 + lax.erf(values * (0.5**0.5)))
     density = jnp.exp(-0.5 * values * values) * (0.5 / jnp.pi) ** 0.5
     return (values * below).astype(B16), (below + values * density).astype(B16)
+
+
+def ffn_backward_kernel(
+    grad_ref, normed_ref, acted_ref, slope_ref, in_ref, out_ref, down_ref, in_grad_ref, out_grad_ref, sums_ref, acc_ref, up_ref
+):
+    step = pl.program_id(0)
+
+    @pl.when(step == 0)
+    def _():
+        up_ref[...] = normed_ref[...].T
+        acc_ref[...] = jnp.zeros_like(acc_ref)
+
+    grad = grad_ref[...]
+    inner = product_nt(grad, out_ref[...]) * slope_ref[...].astype(F32)
+    low = inner.astype(B16)
+    sums_ref[...] = jnp.sum(low.astype(F32), axis=0, keepdims=True)
+    out_grad_ref[...] = product_tn(acted_ref[...], grad).astype(B16)
+    in_grad_ref[...] = product(up_ref[...], low).astype(B16)
+    acc_ref[...] += product_nt(low, in_ref[...])
+
+    @pl.when(step == pl.num_programs(0) - 1)
+    def _():
+        down_ref[...] = acc_ref[...].astype(B16)
+
+
+def ffn_backward(grad, normed, acted, slope, w_in, w_out):
+    count, width = grad.shape
+    hidden = acted.shape[1]
+    cut = 256
+    still = pl.BlockSpec((count, width), lambda i: (0, 0))
+    tall = pl.BlockSpec((count, cut), lambda i: (0, i))
+    side = pl.BlockSpec((width, cut), lambda i: (0, i))
+    flat = pl.BlockSpec((cut, width), lambda i: (i, 0))
+    return pl.pallas_call(
+        ffn_backward_kernel,
+        grid=(hidden // cut,),
+        in_specs=[still, still, tall, tall, side, flat],
+        out_specs=[still, side, flat, pl.BlockSpec((1, cut), lambda i: (0, i))],
+        out_shape=[
+            jax.ShapeDtypeStruct((count, width), B16),
+            jax.ShapeDtypeStruct((width, hidden), B16),
+            jax.ShapeDtypeStruct((hidden, width), B16),
+            jax.ShapeDtypeStruct((1, hidden), F32),
+        ],
+        scratch_shapes=[pltpu.VMEM((count, width), F32), pltpu.VMEM((width, count), B16)],
+        compiler_params=pltpu.CompilerParams(vmem_limit_bytes=40 * 2**20),
+        cost_estimate=pl.CostEstimate(
+            flops=8 * count * width * hidden, bytes_accessed=8 * width * hidden + 4 * count * hidden, transcendentals=0
+        ),
+        name="ffn_grad",
+    )(grad, normed, acted, slope, w_in, w_out)
 
 
 def allowed_rows(causal, kseg_ref, qseg, length, key_at, query_at):
@@ -933,23 +984,26 @@
         keys = sorted(sources)
         outs = gather_all([sources[key] for key in keys], tensors, tensors_at)
         whole = {key: out for key, out in zip(keys, outs)}
-        small = whole.pop(-1)
+        small = self.gathered = whole.pop(-1)
         table = small[..., :r, :].reshape(-1, 128).astype(F32).T
         ffb = small[..., r : r + ffb.shape[0], :].reshape(32, ffb.shape[0], -1).transpose(1, 0, 2)
         weights = {key: value.reshape(-1, value.shape[-1]) for key, value in whole.items()}
         return table, ffb.reshape(ffb.shape[0], -1), weights, [out.reshape(-1, out.shape[-1]) for out in outs[len(keys) :]]
 
-    def gather_late(self, columns, rows, after):
+    def prepare_late(self, columns, rows):
         core = self.place.core
         mine, other = lay_side(own_columns(columns, core)), lay_side(own_columns(columns, 1 - core))
         both = jnp.stack(xor_arrange([mine, self.place.over_core(other)], core))
         width = rows.shape[1]
         wide = both.shape[2] // width
         parts = [both[:, :, k * width : (k + 1) * width].reshape(-1, width) for k in range(wide)]
-        local = jnp.concatenate(parts + [rows], axis=0)
-        local, _ = lax.optimization_barrier((local, after))
+        return jnp.concatenate(parts + [rows], axis=0)
+
+    def gather_late(self, local):
+        width, wide = local.shape[1], 2
+        local, _ = lax.optimization_barrier((local, self.gathered))
         full = lax.all_gather(local, ("dp", "seq"), axis=0, tiled=False)
-        r = parts[0].shape[0]
+        r = local.shape[0] // (2 * wide)
         first = [full[:, k * r : (k + 1) * r].reshape(4, 4, 2, -1, width) for k in range(wide)]
         first = [part.transpose(0, 2, 1, 3, 4).reshape(-1, width) for part in first]
         return lay_wide(first), full[:, wide * r :].reshape(-1, width)
@@ -1012,16 +1066,14 @@
         size = both.shape[-1]
         both = jnp.pad(both, ((0, 0), (0, 0), (0, 0), (0, -size % 2048))).reshape(2, 2, 1, 4, 8, -1)
         grads, keys = [], []
-        for key, (features, grad, _) in columns.items():
-            value = product_tn(features, grad).astype(B16)
+        for key, (value, _) in columns.items():
             grads.append(value.reshape(2, 2, 2, 4, value.shape[0] // 32, value.shape[1]))
             keys.append(key)
-        for key, (features, grad) in rows.items():
-            value = product_tn(features, grad).astype(B16)
+        for key, value in rows.items():
             grads.append(value.reshape(2, 2, 1, 4, value.shape[0] // 16, value.shape[1]))
             keys.append(key)
         order = sorted(range(len(keys)), key=lambda k: keys[k])
-        parts = [columns[keys[k]][2] if keys[k] in columns else 1 for k in order] + [1]
+        parts = [columns[keys[k]][1] if keys[k] in columns else 1 for k in order] + [1]
         outs = sum_all([grads[k] for k in order] + [both], parts, [t.reshape(4, -1, t.shape[-1]) for t in tensors], SUM_ROWS)
         result = {}
         for k, out in zip(order, outs):
@@ -1090,7 +1142,11 @@
         mine = lax.dynamic_index_in_dim(split, self.place.core, 1, keepdims=False)
         return mine.reshape(-1, full.shape[1])
 
-    def gather_late(self, columns, rows, after):
+    def prepare_late(self, columns, rows):
+        return columns, rows
+
+    def gather_late(self, prepared):
+        columns, rows = prepared
         return self.whole_columns(columns), self.whole_rows(rows)
 
     def full_columns(self, pairs):
@@ -1123,10 +1179,10 @@
 
     def sums(self, columns, rows, table, hidden, tensors):
         result = {}
-        for key, (features, grad, parts) in columns.items():
-            result[key] = self.early_columns(self.full_columns([(features, grad)]), parts)
-        for key, (features, grad) in rows.items():
-            result[key] = self.early_rows(self.full_rows(features, grad))
+        for key, (value, parts) in columns.items():
+            result[key] = self.early_columns(value, parts)
+        for key, value in rows.items():
+            result[key] = self.early_rows(value)
         small = [self.scatter(self.spread(v, 1), 1) for v in (table, hidden)]
         return result, small[0], small[1], [self.row_out(tensor) for tensor in tensors]
 
@@ -1164,6 +1220,8 @@
     langs = lang_table.shape[0]
 
     table = jnp.concatenate([lang_table, gains, biases], axis=0)
+    late = moves.prepare_late(dec_in[None], dec_out)
+    table, late = lax.optimization_barrier((table, late))
     table, ffb, weights, tensors = moves.gather(
         table,
         ff_biases,
@@ -1176,7 +1234,7 @@
     enc_qkv_w, enc_o_w, enc_in_w, enc_out_w, dec_qkv_w, dec_o_w, cross_w, cross_o_w = (
         weights[k] for k in range(8)
     )
-    dec_in_w, dec_out_w = moves.gather_late(dec_in[None], dec_out, ffb)
+    dec_in_w, dec_out_w = moves.gather_late(late)
     table, ffb_own = lax.optimization_barrier((table, own_columns(ffb, core).astype(F32)))
     languages = table[: langs + -langs % 16].astype(B16)
     gain_f = [table[langs + k : langs + k + 1] for k in range(5)]
@@ -1254,8 +1312,10 @@
 
     source_cot_f = source_cot.astype(F32) + grad_memory
     enc_ff_branch = source_cot_f.astype(B16)
-    enc_du = (product_nt(enc_ff_branch, enc_out_w) * enc_slope.astype(F32)).astype(B16)
-    enc_dn2 = place.both_parts(product_nt(enc_du, enc_in_w))
+    enc_down, enc_in_full, enc_out_full, enc_hidden = ffn_backward(
+        enc_ff_branch, enc_n2, enc_acted, enc_slope, enc_in_w, enc_out_w
+    )
+    enc_dn2 = place.both_parts(enc_down)
 
     grad_h1, self_branch, self_rows = norm_backward(dec_h1, gain_f[3], dec_dn2, grad_h2)
     dec_do = product_nt(self_branch, dec_o_w).astype(B16)
@@ -1286,17 +1346,17 @@
 
     grads, small, ffb_grad, outputs = moves.sums(
         {
-            1: (dec_n1, dec_dqkv, 3),
-            2: (enc_n2, enc_du, 1),
-            4: (enc_n1, enc_dqkv, 3),
+            1: (moves.full_columns([(dec_n1, dec_dqkv)]), 3),
+            2: (enc_in_full, 1),
+            4: (moves.full_columns([(enc_n1, enc_dqkv)]), 3),
         },
         {
-            0: (dec_mixed, self_branch),
-            3: (enc_acted, enc_ff_branch),
-            5: (enc_mixed, enc_branch),
+            0: moves.full_rows(dec_mixed, self_branch),
+            3: enc_out_full,
+            5: moves.full_rows(enc_mixed, enc_branch),
         },
         small_table,
-        jnp.stack([column_sum(enc_du), column_sum(dec_du)]),
+        jnp.concatenate([enc_hidden, column_sum(dec_du)[None]], axis=0),
         [memory, decoded.astype(B16), source_high, target_high],
     )
     picked = lambda places: jnp.concatenate([small[k : k + 1] for k in places], axis=0)

time: 900 us -> 891 us (0.990)
  Pallas kernels: 569 us -> 605 us
  matrix products: 152 us -> 122 us
  waiting for transfers between devices: 23.7 us -> 14.1 us
    pallas_call x0 -> x1, Pallas kernels: none -> 24.3 us  [ffn_backward(): pl.pallas_call(ffn_backward_kernel, grid=(hidden // cut,), in_specs=[stil...]
    dot_general x11 -> x9, matrix products: 52 us -> 35 us  [product_tn(): lax.dot_general(left, right, (((0,), (0,)), ((), ())), preferred_element_...]
    dot_general x11 -> x9, matrix products: 52.3 us -> 38.2 us  [product_nt(): lax.dot_general(left, right, (((1,), (1,)), ((), ())), preferred_element_...]
    all_gather x1, waiting for transfers between devices: 19.6 us -> 9.67 us  [gather_late(): full = lax.all_gather(local, ('dp', 'seq'), axis=0, tiled=False)]
    unnamed x254 -> x246, local copies, waits for them, and re-layouts: 53.1 us -> 46.7 us
  transfers between devices with their start and end apart: 19 -> 19, of which waited for: 3 -> 3; matrix products, arithmetic and copies ran while one was open for 22% -> 19% of each run, Pallas kernels for 64% -> 42%
where the time goes in v6:
time: 891 us; the launch traced here: 884 us
  Pallas kernels  605 us (68%)
  matrix products  122 us (14%)
  local copies, waits for them, and re-layouts  76.7 us (9%)
  other arithmetic  45.8 us (5%)
  between operations  15.9 us (2%)
  waiting for transfers between devices  14.1 us (2%)
    pallas_call x1, Pallas kernels, gather_all(): pl.pallas_call(kernel, in_specs=[hbm] * len(inputs), out_specs=[hbm] * le...  235 us
    pallas_call x1, Pallas kernels, sum_all(): pl.pallas_call(kernel, in_specs=[hbm] * (len(grads) + tensors), out_specs...  206 us
    pallas_call x3, Pallas kernels, attend_backward(): pl.pallas_call(functools.partial(backward_kernel, causal), grid_spec=pltp...  65.5 us
    dot_general x13, matrix products, product(): return jnp.dot(left, right, preferred_element_type=F32)  49.3 us
    unnamed x246, local copies, waits for them, and re-layouts  46.7 us
    pallas_call x3, Pallas kernels, attend_forward(): pl.pallas_call(functools.partial(forward_kernel, causal), grid_spec=pltpu...  43 us
    dot_general x9, matrix products, product_nt(): lax.dot_general(left, right, (((1,), (1,)), ((), ())), preferred_element_...  38.2 us
    dot_general x9, matrix products, product_tn(): lax.dot_general(left, right, (((0,), (0,)), ((), ())), preferred_element_...  35 us
  transfers between devices with their start and end apart: 19, of which 3 were waited for; matrix products, arithmetic and copies ran while one was open for 19% of the time, Pallas kernels for 42%

profile of v6, /device:TPU:0, one launch (start us, length us, event | category | flops | bytes accessed | tf_op | source)
XLA Modules:
  0.0 883.7 jit_solution(6577341761445321524)
XLA Ops:
  18.5 235.0 %gather_all.1 = (bf16[2,2,2,4,48,128]{5,4,3,2,1,0:T(8,128)(2,1)}, bf16[2,2,2,4,32,1536]{5,4,3,2,1,0:T(8,128)(2,1)}, bf16[2,2,1,4,32,1024]{5,4,3,2,1,0:T(8,128)(2...) custom-call(bf16[1,48,128]{2,1,0:T(8,128)(2,1)} %fusion.24.refs_0_, ...), custom_call_target="tpu_custom_call" | custom-call | tf_op jit(solution)/shard_map/gather_all/pallas_call | solution.py:687
  269.2 18.0 %attend.2 = (bf16[1024,512]{1,0:T(8,128)(2,1)S(1)}, f32[2,8,1024]{2,1,0:T(8,128)S(1)}) custom-call(s32[17]{0:T(128)S(1)} %get-tuple-element.283.info_ref, bf16[1024,1536]{1,0:T(8,128)(2,1)S(1)} %add_convert_fusion.q_ref.k_ref.v_ref, bf16[1024,1536]{1,0:T(8,128)(2,1)S(1)} %add_convert_fusion.q_ref.k_ref.v_ref, ...), custom_call_target="tpu_custom_call" | custom-call | flops 4294967296 | bytes 4194304 | tf_op jit(solution)/shard_map/attend/pallas_call | solution.py:372
  293.2 11.2 %attend_causal.1 = (bf16[1024,512]{1,0:T(8,128)(2,1)S(1)}, f32[2,8,1024]{2,1,0:T(8,128)S(1)}) custom-call(s32[17]{0:T(128)S(1)} %get-tuple-element.282.info_ref, bf16[1024,1536]{1,0:T(8,128)(2,1)S(1)} %add_convert_fusion.1.q_ref.k_ref.v_ref, bf16[1024,1536]{1,0:T(8,128)(2,1)S(1)} %add_convert_fusion.1.q_ref.k_ref.v_ref, ...), custom_call_target="tpu_custom_call" | custom-call | flops 4294967296 | bytes 4194304 | tf_op jit(solution)/shard_map/attend_causal/pallas_call | solution.py:372
  311.2 9.4 %fusion.9 = (bf16[1024,2048]{1,0:T(8,128)(2,1)}, bf16[1024,2048]{1,0:T(8,128)(2,1)S(1)}) fusion(f32[2048]{0:T(1024)S(1)} %bitcast.334, bf16[1024,1024]{1,0:T(8,128)(2,1)S(1)} %add_convert_fusion.6.normed_ref, bf16[1024,2048]{1,0:T(8,128)(2,1)S(1)} %bitcast.338), kind=kOutput, calls=%fused_computation.11 | convolution fusion | flops 4320133120 | bytes 14688256 | tf_op jit(solution)/shard_map/dot_general | solution.py:23
  336.1 13.8 %attend.3 = (bf16[1024,512]{1,0:T(8,128)(2,1)S(1)}, f32[2,8,1024]{2,1,0:T(8,128)S(1)}) custom-call(s32[17]{0:T(128)S(1)} %pad_add_fusion.1.info_ref, bf16[1024,512]{1,0:T(8,128)(2,1)S(1)} %add_convert_fusion.10.q_ref, bf16[1024,1024]{1,0:T(8,128)(2,1)S(1)} %add_convert_fusion.4.k_ref.v_ref, bf16[1024,1024]{1,0:T(8,128)(2,1)S(1)} %add_convert_fusion.4.k_ref.v_ref, ...), custom_call_target="tpu_custom_call" | custom-call | flops 4294967296 | bytes 4194304 | tf_op jit(solution)/shard_map/attend/pallas_call | solution.py:372
  360.4 9.7 %all-gather.3.cloned.1.call-done = bf16[4096,1024]{1,0:T(8,128)(2,1)} async-done(((bf16[256,1024]{1,0:T(8,128)(2,1)}), bf16[4096,1024]{1,0:T(8,128)(2,1)}) %all-gather.3.cloned.1.call-update) | async-done | bytes 8388624 | tf_op jit(solution)/shard_map/all_gather | solution.py:1005
  378.4 7.2 multiply_convert_fusion
  385.6 8.5 convert_reduce_fusion
  401.3 8.6 convolution_convert_fusion.3
  410.0 9.3 %fusion.12.mine_ref = bf16[1024,1024]{1,0:T(8,128)(2,1)} fusion(bf16[1024,2048]{1,0:T(8,128)(2,1)} %copy-done.114, bf16[1024,1024]{1,0:T(8,128)(2,1)} %bitcast.297, bf16[1024,1024]{1,0:T(8,128)(2,1)} %bitcast.295), kind=kOutput, calls=%fused_computation.53 | convolution fusion | flops 4304404480 | bytes 10485760 | tf_op jit(solution)/shard_map/dot_general | solution.py:31
  420.8 9.5 %convolution_convert_fusion.5 = bf16[1024,1024]{1,0:T(8,128)(2,1)} fusion(bf16[1024,2048]{1,0:T(8,128)(2,1)} %get-tuple-element.278, bf16[2048,1024]{1,0:T(8,128)(2,1)} %bitcast.279), kind=kOutput, calls=%fused_computation.55 | convolution fusion | flops 4296015872 | bytes 10485760 | tf_op jit(solution)/shard_map/dot_general | solution.py:23
  430.8 5.8 norm_grad.3
  441.3 20.8 %attend_grad.2 = (bf16[1024,512]{1,0:T(8,128)(2,1)S(1)}, bf16[1024,1024]{1,0:T(8,128)(2,1)S(1)}) custom-call(s32[17]{0:T(128)S(1)} %pad_add_fusion.1.info_ref, bf16[1024,512]{1,0:T(8,128)(2,1)S(1)} %copy-done.65, bf16[1024,1024]{1,0:T(8,128)(2,1)S(1)} %copy-done.67, bf16[1024,1024]{1,0:T(8,128)(2,1)S(1)} %copy-done.67, bf16[1024,512]{1,0:T(8,128)(2,1)S(1)} %copy-done.39, ...), custom_call_target="tpu_custom_call" | custom-call | flops 10737418240 | bytes 8388608 | tf_op jit(solution)/shard_map/attend_grad/pallas_call | solution.py:401
  485.3 6.2 add_convert_fusion.2
  491.5 6.5 convert_reduce_fusion.5
  498.0 24.3 %ffn_grad.1 = (bf16[1024,1024]{1,0:T(8,128)(2,1)}, bf16[1024,2048]{1,0:T(8,128)(2,1)S(1)}, bf16[2048,1024]{1,0:T(8,128)(2,1)}, f32[1,2048]{1,0:T(1,128)S(1)}) custom-call(bf16[1024,1024]{1,0:T(8,128)(2,1)S(1)} %get-tuple-element.185.grad_ref, bf16[1024,1024]{1,0:T(8,128)(2,1)S(1)} %copy-done.22, bf16[1024,2048]{1,0:T(8,128)(2,1)} %copy-done.115, ...), custom_call_target="tpu_custom_call" | custom-call | flops 17179869184 | bytes 25165824 | tf_op jit(solution)/shard_map/ffn_grad/pallas_call | solution.py:141
  522.4 6.2 norm_grad.4
  533.2 17.3 %attend_grad_causal.1 = bf16[1024,1536]{1,0:T(8,128)(2,1)S(1)} custom-call(s32[17]{0:T(128)S(1)} %copy-done.59, bf16[1024,1536]{1,0:T(8,128)(2,1)S(1)} %copy-done.63, bf16[1024,1536]{1,0:T(8,128)(2,1)S(1)} %copy-done.63, bf16[1024,1536]{1,0:T(8,128)(2,1)S(1)} %copy-done.63, bf16[1024,512]{1,0:T(8,128)(2,1)S(1)} %copy-done.36, ...), custom_call_target="tpu_custom_call" | custom-call | flops 10737418240 | bytes 8388608 | tf_op jit(solution)/shard_map/attend_grad_causal/pallas_call | solution.py:401
  552.9 6.9 convolution_convert_fusion.6.mine_ref
  562.6 6.0 norm_grad.5
  573.2 27.5 %attend_grad.3 = bf16[1024,1536]{1,0:T(8,128)(2,1)S(1)} custom-call(s32[17]{0:T(128)S(1)} %copy-done.57, bf16[1024,1536]{1,0:T(8,128)(2,1)S(1)} %copy-done.61, bf16[1024,1536]{1,0:T(8,128)(2,1)S(1)} %copy-done.61, bf16[1024,1536]{1,0:T(8,128)(2,1)S(1)} %copy-done.61, bf16[1024,512]{1,0:T(8,128)(2,1)S(1)} %copy-done.33, ...), custom_call_target="tpu_custom_call" | custom-call | flops 10737418240 | bytes 8388608 | tf_op jit(solution)/shard_map/attend_grad/pallas_call | solution.py:401
  617.2 6.7 norm_last.3
  632.7 6.7 norm_last.2
  643.2 205.8 %sum_all.1 = (f32[32,1024]{1,0:T(8,128)}, f32[3,32,1024]{2,1,0:T(8,128)}, f32[1,32,4096]{2,1,0:T(8,128)}, f32[128,1024]{1,0:T(8,128)}, f32[3,32,1024]{2,1,0:T(8,...) custom-call(bf16[2,2,1,4,32,1024]{5,4,3,2,1,0:T(8,128)(2,1)} %bitcas, ...), custom_call_target="tpu_custom_call" | custom-call | tf_op jit(solution)/shard_map/sum_all/pallas_call | solution.py:933
  (450 shorter events, 181.1 us)
Async XLA Ops:
  7.2 362.9 %all-gather.3.cloned.1.call-start = ((), (), s32[]{:S(2)}) async-start(), calls=%async_computation.6 | async-start | bytes 8912896 | tf_op jit(solution)/shard_map/all_gather | solution.py:1005
  8.8 3.8 collective-permute-start
  10.2 5.8 collective-permute-start.1
  13.3 255.9 %copy-start.54 = (s32[1,1024]{1,0:T(1,128)}, s32[1,1024]{1,0:T(1,128)S(1)}, u32[]{:S(2)}) copy-start(s32[1,1024]{1,0:T(1,128)S(1)} %get-tuple-element.267.qseg_ref) | copy-start | bytes 12292
  14.7 254.5 %copy-start.56 = (s32[17]{0:T(128)}, s32[17]{0:T(128)S(1)}, u32[]{:S(2)}) copy-start(s32[17]{0:T(128)S(1)} %get-tuple-element.283.info_ref) | copy-start | bytes 208
  14.7 278.5 %copy-start.58 = (s32[17]{0:T(128)}, s32[17]{0:T(128)S(1)}, u32[]{:S(2)}) copy-start(s32[17]{0:T(128)S(1)} %get-tuple-element.282.info_ref) | copy-start | bytes 208
  15.6 320.4 %copy-start.41 = (s32[1024,1]{1,0:T(8,128)}, s32[1024,1]{1,0:T(8,128)S(1)}, u32[]{:S(2)}) copy-start(s32[1024,1]{1,0:T(8,128)S(1)} %copy.103.kseg_ref) | copy-start | bytes 12292
  15.9 277.3 %copy-start.44 = (s32[1024,1]{1,0:T(8,128)}, s32[1024,1]{1,0:T(8,128)S(1)}, u32[]{:S(2)}) copy-start(s32[1024,1]{1,0:T(8,128)S(1)} %copy.102.kseg_ref) | copy-start | bytes 12292
  255.3 603.5 %reduce-scatter.6.cloned.1.call-start = ((), (), s32[]{:S(2)}) async-start(), calls=%async_computation.4 | async-start | bytes 4456448 | tf_op jit(solution)/shard_map/reduce_scatter | solution.py:1021
  288.6 17.3 %collective-permute-start.3 = (bf16[1024,1024]{1,0:T(8,128)(2,1)S(1)}, bf16[1024,1024]{1,0:T(8,128)(2,1)S(1)}, u32[]{:S(2)}, u32[]{:S(2)}) collective-permute-start(bf16[1024,1024]{1,0:T(8,128)(2,1)S(1)} %convolution_convert_fusion.12), channel_id=1, source_target_pairs={{0,4},{4,0},{1,5},{5,1},{2,6},{6,2},{3,7},{7,3},{8,12},{12,8},{9,1... | collective-permute-start | bytes 6291464 | tf_op jit(solution)/shard_map/ppermute | solution.py:960
  305.7 20.2 %collective-permute-start.2 = (bf16[1024,1024]{1,0:T(8,128)(2,1)S(1)}, bf16[1024,1024]{1,0:T(8,128)(2,1)S(1)}, u32[]{:S(2)}, u32[]{:S(2)}) collective-permute-start(bf16[1024,1024]{1,0:T(8,128)(2,1)S(1)} %convolution_convert_fusion.13), channel_id=1, source_target_pairs={{0,4},{4,0},{1,5},{5,1},{2,6},{6,2},{3,7},{7,3},{8,12},{12,8},{9,1... | collective-permute-start | bytes 6291464 | tf_op jit(solution)/shard_map/ppermute | solution.py:960
  325.4 7.0 collective-permute-start.4
  351.3 4.2 collective-permute-start.5
  401.3 459.2 %reduce-scatter.8.cloned.1.call-start = ((), (), s32[]{:S(2)}) async-start(), calls=%async_computation.5 | async-start | bytes 4456448 | tf_op jit(solution)/shard_map/reduce_scatter | solution.py:1050
  410.0 455.5 %reduce-scatter.4.cloned.1.call-start = ((), (), s32[]{:S(2)}) async-start(), calls=%async_computation.3 | async-start | bytes 4456448 | tf_op jit(solution)/shard_map/reduce_scatter | solution.py:1038
  419.3 11.5 %collective-permute-start.6 = (bf16[1024,1024]{1,0:T(8,128)(2,1)}, bf16[1024,1024]{1,0:T(8,128)(2,1)}, u32[]{:S(2)}, u32[]{:S(2)}) collective-permute-start(bf16[1024,1024]{1,0:T(8,128)(2,1)} %fusion.12.mine_ref), channel_id=1, source_target_pairs={{0,4},{4,0},{1,5},{5,1},{2,6},{6,2},{3,7},{7,3},{8,12},{12,8},{9,1... | collective-permute-start | bytes 6291464 | tf_op jit(solution)/shard_map/ppermute | solution.py:960
  430.3 55.0 %collective-permute-start.12 = (bf16[1024,1024]{1,0:T(8,128)(2,1)}, bf16[1024,1024]{1,0:T(8,128)(2,1)}, u32[]{:S(2)}, u32[]{:S(2)}) collective-permute-start(bf16[1024,1024]{1,0:T(8,128)(2,1)} %convolution_convert_fusion.5), channel_id=1, source_target_pairs={{0,4},{4,0},{1,5},{5,1},{2,6},{6,2},{3,7},{7,3},{8,12},{12,8},{9,1... | collective-permute-start | bytes 6291464 | tf_op jit(solution)/shard_map/ppermute | solution.py:960
  477.1 14.4 %collective-permute-start.8 = (bf16[1024,1024]{1,0:T(8,128)(2,1)}, bf16[1024,1024]{1,0:T(8,128)(2,1)}, u32[]{:S(2)}, u32[]{:S(2)}) collective-permute-start(bf16[1024,1024]{1,0:T(8,128)(2,1)} %convolution_convert_fusion.8), channel_id=1, source_target_pairs={{0,4},{4,0},{1,5},{5,1},{2,6},{6,2},{3,7},{7,3},{8,12},{12,8},{9,1... | collective-permute-start | bytes 6291464 | tf_op jit(solution)/shard_map/ppermute | solution.py:960
  478.5 43.9 %collective-permute-start.7 = (bf16[1024,1024]{1,0:T(8,128)(2,1)S(1)}, bf16[1024,1024]{1,0:T(8,128)(2,1)}, u32[]{:S(2)}, u32[]{:S(2)}) collective-permute-start(bf16[1024,1024]{1,0:T(8,128)(2,1)S(1)} %convolution_convert_fusion.9.mine_ref), channel_id=1, source_target_pairs={{0,4},{4,0},{1,5},{5,1},{2,6},{6,2},{3,7},{7,3},{8,12},{12,8},{9,1... | collective-permute-start | bytes 6291464 | tf_op jit(solution)/shard_map/ppermute | solution.py:960
  522.3 40.2 %collective-permute-start.9 = (bf16[1024,1024]{1,0:T(8,128)(2,1)}, bf16[1024,1024]{1,0:T(8,128)(2,1)}, u32[]{:S(2)}, u32[]{:S(2)}) collective-permute-start(bf16[1024,1024]{1,0:T(8,128)(2,1)} %get-tuple-element.104.mine_ref), channel_id=1, source_target_pairs={{0,4},{4,0},{1,5},{5,1},{2,6},{6,2},{3,7},{7,3},{8,12},{12,8},{9,1... | collective-permute-start | bytes 6291464 | tf_op jit(solution)/shard_map/ppermute | solution.py:960
  559.8 52.0 %collective-permute-start.11 = (bf16[1024,1024]{1,0:T(8,128)(2,1)}, bf16[1024,1024]{1,0:T(8,128)(2,1)}, u32[]{:S(2)}, u32[]{:S(2)}) collective-permute-start(bf16[1024,1024]{1,0:T(8,128)(2,1)} %convolution_convert_fusion.6.mine_ref), channel_id=1, source_target_pairs={{0,4},{4,0},{1,5},{5,1},{2,6},{6,2},{3,7},{7,3},{8,12},{12,8},{9,1... | collective-permute-start | bytes 6291464 | tf_op jit(solution)/shard_map/ppermute | solution.py:960
  605.3 27.3 %collective-permute-start.10 = (bf16[1024,1024]{1,0:T(8,128)(2,1)}, bf16[1024,1024]{1,0:T(8,128)(2,1)}, u32[]{:S(2)}, u32[]{:S(2)}) collective-permute-start(bf16[1024,1024]{1,0:T(8,128)(2,1)} %convolution_convert_fusion.7.mine_ref), channel_id=1, source_target_pairs={{0,4},{4,0},{1,5},{5,1},{2,6},{6,2},{3,7},{7,3},{8,12},{12,8},{9,1... | collective-permute-start | bytes 6291464 | tf_op jit(solution)/shard_map/ppermute | solution.py:960
  859.7 2.5 collective-permute-start.14
  867.6 1.5 collective-permute-start.13
  (111 other events, 1012.4 us)
Sparse Core Ops, SparseCore 0:
  255.5 114.5 all-gather.2
  401.4 94.6 reduce-scatter.5
  498.4 94.6 reduce-scatter.7
  595.3 113.4 reduce-scatter.3
